TPU v7x, 128 devices: a whole 4x4x4 slice. The times are simulated.
128 devices in a mesh: wide: 16 (over x_hi, z, core), narrow: 8 (over y, x_lo).
Axes of the slice: x: 4 (x_hi: 2, x_lo: 2; x = x_hi * 2 + x_lo), y: 4, z: 4, core: 2. Of those that a mesh axis runs over, the one named last changes fastest.
Arguments:
- prompt_states: bfloat16 [384, 4096], P('wide'), may hold values from -6 to 6
- prompt_lengths: int32 [1], replicated, may hold values from 96 to 384
- feed_gain: float32 [4096], replicated, may hold values from 0.1 to 1.9
- gate_weight: bfloat16 [4096, 5120], P(None, 'narrow'), may hold values from -0.09375 to 0.09375
- up_weight: bfloat16 [4096, 5120], P(None, 'narrow'), may hold values from -0.09375 to 0.09375
- down_weight: bfloat16 [5120, 4096], P('narrow'), may hold values from -0.078125 to 0.078125
- final_gain: float32 [4096], replicated, may hold values from 0.1 to 1.9
- key_weight: bfloat16 [4096, 3072], P(None, 'narrow'), may hold values from -0.09375 to 0.09375
- value_weight: bfloat16 [4096, 3072], P(None, 'narrow'), may hold values from -0.09375 to 0.09375
- prompt_key_gain: float32 [3072], P('narrow'), may hold values from 1 to 2.6
- latent_queries: bfloat16 [16384, 3072], P(('wide', 'narrow')), may hold values from -6 to 6
- latent_keys: bfloat16 [16384, 3072], P(('wide', 'narrow')), may hold values from -6 to 6
- latent_values: bfloat16 [16384, 3072], P(('wide', 'narrow')), may hold values from -4 to 4
- cross_queries: bfloat16 [16384, 3072], P(('wide', 'narrow')), may hold values from -6 to 6
- query_gain: float32 [3072], replicated, may hold values from 1 to 2.6
- key_gain: float32 [3072], replicated, may hold values from 1 to 2.6
- cross_query_gain: float32 [3072], replicated, may hold values from 1 to 2.6
Outputs:
- self_out: bfloat16 [16384, 3072], P('wide', 'narrow')
- cross_out: bfloat16 [16384, 3072], P('wide', 'narrow')
Inputs may be any that keep to these rules, and one draw needn't show every extreme that they name: `prompt_lengths`: the number of live prompt tokens; later prompt positions are padding.
All inputs are finite; a program needn't handle non-finite values.
Results may differ from a plain program's by a relative error of at most 0.017.
Values may be sent and summed in bfloat16 or wider, within the bound.
No kernel may reach another device: no remote copies, remote signals or barrier semaphores. Data moves between devices by JAX's collectives and lax.ppermute only.
A program may use at most 192 MiB of HBM per device.

v0:
```python
import math

import jax
import jax.numpy as jnp
from jax import lax
from jax.sharding import PartitionSpec as P

HEAD_DIM = 128


epsilon = 1e-06
tile_rows = 1024


def rms_rows(values, gain):
    widened = values.astype(jnp.float32)
    inverse = lax.rsqrt(jnp.mean(widened * widened, axis=-1, keepdims=True) + epsilon)
    return widened * inverse * gain


def head_norm(values, gain, head_size):
    count, width = values.shape
    split = values.astype(jnp.float32).reshape(count, width // head_size, head_size)
    inverse = lax.rsqrt(jnp.mean(split * split, axis=-1, keepdims=True) + epsilon)
    return (split * inverse).reshape(count, width) * gain


def add_keys(carry, query_heads, key_piece, value_piece):
    count = key_piece.shape[0]
    block_rows = math.gcd(count, tile_rows)
    heads = query_heads.shape[1]
    head_size = query_heads.shape[2]
    key_blocks = key_piece.reshape(count // block_rows, block_rows, heads, head_size)
    value_blocks = value_piece.reshape(count // block_rows, block_rows, heads, head_size)
    factor = 1.0 / math.sqrt(head_size)

    def advance(state, operands):
        weighted, totals = state
        key_block, value_block = operands
        scores = (
            jnp.einsum("qhd,khd->hqk", query_heads, key_block, preferred_element_type=jnp.float32)
            * factor
        )
        weights = jnp.exp(scores)
        totals = totals + jnp.sum(weights, axis=2)
        weighted = weighted + jnp.einsum(
            "hqk,khd->qhd",
            weights.astype(jnp.bfloat16),
            value_block,
            preferred_element_type=jnp.float32,
        )
        return ((weighted, totals), None)

    carry, _ = lax.scan(advance, carry, (key_blocks, value_blocks))
    return carry


def finish(weighted, totals):
    return (weighted / totals[:, :, None]).reshape(weighted.shape[0], -1).astype(jnp.bfloat16)


def cross_attend(query_heads, key_heads, value_heads, live):
    factor = 1.0 / math.sqrt(query_heads.shape[2])
    scores = (
        jnp.einsum("qhd,khd->hqk", query_heads, key_heads, preferred_element_type=jnp.float32)
        * factor
    )
    weights = jnp.where(live[None, None, :], jnp.exp(scores), 0.0)
    totals = jnp.sum(weights, axis=2)
    weighted = jnp.einsum(
        "hqk,khd->qhd",
        weights.astype(jnp.bfloat16),
        value_heads,
        preferred_element_type=jnp.float32,
    )
    return finish(weighted, totals.T)


def body(
    prompt_states,
    prompt_lengths,
    feed_gain,
    gate_weight,
    up_weight,
    down_weight,
    final_gain,
    key_weight,
    value_weight,
    prompt_key_gain,
    latent_queries,
    latent_keys,
    latent_values,
    cross_queries,
    query_gain,
    key_gain,
    cross_query_gain,
):
    normed = rms_rows(prompt_states, feed_gain).astype(jnp.bfloat16)
    gate = jnp.dot(normed, gate_weight, preferred_element_type=jnp.float32)
    upward = jnp.dot(normed, up_weight, preferred_element_type=jnp.float32)
    hidden = (jax.nn.gelu(gate, approximate=True) * upward).astype(jnp.bfloat16)
    partial_out = jnp.dot(hidden, down_weight, preferred_element_type=jnp.float32)
    feed_out = lax.psum(partial_out, "narrow")
    text = rms_rows(prompt_states.astype(jnp.float32) + feed_out, final_gain).astype(jnp.bfloat16)
    group_width = key_weight.shape[1]
    piece = lax.all_gather(text, "wide", axis=0, tiled=True)
    projected_keys = head_norm(
        jnp.dot(piece, key_weight, preferred_element_type=jnp.float32), prompt_key_gain, HEAD_DIM
    ).astype(jnp.bfloat16)
    projected_values = jnp.dot(piece, value_weight, preferred_element_type=jnp.float32).astype(
        jnp.bfloat16
    )
    projected_keys, projected_values = (projected_keys, projected_values)
    joined = jnp.concatenate([projected_keys, projected_values], axis=1)
    prompt_keys = joined[:, :group_width]
    prompt_values = joined[:, group_width:]
    queries = head_norm(latent_queries, query_gain, HEAD_DIM).astype(jnp.bfloat16)
    keys_normed = head_norm(latent_keys, key_gain, HEAD_DIM).astype(jnp.bfloat16)
    cross_normed = head_norm(cross_queries, cross_query_gain, HEAD_DIM).astype(jnp.bfloat16)
    heads = group_width // HEAD_DIM

    def as_heads(array):
        return array.reshape(array.shape[0], heads, HEAD_DIM)

    query_group, key_group, value_group, cross_group = (
        lax.all_to_all(queries, "narrow", split_axis=1, concat_axis=0, tiled=True),
        lax.all_to_all(keys_normed, "narrow", split_axis=1, concat_axis=0, tiled=True),
        lax.all_to_all(latent_values, "narrow", split_axis=1, concat_axis=0, tiled=True),
        lax.all_to_all(cross_normed, "narrow", split_axis=1, concat_axis=0, tiled=True),
    )
    count = query_group.shape[0]
    query_heads = as_heads(query_group)
    empty = (
        jnp.zeros((count, heads, HEAD_DIM), jnp.float32),
        jnp.zeros((heads, count), jnp.float32),
    )
    piece = (
        lax.all_gather(key_group, "wide", axis=0, tiled=True),
        lax.all_gather(value_group, "wide", axis=0, tiled=True),
    )
    weighted, totals = add_keys(empty, query_heads, as_heads(piece[0]), as_heads(piece[1]))
    self_out = finish(weighted, totals.T)
    prompt_live = jnp.arange(prompt_keys.shape[0], dtype=jnp.int32) < prompt_lengths[0]
    cross_out = cross_attend(
        as_heads(cross_group), as_heads(prompt_keys), as_heads(prompt_values), prompt_live
    )
    return (self_out, cross_out)


def solution(mesh):
    return jax.shard_map(
        body,
        mesh=mesh,
        in_specs=(
            P("wide", None),
            P(),
            P(),
            P(None, "narrow"),
            P(None, "narrow"),
            P("narrow", None),
            P(),
            P(None, "narrow"),
            P(None, "narrow"),
            P("narrow"),
            P(("wide", "narrow"), None),
            P(("wide", "narrow"), None),
            P(("wide", "narrow"), None),
            P(("wide", "narrow"), None),
            P(),
            P(),
            P(),
        ),
        out_specs=(P("wide", "narrow"), P("wide", "narrow")),
        check_vma=False,
    )
```

profile of v0, /device:TPU:14, one launch (start us, length us, event | category | flops | bytes accessed | tf_op | source)
XLA Modules:
  0.0 658.2 jit_solution(15029052443141421335)
XLA Ops:
  18.4 73.6 %all-reduce.2.cloned.1.call-done = f32[24,4096]{1,0:T(8,128)} async-done(((f32[24,4096]{1,0:T(8,128)}), f32[24,4096]{1,0:T(8,128)}) %all-reduce.2.cloned.1.call-update) | async-done | bytes 393232 | tf_op jit(solution)/shard_map/psum | solution.py:103
  103.0 15.0 %all_to_all.70 = bf16[128,8,384]{0,2,1:T(8,128)(2,1)} all-to-all(bf16[128,8,384]{0,2,1:T(8,128)(2,1)S(1)} %bitcast.96), channel_id=1, replica_groups=mesh['wide'=16,'narrow'=8] {'narrow'}, dimensions={1} | all-to-all | bytes 1572864 | tf_op jit(solution)/shard_map/all_to_all | solution.py:127
  122.7 21.5 %all_to_all.71 = bf16[128,8,384]{0,2,1:T(8,128)(2,1)} all-to-all(bf16[128,8,384]{0,2,1:T(8,128)(2,1)} %bitcast.99), channel_id=1, replica_groups=mesh['wide'=16,'narrow'=8] {'narrow'}, dimensions={1} | all-to-all | bytes 1572864 | tf_op jit(solution)/shard_map/all_to_all | solution.py:128
  173.3 8.4 %all-to-all-done.3 = bf16[128,8,384]{0,2,1:T(8,128)(2,1)} async-done(((bf16[128,8,384]{0,2,1:T(8,128)(2,1)}), bf16[128,8,384]{0,2,1:T(8,128)(2,1)}, u32[]{:S(2)}, u32[]{:S(2)}) %all-to-all-start.3) | async-done | bytes 786464 | tf_op jit(solution)/shard_map/all_to_all | solution.py:129
  181.7 7.9 %all-to-all-start.2 = ((bf16[128,8,384]{0,2,1:T(8,128)(2,1)}), bf16[128,8,384]{0,2,1:T(8,128)(2,1)}, u32[]{:S(2)}, u32[]{:S(2)}) async-start(bf16[128,8,384]{0,2,1:T(8,128)(2,1)} %bitcast.95), calls=%async_computation.2 | async-start | bytes 1572864 | tf_op jit(solution)/shard_map/all_to_all | solution.py:126
  219.2 32.0 %all-gather.6.cloned.1.call-done = bf16[16384,384]{1,0:T(8,128)(2,1)} async-done(((bf16[1024,384]{1,0:T(8,128)(2,1)}), bf16[16384,384]{1,0:T(8,128)(2,1)}) %all-gather.6.cloned.1.call-update) | async-done | bytes 12582928 | tf_op jit(solution)/shard_map/all_gather | solution.py:138
  251.2 32.2 %reshape.115 = bf16[16,1024,3,128]{3,2,1,0:T(4,128)(2,1)} reshape(bf16[16384,384]{1,0:T(8,128)(2,1)} %all-gather.6.cloned.1.call-done) | data formatting | bytes 25165824 | tf_op jit(solution)/shard_map/reshape;reshape | solution.py:33
  283.4 13.8 %copy.88 = bf16[16,1024,3,128]{3,1,2,0:T(8,128)(2,1)} copy(bf16[16,1024,3,128]{3,2,1,0:T(4,128)(2,1)} %reshape.115) | data formatting | bytes 25165824
  297.2 45.8 %all-gather.4.cloned.1.call-done = bf16[16384,384]{1,0:T(8,128)(2,1)} async-done(((bf16[1024,384]{1,0:T(8,128)(2,1)}), bf16[16384,384]{1,0:T(8,128)(2,1)}) %all-gather.4.cloned.1.call-update) | async-done | bytes 12582928 | tf_op jit(solution)/shard_map/all_gather | solution.py:139
  343.0 32.1 %reshape.114 = bf16[16,1024,3,128]{3,2,1,0:T(4,128)(2,1)} reshape(bf16[16384,384]{1,0:T(8,128)(2,1)} %all-gather.4.cloned.1.call-done) | data formatting | bytes 25165824 | tf_op jit(solution)/shard_map/reshape;reshape | solution.py:34
  375.1 24.9 %copy.87 = bf16[16,1024,3,128]{1,3,2,0:T(8,128)(2,1)} copy(bf16[16,1024,3,128]{3,2,1,0:T(4,128)(2,1)} %reshape.114) | data formatting | bytes 25165824
  400.1 246.7 %while.13 = (s32[]{:T(128)}, f32[1024,3,128]{0,2,1:T(8,128)}, f32[3,1024]{1,0:T(4,128)S(1)}, bf16[16,1024,3,128]{1,3,2,0:T(8,128)(2,1)}, bf16[16,1024,3,128]{3,1...) while((s32[]{:T(128)}, f32[1024,3,128]{0,2,1:T(8,128)}, ...), condition=%wide.region_4.0_spmd.clone, body=%wide.region_2.4_spmd.clone.sunk | while | flops 1623985152 | bytes 30721120 | solution.py:54
  406.7 8.3 %bitcast_add_fusion.2 = f32[1024,3,128]{0,2,1:T(8,128)} fusion(f32[1024,3,128]{0,2,1:T(8,128)} %get-tuple-element.160, f32[3,1024,1024]{2,1,0:T(8,128)} %get-tuple-element.149, bf16[16,1024,3,128]{1,3,2,0:T(8,128)(2,1)} %get-tuple-element.170, s32[]{:T(128)} %get-tuple-element.159, pred[]{:T(512)S(6)} %compare.3), kind=kOutput, calls=%fused_computation.5.clone.1 | convolution fusion | flops 812384256 | bytes 16515585 | tf_op jit(solution)/shard_map/while/body/eval_jaxpr/hqk,khd->qhd/dot_general | solution.py:46
  415.1 6.7 %bitcast_reduce_fusion.2 = (f32[3,1024]{1,0:T(4,128)S(1)}, f32[3,1024,1024]{2,1,0:T(8,128)}) fusion(bf16[1024,3,128]{2,0,1:T(8,128)(2,1)S(1)} %get-tuple-element.172, bf16[16,1024,3,128]{3,1,2,0:T(8,128)(2,1)} %get-tuple-element.171, s32[]{:T(128)} %get-tuple-element.159), kind=kOutput, calls=%fused_computation.clone.1 | convolution fusion | flops 811594752 | bytes 14168576 | tf_op jit(solution)/shard_map/while/body/eval_jaxpr/qhd,khd->hqk/dot_general | solution.py:41
  421.8 8.7 %bitcast_add_fusion.2 = f32[1024,3,128]{0,2,1:T(8,128)} fusion(f32[1024,3,128]{0,2,1:T(8,128)} %get-tuple-element.160, f32[3,1024,1024]{2,1,0:T(8,128)} %get-tuple-element.149, bf16[16,1024,3,128]{1,3,2,0:T(8,128)(2,1)} %get-tuple-element.170, s32[]{:T(128)} %get-tuple-element.159, pred[]{:T(512)S(6)} %compare.3), kind=kOutput, calls=%fused_computation.5.clone.1 | convolution fusion | flops 812384256 | bytes 16515585 | tf_op jit(solution)/shard_map/while/body/eval_jaxpr/hqk,khd->qhd/dot_general | solution.py:46
  430.6 6.7 %bitcast_reduce_fusion.2 = (f32[3,1024]{1,0:T(4,128)S(1)}, f32[3,1024,1024]{2,1,0:T(8,128)}) fusion(bf16[1024,3,128]{2,0,1:T(8,128)(2,1)S(1)} %get-tuple-element.172, bf16[16,1024,3,128]{3,1,2,0:T(8,128)(2,1)} %get-tuple-element.171, s32[]{:T(128)} %get-tuple-element.159), kind=kOutput, calls=%fused_computation.clone.1 | convolution fusion | flops 811594752 | bytes 14168576 | tf_op jit(solution)/shard_map/while/body/eval_jaxpr/qhd,khd->hqk/dot_general | solution.py:41
  437.2 8.7 %bitcast_add_fusion.2 = f32[1024,3,128]{0,2,1:T(8,128)} fusion(f32[1024,3,128]{0,2,1:T(8,128)} %get-tuple-element.160, f32[3,1024,1024]{2,1,0:T(8,128)} %get-tuple-element.149, bf16[16,1024,3,128]{1,3,2,0:T(8,128)(2,1)} %get-tuple-element.170, s32[]{:T(128)} %get-tuple-element.159, pred[]{:T(512)S(6)} %compare.3), kind=kOutput, calls=%fused_computation.5.clone.1 | convolution fusion | flops 812384256 | bytes 16515585 | tf_op jit(solution)/shard_map/while/body/eval_jaxpr/hqk,khd->qhd/dot_general | solution.py:46
  446.0 6.7 %bitcast_reduce_fusion.2 = (f32[3,1024]{1,0:T(4,128)S(1)}, f32[3,1024,1024]{2,1,0:T(8,128)}) fusion(bf16[1024,3,128]{2,0,1:T(8,128)(2,1)S(1)} %get-tuple-element.172, bf16[16,1024,3,128]{3,1,2,0:T(8,128)(2,1)} %get-tuple-element.171, s32[]{:T(128)} %get-tuple-element.159), kind=kOutput, calls=%fused_computation.clone.1 | convolution fusion | flops 811594752 | bytes 14168576 | tf_op jit(solution)/shard_map/while/body/eval_jaxpr/qhd,khd->hqk/dot_general | solution.py:41
  452.7 8.7 %bitcast_add_fusion.2 = f32[1024,3,128]{0,2,1:T(8,128)} fusion(f32[1024,3,128]{0,2,1:T(8,128)} %get-tuple-element.160, f32[3,1024,1024]{2,1,0:T(8,128)} %get-tuple-element.149, bf16[16,1024,3,128]{1,3,2,0:T(8,128)(2,1)} %get-tuple-element.170, s32[]{:T(128)} %get-tuple-element.159, pred[]{:T(512)S(6)} %compare.3), kind=kOutput, calls=%fused_computation.5.clone.1 | convolution fusion | flops 812384256 | bytes 16515585 | tf_op jit(solution)/shard_map/while/body/eval_jaxpr/hqk,khd->qhd/dot_general | solution.py:46
  468.1 8.7 %bitcast_add_fusion.2 = f32[1024,3,128]{0,2,1:T(8,128)} fusion(f32[1024,3,128]{0,2,1:T(8,128)} %get-tuple-element.160, f32[3,1024,1024]{2,1,0:T(8,128)} %get-tuple-element.149, bf16[16,1024,3,128]{1,3,2,0:T(8,128)(2,1)} %get-tuple-element.170, s32[]{:T(128)} %get-tuple-element.159, pred[]{:T(512)S(6)} %compare.3), kind=kOutput, calls=%fused_computation.5.clone.1 | convolution fusion | flops 812384256 | bytes 16515585 | tf_op jit(solution)/shard_map/while/body/eval_jaxpr/hqk,khd->qhd/dot_general | solution.py:46
  483.6 8.7 %bitcast_add_fusion.2 = f32[1024,3,128]{0,2,1:T(8,128)} fusion(f32[1024,3,128]{0,2,1:T(8,128)} %get-tuple-element.160, f32[3,1024,1024]{2,1,0:T(8,128)} %get-tuple-element.149, bf16[16,1024,3,128]{1,3,2,0:T(8,128)(2,1)} %get-tuple-element.170, s32[]{:T(128)} %get-tuple-element.159, pred[]{:T(512)S(6)} %compare.3), kind=kOutput, calls=%fused_computation.5.clone.1 | convolution fusion | flops 812384256 | bytes 16515585 | tf_op jit(solution)/shard_map/while/body/eval_jaxpr/hqk,khd->qhd/dot_general | solution.py:46
  499.0 8.7 %bitcast_add_fusion.2 = f32[1024,3,128]{0,2,1:T(8,128)} fusion(f32[1024,3,128]{0,2,1:T(8,128)} %get-tuple-element.160, f32[3,1024,1024]{2,1,0:T(8,128)} %get-tuple-element.149, bf16[16,1024,3,128]{1,3,2,0:T(8,128)(2,1)} %get-tuple-element.170, s32[]{:T(128)} %get-tuple-element.159, pred[]{:T(512)S(6)} %compare.3), kind=kOutput, calls=%fused_computation.5.clone.1 | convolution fusion | flops 812384256 | bytes 16515585 | tf_op jit(solution)/shard_map/while/body/eval_jaxpr/hqk,khd->qhd/dot_general | solution.py:46
  514.5 8.7 %bitcast_add_fusion.2 = f32[1024,3,128]{0,2,1:T(8,128)} fusion(f32[1024,3,128]{0,2,1:T(8,128)} %get-tuple-element.160, f32[3,1024,1024]{2,1,0:T(8,128)} %get-tuple-element.149, bf16[16,1024,3,128]{1,3,2,0:T(8,128)(2,1)} %get-tuple-element.170, s32[]{:T(128)} %get-tuple-element.159, pred[]{:T(512)S(6)} %compare.3), kind=kOutput, calls=%fused_computation.5.clone.1 | convolution fusion | flops 812384256 | bytes 16515585 | tf_op jit(solution)/shard_map/while/body/eval_jaxpr/hqk,khd->qhd/dot_general | solution.py:46
  529.9 8.7 %bitcast_add_fusion.2 = f32[1024,3,128]{0,2,1:T(8,128)} fusion(f32[1024,3,128]{0,2,1:T(8,128)} %get-tuple-element.160, f32[3,1024,1024]{2,1,0:T(8,128)} %get-tuple-element.149, bf16[16,1024,3,128]{1,3,2,0:T(8,128)(2,1)} %get-tuple-element.170, s32[]{:T(128)} %get-tuple-element.159, pred[]{:T(512)S(6)} %compare.3), kind=kOutput, calls=%fused_computation.5.clone.1 | convolution fusion | flops 812384256 | bytes 16515585 | tf_op jit(solution)/shard_map/while/body/eval_jaxpr/hqk,khd->qhd/dot_general | solution.py:46
  545.4 8.7 %bitcast_add_fusion.2 = f32[1024,3,128]{0,2,1:T(8,128)} fusion(f32[1024,3,128]{0,2,1:T(8,128)} %get-tuple-element.160, f32[3,1024,1024]{2,1,0:T(8,128)} %get-tuple-element.149, bf16[16,1024,3,128]{1,3,2,0:T(8,128)(2,1)} %get-tuple-element.170, s32[]{:T(128)} %get-tuple-element.159, pred[]{:T(512)S(6)} %compare.3), kind=kOutput, calls=%fused_computation.5.clone.1 | convolution fusion | flops 812384256 | bytes 16515585 | tf_op jit(solution)/shard_map/while/body/eval_jaxpr/hqk,khd->qhd/dot_general | solution.py:46
  560.8 8.7 %bitcast_add_fusion.2 = f32[1024,3,128]{0,2,1:T(8,128)} fusion(f32[1024,3,128]{0,2,1:T(8,128)} %get-tuple-element.160, f32[3,1024,1024]{2,1,0:T(8,128)} %get-tuple-element.149, bf16[16,1024,3,128]{1,3,2,0:T(8,128)(2,1)} %get-tuple-element.170, s32[]{:T(128)} %get-tuple-element.159, pred[]{:T(512)S(6)} %compare.3), kind=kOutput, calls=%fused_computation.5.clone.1 | convolution fusion | flops 812384256 | bytes 16515585 | tf_op jit(solution)/shard_map/while/body/eval_jaxpr/hqk,khd->qhd/dot_general | solution.py:46
  576.2 8.7 %bitcast_add_fusion.2 = f32[1024,3,128]{0,2,1:T(8,128)} fusion(f32[1024,3,128]{0,2,1:T(8,128)} %get-tuple-element.160, f32[3,1024,1024]{2,1,0:T(8,128)} %get-tuple-element.149, bf16[16,1024,3,128]{1,3,2,0:T(8,128)(2,1)} %get-tuple-element.170, s32[]{:T(128)} %get-tuple-element.159, pred[]{:T(512)S(6)} %compare.3), kind=kOutput, calls=%fused_computation.5.clone.1 | convolution fusion | flops 812384256 | bytes 16515585 | tf_op jit(solution)/shard_map/while/body/eval_jaxpr/hqk,khd->qhd/dot_general | solution.py:46
  591.7 8.7 %bitcast_add_fusion.2 = f32[1024,3,128]{0,2,1:T(8,128)} fusion(f32[1024,3,128]{0,2,1:T(8,128)} %get-tuple-element.160, f32[3,1024,1024]{2,1,0:T(8,128)} %get-tuple-element.149, bf16[16,1024,3,128]{1,3,2,0:T(8,128)(2,1)} %get-tuple-element.170, s32[]{:T(128)} %get-tuple-element.159, pred[]{:T(512)S(6)} %compare.3), kind=kOutput, calls=%fused_computation.5.clone.1 | convolution fusion | flops 812384256 | bytes 16515585 | tf_op jit(solution)/shard_map/while/body/eval_jaxpr/hqk,khd->qhd/dot_general | solution.py:46
  607.1 8.7 %bitcast_add_fusion.2 = f32[1024,3,128]{0,2,1:T(8,128)} fusion(f32[1024,3,128]{0,2,1:T(8,128)} %get-tuple-element.160, f32[3,1024,1024]{2,1,0:T(8,128)} %get-tuple-element.149, bf16[16,1024,3,128]{1,3,2,0:T(8,128)(2,1)} %get-tuple-element.170, s32[]{:T(128)} %get-tuple-element.159, pred[]{:T(512)S(6)} %compare.3), kind=kOutput, calls=%fused_computation.5.clone.1 | convolution fusion | flops 812384256 | bytes 16515585 | tf_op jit(solution)/shard_map/while/body/eval_jaxpr/hqk,khd->qhd/dot_general | solution.py:46
  615.9 6.7 %bitcast_reduce_fusion.2 = (f32[3,1024]{1,0:T(4,128)S(1)}, f32[3,1024,1024]{2,1,0:T(8,128)}) fusion(bf16[1024,3,128]{2,0,1:T(8,128)(2,1)S(1)} %get-tuple-element.172, bf16[16,1024,3,128]{3,1,2,0:T(8,128)(2,1)} %get-tuple-element.171, s32[]{:T(128)} %get-tuple-element.159), kind=kOutput, calls=%fused_computation.clone.1 | convolution fusion | flops 811594752 | bytes 14168576 | tf_op jit(solution)/shard_map/while/body/eval_jaxpr/qhd,khd->hqk/dot_general | solution.py:41
  622.6 8.7 %bitcast_add_fusion.2 = f32[1024,3,128]{0,2,1:T(8,128)} fusion(f32[1024,3,128]{0,2,1:T(8,128)} %get-tuple-element.160, f32[3,1024,1024]{2,1,0:T(8,128)} %get-tuple-element.149, bf16[16,1024,3,128]{1,3,2,0:T(8,128)(2,1)} %get-tuple-element.170, s32[]{:T(128)} %get-tuple-element.159, pred[]{:T(512)S(6)} %compare.3), kind=kOutput, calls=%fused_computation.5.clone.1 | convolution fusion | flops 812384256 | bytes 16515585 | tf_op jit(solution)/shard_map/while/body/eval_jaxpr/hqk,khd->qhd/dot_general | solution.py:46
  638.0 8.7 %bitcast_add_fusion.2 = f32[1024,3,128]{0,2,1:T(8,128)} fusion(f32[1024,3,128]{0,2,1:T(8,128)} %get-tuple-element.160, f32[3,1024,1024]{2,1,0:T(8,128)} %get-tuple-element.149, bf16[16,1024,3,128]{1,3,2,0:T(8,128)(2,1)} %get-tuple-element.170, s32[]{:T(128)} %get-tuple-element.159, pred[]{:T(512)S(6)} %compare.3), kind=kOutput, calls=%fused_computation.5.clone.1 | convolution fusion | flops 812384256 | bytes 16515585 | tf_op jit(solution)/shard_map/while/body/eval_jaxpr/hqk,khd->qhd/dot_general | solution.py:46
  (114 shorter events, 170.0 us)
Async XLA Ops:
  7.2 197.8 %copy-start = (bf16[4096,384]{1,0:T(8,128)(2,1)S(1)}, bf16[4096,384]{1,0:T(8,128)(2,1)}, u32[]{:S(2)}) copy-start(bf16[4096,384]{1,0:T(8,128)(2,1)} %param.26) | copy-start | bytes 9437188
  7.2 4.8 copy-start.3
  7.2 4.8 copy-start.4
  7.2 84.9 %all-reduce.2.cloned.1.call-start = ((), (), s32[]{:S(2)}) async-start(), calls=%async_computation.6 | async-start | bytes 786432 | tf_op jit(solution)/shard_map/psum | solution.py:103
  12.0 81.3 %copy-start.5 = (f32[4096]{0:T(1024)S(1)}, f32[4096]{0:T(1024)}, u32[]{:S(2)}) copy-start(f32[4096]{0:T(1024)} %param.25) | copy-start | bytes 49156
  18.4 186.6 %all-gather.8.cloned.1.call-start = ((), (), s32[]{:S(2)}) async-start(), calls=%async_computation.7 | async-start | bytes 3342336 | tf_op jit(solution)/shard_map/all_gather | solution.py:106
  93.3 8.1 %copy-start.6 = (f32[3072]{0:T(1024)S(1)}, f32[3072]{0:T(1024)}, u32[]{:S(2)}) copy-start(f32[3072]{0:T(1024)} %param.34) | copy-start | bytes 36868
  95.1 156.1 %all-gather.6.cloned.1.call-start = ((), (), s32[]{:S(2)}) async-start(), calls=%async_computation.5 | async-start | bytes 13369344 | tf_op jit(solution)/shard_map/all_gather | solution.py:138
  120.3 222.7 %all-gather.4.cloned.1.call-start = ((), (), s32[]{:S(2)}) async-start(), calls=%async_computation.4 | async-start | bytes 13369344 | tf_op jit(solution)/shard_map/all_gather | solution.py:139
  147.8 4.1 copy-start.7
  156.6 25.1 %all-to-all-start.3 = ((bf16[128,8,384]{0,2,1:T(8,128)(2,1)}), bf16[128,8,384]{0,2,1:T(8,128)(2,1)}, u32[]{:S(2)}, u32[]{:S(2)}) async-start(bf16[128,8,384]{0,2,1:T(8,128)(2,1)} %bitcast.94), calls=%async_computation.3 | async-start | bytes 1572864 | tf_op jit(solution)/shard_map/all_to_all | solution.py:129
  164.6 4.0 copy-start.8
  181.7 16.1 %all-to-all-start.2 = ((bf16[128,8,384]{0,2,1:T(8,128)(2,1)}), bf16[128,8,384]{0,2,1:T(8,128)(2,1)}, u32[]{:S(2)}, u32[]{:S(2)}) async-start(bf16[128,8,384]{0,2,1:T(8,128)(2,1)} %bitcast.95), calls=%async_computation.2 | async-start | bytes 1572864 | tf_op jit(solution)/shard_map/all_to_all | solution.py:126
  205.0 5.9 copy-start.9
  212.1 2.6 copy-start.10
  212.1 3.1 copy-start.11
  375.1 24.9 %copy-start.2 = (bf16[1024,3,128]{2,0,1:T(8,128)(2,1)S(1)}, bf16[1024,3,128]{2,0,1:T(8,128)(2,1)}, u32[]{:S(2)}) copy-start(bf16[1024,3,128]{2,0,1:T(8,128)(2,1)} %copy.89) | copy-start | bytes 2359300
  646.8 4.9 copy-start.1
Sparse Core Ops, SparseCore 0:
  18.5 73.5 all-reduce.1
  95.2 56.3 all-gather.7
  154.4 96.7 all-gather.5
  254.4 88.5 all-gather.3
where the time goes:
time: 666 us; the launch traced here: 658 us
  matrix products  266 us (40%)
  waiting for transfers between devices  163 us (24%)
  local copies, waits for them, and re-layouts  137 us (21%)
  blocking collectives  36.6 us (5%)
  other arithmetic  26.3 us (4%)
  starting transfers between devices  14.7 us (2%)
  between operations  14.7 us (2%)
    dot_general x16, matrix products, advance(): jnp.einsum('hqk,khd->qhd', weights.astype(jnp.bfloat16), value_block, pre...  139 us
    dot_general x16, matrix products, advance(): jnp.einsum('qhd,khd->hqk', query_heads, key_block, preferred_element_type...  107 us
    psum x1, waiting for transfers between devices, body(): feed_out = lax.psum(partial_out, 'narrow')  73.6 us
    unnamed x33, local copies, waits for them, and re-layouts  52.6 us
    all_gather x1, waiting for transfers between devices, body(): lax.all_gather(value_group, 'wide', axis=0, tiled=True)  45.8 us
    another operation x1, local copies, waits for them, and re-layouts, add_keys(): key_piece.reshape(count // block_rows, block_rows, heads, head_size)  32.2 us
    another operation x1, local copies, waits for them, and re-layouts, add_keys(): value_piece.reshape(count // block_rows, block_rows, heads, head_size)  32.1 us
    all_gather x1, waiting for transfers between devices, body(): lax.all_gather(key_group, 'wide', axis=0, tiled=True)  32 us
  transfers between devices with their start and end apart: 6, of which 5 were waited for; matrix products, arithmetic and copies ran while one was open for 16% of the time, Pallas kernels for 0%

commit v1 on v0

v1 whole, which is shorter than its diff:
```python
import math

import jax
import jax.numpy as jnp
from jax import lax
from jax.experimental import pallas as pl
from jax.experimental.pallas import tpu as pltpu
from jax.sharding import PartitionSpec as P

HEAD = 128
EPS = 1e-06
SCALE = math.log2(math.e) / math.sqrt(HEAD)
TILE = 512
CHUNK = 2048
EXTRA = 16


def vmem(mib):
    return pltpu.CompilerParams(vmem_limit_bytes=mib * 2**20)


def pack_kernel(q_ref, k_ref, v_ref, c_ref, qg_ref, kg_ref, cg_ref, *outs):
    heads = len(outs) // 2

    def norm(ref, gain_ref, h, factor):
        x = ref[:, h * HEAD : (h + 1) * HEAD].astype(jnp.float32)
        inverse = lax.rsqrt(jnp.mean(x * x, axis=-1, keepdims=True) + EPS)
        gain = gain_ref[:, h * HEAD : (h + 1) * HEAD] * factor
        return (x * inverse * gain).astype(jnp.bfloat16)

    c_out = outs[-1]
    for h in range(heads):
        kv_out, q_out = outs[2 * h], outs[2 * h + 1]
        kv_out[0, :HEAD, :] = norm(k_ref, kg_ref, h, 1.0)
        v = v_ref[:, h * HEAD : (h + 1) * HEAD].astype(jnp.float32)
        kv_out[0, HEAD:, :] = v.T.astype(jnp.bfloat16)
        q_out[0] = norm(q_ref, qg_ref, h, SCALE)
        c_out[0, h * HEAD : (h + 1) * HEAD, :] = norm(c_ref, cg_ref, h, SCALE)


def pack(q, k, v, c, qg, kg, cg, groups):
    rows, width = q.shape
    part = width // groups
    heads = part // HEAD
    block = pl.BlockSpec((rows, part), lambda n: (0, n))
    gain = pl.BlockSpec((1, part), lambda n: (0, n))
    shapes, specs = [], []
    for depth in (2 * HEAD, rows) * heads + (heads * rows,):
        shapes.append(jax.ShapeDtypeStruct((groups, depth, HEAD), jnp.bfloat16))
        specs.append(pl.BlockSpec((1, depth, HEAD), lambda n: (n, 0, 0)))
    return pl.pallas_call(
        pack_kernel,
        grid=(groups,),
        in_specs=[block] * 4 + [gain] * 3,
        out_specs=specs,
        out_shape=shapes,
        compiler_params=vmem(32),
        cost_estimate=pl.CostEstimate(
            flops=8 * q.size * 4, bytes_accessed=16 * q.size, transcendentals=0
        ),
        name="pack",
    )(q, k, v, c, qg[None, :], kg[None, :], cg[None, :])


def attend_kernel(nq, nkv, *refs):
    q_in, kv_in = refs[:nq], refs[nq : nq + nkv]
    outs = refs[nq + nkv : 2 * nq + nkv]
    q_s, k_s, v_s, o_s, sems = refs[2 * nq + nkv :]
    blocks = q_in[0].shape[0]
    copies = []
    for i, ref in enumerate(q_in):
        copies.append((ref, q_s.at[pl.ds(i * blocks, blocks)]))
    for i, ref in enumerate(kv_in):
        copies.append((ref.at[:, pl.ds(0, HEAD), :], k_s.at[pl.ds(i * blocks, blocks)]))
        copies.append((ref.at[:, pl.ds(HEAD, HEAD), :], v_s.at[pl.ds(i * blocks, blocks)]))
    copies = [
        pltpu.make_async_copy(src, dst, sems.at[i]) for i, (src, dst) in enumerate(copies)
    ]
    for copy in copies:
        copy.start()
    for copy in copies:
        copy.wait()
    per_q = TILE // HEAD
    per_k = CHUNK // HEAD
    per_block = blocks // per_q

    def tile(t, _):
        q = q_s[pl.ds(t * per_q, per_q)].reshape(TILE, HEAD)
        acc = jnp.zeros((HEAD, TILE), jnp.float32)
        total = jnp.zeros((8, TILE), jnp.float32)
        for j in range(nkv * blocks // per_k):
            keys = k_s[j * per_k : (j + 1) * per_k].reshape(CHUNK, HEAD)
            s = lax.dot_general(
                keys, q, (((1,), (1,)), ((), ())), preferred_element_type=jnp.float32
            )
            p = jnp.exp2(s)
            total = total + jnp.sum(p.reshape(CHUNK // 8, 8, TILE), axis=0)
            values = jnp.concatenate(
                [v_s[j * per_k + i] for i in range(per_k)], axis=1
            )
            acc = acc + jnp.dot(
                values, p.astype(jnp.bfloat16), preferred_element_type=jnp.float32
            )
        row = jnp.sum(total, axis=0, keepdims=True)
        high = row.astype(jnp.bfloat16).astype(jnp.float32)
        words = jnp.concatenate(
            [jnp.broadcast_to(high, (8, TILE)), jnp.broadcast_to(row - high, (8, TILE))], axis=0
        )
        columns = pl.ds(pl.multiple_of((t % per_block) * TILE, TILE), TILE)
        o_s[t // per_block, :HEAD, columns] = acc.astype(jnp.bfloat16)
        o_s[t // per_block, HEAD:, columns] = words.astype(jnp.bfloat16)
        return 0

    lax.fori_loop(0, nq * per_block, tile, 0)
    copies = [
        pltpu.make_async_copy(o_s.at[i], ref, sems.at[i]) for i, ref in enumerate(outs)
    ]
    for copy in copies:
        copy.start()
    for copy in copies:
        copy.wait()


def attend(queries, pairs):
    nq, nkv = len(queries), len(pairs)
    blocks = queries[0].shape[0]
    count = blocks * HEAD
    shape = jax.ShapeDtypeStruct((HEAD + EXTRA, count), jnp.bfloat16)
    work = nq * nkv * count * count
    return pl.pallas_call(
        lambda *refs: attend_kernel(nq, nkv, *refs),
        in_specs=[pl.BlockSpec(memory_space=pl.ANY)] * (nq + nkv),
        out_specs=[pl.BlockSpec(memory_space=pl.ANY)] * nq,
        out_shape=[shape] * nq,
        scratch_shapes=[
            pltpu.VMEM((nq * blocks, HEAD, HEAD), jnp.bfloat16),
            pltpu.VMEM((nkv * blocks, HEAD, HEAD), jnp.bfloat16),
            pltpu.VMEM((nkv * blocks, HEAD, HEAD), jnp.bfloat16),
            pltpu.VMEM((nq, HEAD + EXTRA, count), jnp.bfloat16),
            pltpu.SemaphoreType.DMA((nq + 2 * nkv,)),
        ],
        compiler_params=vmem(48),
        cost_estimate=pl.CostEstimate(
            flops=4 * HEAD * work, bytes_accessed=6 * 2**20, transcendentals=work
        ),
        name="attend",
    )(*queries, *pairs)


def merge_kernel(parts, *refs):
    out_ref = refs[-1]
    for h in range((len(refs) - 1) // parts):
        group = refs[h * parts : (h + 1) * parts]
        weighted = sum(ref[:HEAD, :].astype(jnp.float32) for ref in group)
        words = sum(ref[HEAD:, :].astype(jnp.float32) for ref in group)
        total = words[0:1] + words[8:9]
        out_ref[:, h * HEAD : (h + 1) * HEAD] = (weighted / total).T.astype(jnp.bfloat16)


def merge(groups):
    parts, heads = len(groups[0]), len(groups)
    rows, count = groups[0][0].shape
    step = 256
    return pl.pallas_call(
        lambda *refs: merge_kernel(parts, *refs),
        grid=(count // step,),
        in_specs=[pl.BlockSpec((rows, step), lambda i: (0, i))] * (parts * heads),
        out_specs=pl.BlockSpec((step, heads * HEAD), lambda i: (i, 0)),
        out_shape=jax.ShapeDtypeStruct((count, heads * HEAD), jnp.bfloat16),
        compiler_params=vmem(32),
        cost_estimate=pl.CostEstimate(
            flops=count * heads * HEAD * 8, bytes_accessed=4 * 2**20, transcendentals=0
        ),
        name="merge",
    )(*[a for group in groups for a in group])


def cross_kernel(length_ref, c_ref, kv_ref, out_ref):
    live = length_ref[0]
    blocks = c_ref.shape[0]
    heads = c_ref.shape[1] // HEAD
    count = kv_ref.shape[0]
    for h in range(heads):
        keys = kv_ref[:, h * HEAD : (h + 1) * HEAD]
        values = kv_ref[:, (heads + h) * HEAD : (heads + h + 1) * HEAD]
        values = values.astype(jnp.float32).T.astype(jnp.bfloat16)
        q = c_ref[:, h * HEAD : (h + 1) * HEAD, :].reshape(blocks * HEAD, HEAD)
        s = lax.dot_general(
            keys, q, (((1,), (1,)), ((), ())), preferred_element_type=jnp.float32
        )
        row = lax.broadcasted_iota(jnp.int32, s.shape, 0)
        p = jnp.where(row < live, jnp.exp2(s), 0.0)
        total = jnp.sum(p, axis=0, keepdims=True)
        weighted = jnp.dot(values, p.astype(jnp.bfloat16), preferred_element_type=jnp.float32)
        out_ref[:, h * HEAD : (h + 1) * HEAD] = (weighted / total).T.astype(jnp.bfloat16)


def cross(lengths, c, kv):
    blocks, depth, _ = c.shape
    step = 4
    heads = depth // HEAD
    return pl.pallas_call(
        cross_kernel,
        grid=(blocks // step,),
        in_specs=[
            pl.BlockSpec(memory_space=pltpu.SMEM),
            pl.BlockSpec((step, depth, HEAD), lambda i: (i, 0, 0)),
            pl.BlockSpec(kv.shape, lambda i: (0, 0)),
        ],
        out_specs=pl.BlockSpec((step * HEAD, depth), lambda i: (i, 0)),
        out_shape=jax.ShapeDtypeStruct((blocks * HEAD, depth), jnp.bfloat16),
        compiler_params=vmem(32),
        cost_estimate=pl.CostEstimate(
            flops=4 * HEAD * heads * blocks * HEAD * kv.shape[0],
            bytes_accessed=3 * 2**20,
            transcendentals=heads * blocks * HEAD * kv.shape[0],
        ),
        name="cross",
    )(lengths, c, kv)


def rms_rows(values, gain):
    widened = values.astype(jnp.float32)
    inverse = lax.rsqrt(jnp.mean(widened * widened, axis=-1, keepdims=True) + EPS)
    return widened * inverse * gain


def head_norm(values, gain):
    count, width = values.shape
    split = values.reshape(count, width // HEAD, HEAD)
    inverse = lax.rsqrt(jnp.mean(split * split, axis=-1, keepdims=True) + EPS)
    return (split * inverse).reshape(count, width) * gain


def wide_pairs(move):
    pairs = []
    for hi in range(2):
        for z in range(4):
            for core in range(2):
                to_hi, to_z, to_core = move(hi, z, core)
                pairs.append((hi * 8 + z * 2 + core, to_hi * 8 + (to_z % 4) * 2 + to_core))
    return pairs


UP = wide_pairs(lambda hi, z, core: (hi, z + 1, core))
DOWN = wide_pairs(lambda hi, z, core: (hi, z + 3, core))
ACROSS = wide_pairs(lambda hi, z, core: (hi, z + 2, core))
OTHER_X = wide_pairs(lambda hi, z, core: (1 - hi, z, core))
OTHER_CORE = wide_pairs(lambda hi, z, core: (hi, z, 1 - core))


def send(array, pairs):
    return lax.ppermute(array, "wide", pairs)


def trade(array):
    return lax.all_to_all(array, "narrow", split_axis=0, concat_axis=0, tiled=True)


def body(
    prompt_states,
    prompt_lengths,
    feed_gain,
    gate_weight,
    up_weight,
    down_weight,
    final_gain,
    key_weight,
    value_weight,
    prompt_key_gain,
    latent_queries,
    latent_keys,
    latent_values,
    cross_queries,
    query_gain,
    key_gain,
    cross_query_gain,
):
    groups = latent_queries.shape[1] // key_weight.shape[1]
    packed = pack(
        latent_queries,
        latent_keys,
        latent_values,
        cross_queries,
        query_gain,
        key_gain,
        cross_query_gain,
        groups,
    )
    heads = len(packed) // 2

    normed = rms_rows(prompt_states, feed_gain).astype(jnp.bfloat16)
    gate = jnp.dot(normed, gate_weight, preferred_element_type=jnp.float32)
    upward = jnp.dot(normed, up_weight, preferred_element_type=jnp.float32)
    hidden = (jax.nn.gelu(gate, approximate=True) * upward).astype(jnp.bfloat16)
    partial_out = jnp.dot(hidden, down_weight, preferred_element_type=jnp.float32)
    rows, width = partial_out.shape
    part = width // groups
    pieces = partial_out.reshape(rows, groups, part).transpose(1, 0, 2)
    feed_piece = jnp.sum(trade(pieces), axis=0)
    mine = lax.axis_index("narrow") * part
    summed_piece = (
        lax.dynamic_slice_in_dim(prompt_states, mine, part, axis=1).astype(jnp.float32)
        + feed_piece
    )
    summed = trade(jnp.broadcast_to(summed_piece[None], (groups, rows, part)))
    summed = summed.transpose(1, 0, 2).reshape(rows, width)
    text = rms_rows(summed, final_gain).astype(jnp.bfloat16)
    prompt_keys = head_norm(
        jnp.dot(text, key_weight, preferred_element_type=jnp.float32), prompt_key_gain
    ).astype(jnp.bfloat16)
    prompt_values = jnp.dot(text, value_weight, preferred_element_type=jnp.float32).astype(
        jnp.bfloat16
    )
    prompt_pair = lax.all_gather(
        jnp.concatenate([prompt_keys, prompt_values], axis=1), "wide", axis=0, tiled=True
    )

    results = []
    for h in range(heads):
        pair, query = trade(packed[2 * h]), trade(packed[2 * h + 1])
        pair_x = send(pair, OTHER_X)
        pairs = [pair, send(pair, OTHER_CORE), pair_x, send(pair_x, OTHER_CORE)]
        queries = [query, send(query, UP), send(query, DOWN), send(query, ACROSS)]
        own, below, above, across = attend(queries, pairs)
        results.append([own, send(below, DOWN), send(above, UP), send(across, ACROSS)])
    crossed = trade(packed[-1])
    cross_out = cross(prompt_lengths, crossed, prompt_pair)
    self_out = merge(results)
    return (self_out, cross_out)


def solution(mesh):
    rows = P(("wide", "narrow"), None)
    return jax.shard_map(
        body,
        mesh=mesh,
        in_specs=(
            P("wide", None),
            P(),
            P(),
            P(None, "narrow"),
            P(None, "narrow"),
            P("narrow", None),
            P(),
            P(None, "narrow"),
            P(None, "narrow"),
            P("narrow"),
            rows,
            rows,
            rows,
            rows,
            P(),
            P(),
            P(),
        ),
        out_specs=(P("wide", "narrow"), P("wide", "narrow")),
        check_vma=False,
    )
```

time: 666 us -> 269 us (0.40)
  matrix products: 266 us -> 13.5 us
  waiting for transfers between devices: 163 us -> 14.4 us
  local copies, waits for them, and re-layouts: 137 us -> 37.7 us
  Pallas kernels: 0 us -> 61.8 us
  starting transfers between devices: 14.7 us -> 75 us
  other arithmetic: 26.3 us -> 5.22 us
  blocking collectives: 36.6 us -> 54.9 us
  between operations: 14.7 us -> 1.55 us
    dot_general x36 -> x2, matrix products: 256 us -> 3.61 us  [the longest x1 3.03 us: body(): jnp.dot(text, key_weight, preferred_element_type=jnp.float32)]
    all_gather x3 -> x0, waiting for transfers between devices: 77.8 us -> none  [the longest x1 45.8 us: body(): lax.all_gather(value_group, 'wide', axis=0, tiled=True)]
    psum x1 -> x0, waiting for transfers between devices: 73.6 us -> none  [body(): feed_out = lax.psum(partial_out, 'narrow')]
    another operation x2 -> x0, local copies, waits for them, and re-layouts: 64.3 us -> none  [the longest x1 32.2 us: add_keys(): key_piece.reshape(count // block_rows, block_rows, heads, head_size)]
    pallas_call x0 -> x6, Pallas kernels: none -> 61.8 us  [the longest x3 50.1 us: attend(): pl.pallas_call(lambda *refs: attend_kernel(nq, nkv, *refs), in_specs=[pl....]
    ppermute x0 -> x27, starting transfers between devices: none -> 32.5 us  [send(): return lax.ppermute(array, 'wide', pairs)]
    all_gather x0 -> x1, blocking collectives: none -> 30.1 us  [body(): lax.all_gather(jnp.concatenate([prompt_keys, prompt_values], axis=1), 'wi...]
    all_to_all x2 -> x7, starting transfers between devices: 14.5 us -> 42.5 us  [trade(): lax.all_to_all(array, 'narrow', split_axis=0, concat_axis=0, tiled=True)]
  transfers between devices with their start and end apart: 6 -> 34, of which waited for: 5 -> 3; matrix products, arithmetic and copies ran while one was open for 16% -> 11% of each run, Pallas kernels for 0% -> 21%
where the time goes in v1:
time: 269 us; the launch traced here: 264 us
  starting transfers between devices  75 us (28%)
  Pallas kernels  61.8 us (23%)
  blocking collectives  54.9 us (20%)
  local copies, waits for them, and re-layouts  37.7 us (14%)
  waiting for transfers between devices  14.4 us (5%)
  matrix products  13.5 us (5%)
  other arithmetic  5.22 us (2%)
    pallas_call x3, Pallas kernels, attend(): pl.pallas_call(lambda *refs: attend_kernel(nq, nkv, *refs), in_specs=[pl....  50.1 us
    all_to_all x7, starting transfers between devices, trade(): lax.all_to_all(array, 'narrow', split_axis=0, concat_axis=0, tiled=True)  42.5 us
    ppermute x27, starting transfers between devices, send(): return lax.ppermute(array, 'wide', pairs)  32.5 us
    unnamed x79, local copies, waits for them, and re-layouts  31.6 us
    all_gather x1, blocking collectives, body(): lax.all_gather(jnp.concatenate([prompt_keys, prompt_values], axis=1), 'wi...  30.1 us
    all_to_all x2, blocking collectives, trade(): lax.all_to_all(array, 'narrow', split_axis=0, concat_axis=0, tiled=True)  24.8 us
    all_to_all x7, waiting for transfers between devices, trade(): lax.all_to_all(array, 'narrow', split_axis=0, concat_axis=0, tiled=True)  14.3 us
    dot_general x1, matrix products, body(): jnp.dot(hidden, down_weight, preferred_element_type=jnp.float32)  6.44 us
  transfers between devices with their start and end apart: 34, of which 3 were waited for; matrix products, arithmetic and copies ran while one was open for 11% of the time, Pallas kernels for 21%

profile of v1, /device:TPU:14, one launch (start us, length us, event | category | flops | bytes accessed | tf_op | source)
XLA Modules:
  0.0 264.1 jit_solution(15125067069229837563)
XLA Ops:
  7.5 3.8 %pack.1 = (bf16[8,256,128]{2,1,0:T(8,128)(2,1)S(1)}, bf16[8,128,128]{2,1,0:T(8,128)(2,1)}, bf16[8,256,128]{2,1,0:T(8,128)(2,1)S(1)}, bf16[8,128,128]{2,1,0:T(8,1...) custom-call(bf16[128,3072]{1,0:T(8,128)(2,1)S(1)} %copy-done.2, ...), custom_call_target="tpu_custom_call" | custom-call | flops 12582912 | bytes 6291456 | tf_op jit(solution)/shard_map/pack/pallas_call | solution.py:51
  16.0 5.8 %all-to-all-start.4 = ((bf16[8,128,128]{2,1,0:T(8,128)(2,1)}), bf16[8,128,128]{2,1,0:T(8,128)(2,1)S(1)}, u32[]{:S(2)}, u32[]{:S(2)}) async-start(bf16[8,128,128]{2,1,0:T(8,128)(2,1)} %copy-done.26), calls=%async_computation.4 | async-start | bytes 524288 | tf_op jit(solution)/shard_map/all_to_all | solution.py:257
  22.9 3.5 %fusion.20 = f32[24,640]{1,0:T(8,128)S(1)} fusion(bf16[4096,640]{1,0:T(8,128)(2,1)} %param.20, bf16[24,4096]{1,0:T(8,128)(2,1)} %param.17, f32[4096]{0:T(1024)} %param.19, f32[24]{0:T(128)S(1)} %add_rsqrt_fusion.2), kind=kOutput, calls=%fused_computation.27 | convolution fusion | flops 126222336 | bytes 5517408 | tf_op jit(solution)/shard_map/dot_general | solution.py:293
  26.4 6.4 %fusion.1 = f32[24,4096]{1,0:T(8,128)} fusion(bf16[640,4096]{1,0:T(8,128)(2,1)} %param.22, bf16[4096,640]{1,0:T(8,128)(2,1)} %param.21, f32[24,640]{1,0:T(8,128)S(1)} %fusion.20, bf16[24,4096]{1,0:T(8,128)(2,1)} %param.17, f32[4096]{0:T(1024)S(1)} %copy-done.36, f32[24]{0:T(128)S(1)} %add_rsqrt_fusion.2), kind=kOutput, calls=%fused_computation.3 | convolution fusion | flops 252205056 | bytes 11153504 | tf_op jit(solution)/shard_map/dot_general | solution.py:296
  34.6 11.9 %all_to_all.45 = f32[8,24,512]{2,1,0:T(8,128)} all-to-all(f32[8,24,512]{2,1,0:T(8,128)} %bitcast.42), channel_id=1, replica_groups=mesh['wide'=16,'narrow'=8] {'narrow'}, dimensions={0} | all-to-all | bytes 786432 | tf_op jit(solution)/shard_map/all_to_all | solution.py:257
  46.5 12.9 %all_to_all.46.refs_4_ = bf16[8,256,128]{2,1,0:T(8,128)(2,1)} all-to-all(bf16[8,256,128]{2,1,0:T(8,128)(2,1)} %copy-done.10), channel_id=1, replica_groups=mesh['wide'=16,'narrow'=8] {'narrow'}, dimensions={0} | all-to-all | bytes 1048576 | tf_op jit(solution)/shard_map/all_to_all | solution.py:257
  59.4 6.1 %all-to-all-start.3 = ((bf16[8,256,128]{2,1,0:T(8,128)(2,1)}), bf16[8,256,128]{2,1,0:T(8,128)(2,1)}, u32[]{:S(2)}, u32[]{:S(2)}) async-start(bf16[8,256,128]{2,1,0:T(8,128)(2,1)} %copy-done.9), calls=%async_computation.3 | async-start | bytes 1048576 | tf_op jit(solution)/shard_map/all_to_all | solution.py:257
  67.3 5.0 %all-to-all-done.3.refs_4_ = bf16[8,256,128]{2,1,0:T(8,128)(2,1)} async-done(((bf16[8,256,128]{2,1,0:T(8,128)(2,1)}), bf16[8,256,128]{2,1,0:T(8,128)(2,1)}, u32[]{:S(2)}, u32[]{:S(2)}) %all-to-all-start.3) | async-done | bytes 524320 | tf_op jit(solution)/shard_map/all_to_all | solution.py:257
  73.0 6.1 %all-to-all-start.8 = ((f32[8,24,512]{2,1,0:T(8,128)}), f32[8,24,512]{2,1,0:T(8,128)}, u32[]{:S(2)}, u32[]{:S(2)}) async-start(f32[8,24,512]{2,1,0:T(8,128)} %broadcast_in_dim.11), calls=%async_computation.8 | async-start | bytes 786432 | tf_op jit(solution)/shard_map/all_to_all | solution.py:257
  79.1 4.8 %copy.28 = bf16[4096,384]{0,1:T(8,128)(2,1)} copy(bf16[4096,384]{1,0:T(8,128)(2,1)} %param.24) | data formatting | bytes 6291456 | tf_op args[7]
  84.6 2.0 collective-permute-start.18
  86.6 2.2 collective-permute-start.19
  90.2 2.1 collective-permute-start.13
  92.3 5.7 %all-to-all-start.2 = ((bf16[8,128,128]{2,1,0:T(8,128)(2,1)}), bf16[8,128,128]{2,1,0:T(8,128)(2,1)}, u32[]{:S(2)}, u32[]{:S(2)}) async-start(bf16[8,128,128]{2,1,0:T(8,128)(2,1)} %copy-done.25), calls=%async_computation.2 | async-start | bytes 524288 | tf_op jit(solution)/shard_map/all_to_all | solution.py:257
  104.4 3.0 %multiply_reduce_fusion = (f32[24,3]{0,1:T(4,128)S(1)}, f32[24,3,128]{2,0,1:T(8,128)S(1)}) fusion(bf16[24,4096,1]{1,0,2:T(8,128)(2,1)} %reshape.57, bf16[3,128,4096]{2,1,0:T(8,128)(2,1)} %bitcast.40), kind=kOutput, calls=%fused_computation.32 | convolution fusion | flops 75515832 | bytes 3379488 | tf_op jit(solution)/shard_map/dot_general | solution.py:310
  107.5 5.3 %all-to-all-done.2.refs_0_ = bf16[8,128,128]{2,1,0:T(8,128)(2,1)} async-done(((bf16[8,128,128]{2,1,0:T(8,128)(2,1)}), bf16[8,128,128]{2,1,0:T(8,128)(2,1)}, u32[]{:S(2)}, u32[]{:S(2)}) %all-to-all-start.2) | async-done | bytes 262176 | tf_op jit(solution)/shard_map/all_to_all | solution.py:257
  112.8 7.1 %all-to-all-start.1 = ((bf16[8,256,128]{2,1,0:T(8,128)(2,1)}), bf16[8,256,128]{2,1,0:T(8,128)(2,1)}, u32[]{:S(2)}, u32[]{:S(2)}) async-start(bf16[8,256,128]{2,1,0:T(8,128)(2,1)} %copy-done.8), calls=%async_computation.1 | async-start | bytes 1048576 | tf_op jit(solution)/shard_map/all_to_all | solution.py:257
  119.9 1.9 collective-permute-start.20
  122.6 4.1 %all-to-all-done.1.refs_4_ = bf16[8,256,128]{2,1,0:T(8,128)(2,1)} async-done(((bf16[8,256,128]{2,1,0:T(8,128)(2,1)}), bf16[8,256,128]{2,1,0:T(8,128)(2,1)}, u32[]{:S(2)}, u32[]{:S(2)}) %all-to-all-start.1) | async-done | bytes 524320 | tf_op jit(solution)/shard_map/all_to_all | solution.py:257
  126.6 6.0 %all-to-all-start = ((bf16[8,128,128]{2,1,0:T(8,128)(2,1)}), bf16[8,128,128]{2,1,0:T(8,128)(2,1)}, u32[]{:S(2)}, u32[]{:S(2)}) async-start(bf16[8,128,128]{2,1,0:T(8,128)(2,1)} %get-tuple-element.21), calls=%async_computation | async-start | bytes 524288 | tf_op jit(solution)/shard_map/all_to_all | solution.py:257
  135.5 2.2 collective-permute-start.4
  139.8 16.2 %attend.5 = (bf16[144,1024]{1,0:T(8,128)(2,1)S(1)}, bf16[144,1024]{1,0:T(8,128)(2,1)S(1)}, bf16[144,1024]{1,0:T(8,128)(2,1)S(1)}, bf16[144,1024]{1,0:T(8,128)(2,1)S(1)}) custom-call(bf16[8,128,128]{2,1,0:T(8,128)(2,1)S(1)} %copy-done.24, bf16[8,128,128]{2,1,0:T(8,128)(2,1)} %collective-permute-done.18.refs_1_, ...), custom_call_target="tpu_custom_call" | custom-call | flops 8589934592 | bytes 6291456 | tf_op jit(solution)/shard_map/attend/pallas_call | solution.py:130
  158.3 5.7 %all-to-all-start.6 = ((bf16[8,384,128]{2,1,0:T(8,128)(2,1)}), bf16[8,384,128]{2,1,0:T(8,128)(2,1)}, u32[]{:S(2)}, u32[]{:S(2)}) async-start(bf16[8,384,128]{2,1,0:T(8,128)(2,1)} %copy-done.1), calls=%async_computation.6 | async-start | bytes 1572864 | tf_op jit(solution)/shard_map/all_to_all | solution.py:257
  164.8 2.6 collective-permute-start.1
  168.4 17.2 %attend.4 = (bf16[144,1024]{1,0:T(8,128)(2,1)S(1)}, bf16[144,1024]{1,0:T(8,128)(2,1)S(1)}, bf16[144,1024]{1,0:T(8,128)(2,1)}, bf16[144,1024]{1,0:T(8,128)(2,1)}) custom-call(bf16[8,128,128]{2,1,0:T(8,128)(2,1)} %all-to-all-done.2.refs_0_, bf16[8,128,128]{2,1,0:T(8,128)(2,1)} %collective-permute-done.9.refs_1_, ...), custom_call_target="tpu_custom_call" | custom-call | flops 8589934592 | bytes 6291456 | tf_op jit(solution)/shard_map/attend/pallas_call | solution.py:130
  188.3 3.0 %collective-permute-start.26 = (bf16[144,1024]{1,0:T(8,128)(2,1)S(1)}, bf16[144,1024]{1,0:T(8,128)(2,1)S(1)}, u32[]{:S(2)}, u32[]{:S(2)}) collective-permute-start(bf16[144,1024]{1,0:T(8,128)(2,1)S(1)} %copy-done.31), channel_id=1, source_target_pairs={{0,32},{8,40},{16,48},{24,56},{32,0},{40,8},{48,16},{56,24},{64,96... | collective-permute-start | bytes 884744 | tf_op jit(solution)/shard_map/ppermute | solution.py:253
  193.4 16.7 %attend.3 = (bf16[144,1024]{1,0:T(8,128)(2,1)S(1)}, bf16[144,1024]{1,0:T(8,128)(2,1)}, bf16[144,1024]{1,0:T(8,128)(2,1)}, bf16[144,1024]{1,0:T(8,128)(2,1)}) custom-call(bf16[8,128,128]{2,1,0:T(8,128)(2,1)} %all-to-all-done.refs_0_, bf16[8,128,128]{2,1,0:T(8,128)(2,1)S(1)} %collective-permute-done.refs_1_, ...), custom_call_target="tpu_custom_call" | custom-call | flops 8589934592 | bytes 6291456 | tf_op jit(solution)/shard_map/attend/pallas_call | solution.py:130
  212.9 2.6 collective-permute-start.6
  217.0 2.2 collective-permute-start.8
  219.2 30.1 %all_gather.3.kv_ref = bf16[384,768]{1,0:T(8,128)(2,1)} all-gather(bf16[24,768]{1,0:T(8,128)(2,1)S(1)} %pad_maximum_fusion), channel_id=1, replica_groups=mesh['wide'=16,'narrow'=8] {'wide'}, dimensions={0}, use_global_device_ids=true | all-gather | bytes 626688 | tf_op jit(solution)/shard_map/all_gather | solution.py:315
  250.4 4.0 %cross.1 = bf16[1024,384]{1,0:T(8,128)(2,1)} custom-call(s32[1]{0:T(128)S(6)} %copy.37.length_ref, bf16[8,384,128]{2,1,0:T(8,128)(2,1)} %all-to-all-done.6.c_ref, bf16[384,768]{1,0:T(8,128)(2,1)S(1)} %copy-done.6), custom_call_target="tpu_custom_call" | custom-call | flops 603979776 | bytes 3145728 | tf_op jit(solution)/shard_map/cross/pallas_call | solution.py:202
  260.2 3.9 %merge.1 = bf16[1024,384]{1,0:T(8,128)(2,1)} custom-call(bf16[144,1024]{1,0:T(8,128)(2,1)S(1)} %copy-done.22, bf16[144,1024]{1,0:T(8,128)(2,1)} %collective-permute-done.6.refs_1_, bf16[144,1024]{1,0:T(8,128)(2,1)} %collective-permute-done.7.refs_2_, bf16[144,1024]{1,0:T(8,128)(2,1)} %collective-permute-done.8.refs_3_, bf16[144,1024]{1,0:T(8,128)(2,1)S(1)} %copy-done.12, ...), custom_call_target="tpu_custom_call" | custom-call | flops 3145728 | bytes 4194304 | tf_op jit(solution)/shard_map/merge/pallas_call | solution.py:164
  (144 shorter events, 50.5 us)
Async XLA Ops:
  16.0 18.6 %all-to-all-start.4 = ((bf16[8,128,128]{2,1,0:T(8,128)(2,1)}), bf16[8,128,128]{2,1,0:T(8,128)(2,1)S(1)}, u32[]{:S(2)}, u32[]{:S(2)}) async-start(bf16[8,128,128]{2,1,0:T(8,128)(2,1)} %copy-done.26), calls=%async_computation.4 | async-start | bytes 524288 | tf_op jit(solution)/shard_map/all_to_all | solution.py:257
  59.4 12.8 %all-to-all-start.3 = ((bf16[8,256,128]{2,1,0:T(8,128)(2,1)}), bf16[8,256,128]{2,1,0:T(8,128)(2,1)}, u32[]{:S(2)}, u32[]{:S(2)}) async-start(bf16[8,256,128]{2,1,0:T(8,128)(2,1)} %copy-done.9), calls=%async_computation.3 | async-start | bytes 1048576 | tf_op jit(solution)/shard_map/all_to_all | solution.py:257
  73.0 19.3 %all-to-all-start.8 = ((f32[8,24,512]{2,1,0:T(8,128)}), f32[8,24,512]{2,1,0:T(8,128)}, u32[]{:S(2)}, u32[]{:S(2)}) async-start(f32[8,24,512]{2,1,0:T(8,128)} %broadcast_in_dim.11), calls=%async_computation.8 | async-start | bytes 786432 | tf_op jit(solution)/shard_map/all_to_all | solution.py:257
  84.6 35.3 %collective-permute-start.18 = (bf16[8,128,128]{2,1,0:T(8,128)(2,1)S(1)}, bf16[8,128,128]{2,1,0:T(8,128)(2,1)}, u32[]{:S(2)}, u32[]{:S(2)}) collective-permute-start(bf16[8,128,128]{2,1,0:T(8,128)(2,1)S(1)} %all-to-all-done.4.refs_0_), channel_id=1, source_target_pairs={{0,16},{8,24},{16,32},{24,40},{32,48},{40,56},{48,0},{56,8},{64,80... | collective-permute-start | bytes 786440 | tf_op jit(solution)/shard_map/ppermute | solution.py:253
  86.6 35.2 %collective-permute-start.19 = (bf16[8,128,128]{2,1,0:T(8,128)(2,1)S(1)}, bf16[8,128,128]{2,1,0:T(8,128)(2,1)}, u32[]{:S(2)}, u32[]{:S(2)}) collective-permute-start(bf16[8,128,128]{2,1,0:T(8,128)(2,1)S(1)} %all-to-all-done.4.refs_0_), channel_id=1, source_target_pairs={{0,48},{8,56},{16,0},{24,8},{32,16},{40,24},{48,32},{56,40},{64,11... | collective-permute-start | bytes 786440 | tf_op jit(solution)/shard_map/ppermute | solution.py:253
  88.8 18.7 %collective-permute-start.22 = (bf16[8,256,128]{2,1,0:T(8,128)(2,1)}, bf16[8,256,128]{2,1,0:T(8,128)(2,1)}, u32[]{:S(2)}, u32[]{:S(2)}) collective-permute-start(bf16[8,256,128]{2,1,0:T(8,128)(2,1)} %all_to_all.46.refs_4_), channel_id=1, source_target_pairs={{0,64},{8,72},{16,80},{24,88},{32,96},{40,104},{48,112},{56,120},{... | collective-permute-start | bytes 1572872 | tf_op jit(solution)/shard_map/ppermute | solution.py:253
  90.2 45.3 %collective-permute-start.21 = (bf16[8,256,128]{2,1,0:T(8,128)(2,1)}, bf16[8,256,128]{2,1,0:T(8,128)(2,1)}, u32[]{:S(2)}, u32[]{:S(2)}) collective-permute-start(bf16[8,256,128]{2,1,0:T(8,128)(2,1)} %all_to_all.46.refs_4_), channel_id=1, source_target_pairs={{0,8},{8,0},{16,24},{24,16},{32,40},{40,32},{48,56},{56,48},{64,72... | collective-permute-start | bytes 1572872 | tf_op jit(solution)/shard_map/ppermute | solution.py:253
  90.2 45.3 %collective-permute-start.13 = (bf16[8,256,128]{2,1,0:T(8,128)(2,1)}, bf16[8,256,128]{2,1,0:T(8,128)(2,1)}, u32[]{:S(2)}, u32[]{:S(2)}) collective-permute-start(bf16[8,256,128]{2,1,0:T(8,128)(2,1)} %all-to-all-done.3.refs_4_), channel_id=1, source_target_pairs={{0,64},{8,72},{16,80},{24,88},{32,96},{40,104},{48,112},{56,120},{... | collective-permute-start | bytes 1572872 | tf_op jit(solution)/shard_map/ppermute | solution.py:253
  92.3 20.5 %all-to-all-start.2 = ((bf16[8,128,128]{2,1,0:T(8,128)(2,1)}), bf16[8,128,128]{2,1,0:T(8,128)(2,1)}, u32[]{:S(2)}, u32[]{:S(2)}) async-start(bf16[8,128,128]{2,1,0:T(8,128)(2,1)} %copy-done.25), calls=%async_computation.2 | async-start | bytes 524288 | tf_op jit(solution)/shard_map/all_to_all | solution.py:257
  107.4 30.2 %collective-permute-start.23 = (bf16[8,256,128]{2,1,0:T(8,128)(2,1)}, bf16[8,256,128]{2,1,0:T(8,128)(2,1)}, u32[]{:S(2)}, u32[]{:S(2)}) collective-permute-start(bf16[8,256,128]{2,1,0:T(8,128)(2,1)} %collective-permute-done.22.refs_6_), channel_id=1, source_target_pairs={{0,8},{8,0},{16,24},{24,16},{32,40},{40,32},{48,56},{56,48},{64,72... | collective-permute-start | bytes 1572872 | tf_op jit(solution)/shard_map/ppermute | solution.py:253
  112.8 13.8 %all-to-all-start.1 = ((bf16[8,256,128]{2,1,0:T(8,128)(2,1)}), bf16[8,256,128]{2,1,0:T(8,128)(2,1)}, u32[]{:S(2)}, u32[]{:S(2)}) async-start(bf16[8,256,128]{2,1,0:T(8,128)(2,1)} %copy-done.8), calls=%async_computation.1 | async-start | bytes 1048576 | tf_op jit(solution)/shard_map/all_to_all | solution.py:257
  126.6 31.6 %all-to-all-start = ((bf16[8,128,128]{2,1,0:T(8,128)(2,1)}), bf16[8,128,128]{2,1,0:T(8,128)(2,1)}, u32[]{:S(2)}, u32[]{:S(2)}) async-start(bf16[8,128,128]{2,1,0:T(8,128)(2,1)} %get-tuple-element.21), calls=%async_computation | async-start | bytes 524288 | tf_op jit(solution)/shard_map/all_to_all | solution.py:257
  132.7 31.3 %collective-permute-start.11 = (bf16[8,128,128]{2,1,0:T(8,128)(2,1)}, bf16[8,128,128]{2,1,0:T(8,128)(2,1)}, u32[]{:S(2)}, u32[]{:S(2)}) collective-permute-start(bf16[8,128,128]{2,1,0:T(8,128)(2,1)} %all-to-all-done.2.refs_0_), channel_id=1, source_target_pairs={{0,32},{8,40},{16,48},{24,56},{32,0},{40,8},{48,16},{56,24},{64,96... | collective-permute-start | bytes 786440 | tf_op jit(solution)/shard_map/ppermute | solution.py:253
  134.4 30.3 %collective-permute-start.9 = (bf16[8,128,128]{2,1,0:T(8,128)(2,1)}, bf16[8,128,128]{2,1,0:T(8,128)(2,1)}, u32[]{:S(2)}, u32[]{:S(2)}) collective-permute-start(bf16[8,128,128]{2,1,0:T(8,128)(2,1)} %all-to-all-done.2.refs_0_), channel_id=1, source_target_pairs={{0,16},{8,24},{16,32},{24,40},{32,48},{40,56},{48,0},{56,8},{64,80... | collective-permute-start | bytes 786440 | tf_op jit(solution)/shard_map/ppermute | solution.py:253
  135.5 31.8 %collective-permute-start.12 = (bf16[8,256,128]{2,1,0:T(8,128)(2,1)}, bf16[8,256,128]{2,1,0:T(8,128)(2,1)}, u32[]{:S(2)}, u32[]{:S(2)}) collective-permute-start(bf16[8,256,128]{2,1,0:T(8,128)(2,1)} %all-to-all-done.3.refs_4_), channel_id=1, source_target_pairs={{0,8},{8,0},{16,24},{24,16},{32,40},{40,32},{48,56},{56,48},{64,72... | collective-permute-start | bytes 1572872 | tf_op jit(solution)/shard_map/ppermute | solution.py:253
  135.5 32.4 %collective-permute-start.4 = (bf16[8,256,128]{2,1,0:T(8,128)(2,1)}, bf16[8,256,128]{2,1,0:T(8,128)(2,1)}, u32[]{:S(2)}, u32[]{:S(2)}) collective-permute-start(bf16[8,256,128]{2,1,0:T(8,128)(2,1)} %all-to-all-done.1.refs_4_), channel_id=1, source_target_pairs={{0,64},{8,72},{16,80},{24,88},{32,96},{40,104},{48,112},{56,120},{... | collective-permute-start | bytes 1572872 | tf_op jit(solution)/shard_map/ppermute | solution.py:253
  137.7 30.2 %collective-permute-start.14 = (bf16[8,256,128]{2,1,0:T(8,128)(2,1)}, bf16[8,256,128]{2,1,0:T(8,128)(2,1)}, u32[]{:S(2)}, u32[]{:S(2)}) collective-permute-start(bf16[8,256,128]{2,1,0:T(8,128)(2,1)} %collective-permute-done.13.refs_6_), channel_id=1, source_target_pairs={{0,8},{8,0},{16,24},{24,16},{32,40},{40,32},{48,56},{56,48},{64,72... | collective-permute-start | bytes 1572872 | tf_op jit(solution)/shard_map/ppermute | solution.py:253
  158.3 91.1 %all-to-all-start.6 = ((bf16[8,384,128]{2,1,0:T(8,128)(2,1)}), bf16[8,384,128]{2,1,0:T(8,128)(2,1)}, u32[]{:S(2)}, u32[]{:S(2)}) async-start(bf16[8,384,128]{2,1,0:T(8,128)(2,1)} %copy-done.1), calls=%async_computation.6 | async-start | bytes 1572864 | tf_op jit(solution)/shard_map/all_to_all | solution.py:257
  164.0 22.3 %collective-permute-start = (bf16[8,128,128]{2,1,0:T(8,128)(2,1)}, bf16[8,128,128]{2,1,0:T(8,128)(2,1)S(1)}, u32[]{:S(2)}, u32[]{:S(2)}) collective-permute-start(bf16[8,128,128]{2,1,0:T(8,128)(2,1)} %all-to-all-done.refs_0_), channel_id=1, source_target_pairs={{0,16},{8,24},{16,32},{24,40},{32,48},{40,56},{48,0},{56,8},{64,80... | collective-permute-start | bytes 786440 | tf_op jit(solution)/shard_map/ppermute | solution.py:253
  164.8 23.2 %collective-permute-start.1 = (bf16[8,128,128]{2,1,0:T(8,128)(2,1)}, bf16[8,128,128]{2,1,0:T(8,128)(2,1)S(1)}, u32[]{:S(2)}, u32[]{:S(2)}) collective-permute-start(bf16[8,128,128]{2,1,0:T(8,128)(2,1)} %all-to-all-done.refs_0_), channel_id=1, source_target_pairs={{0,48},{8,56},{16,0},{24,8},{32,16},{40,24},{48,32},{56,40},{64,11... | collective-permute-start | bytes 786440 | tf_op jit(solution)/shard_map/ppermute | solution.py:253
  167.3 21.0 %collective-permute-start.2 = (bf16[8,128,128]{2,1,0:T(8,128)(2,1)}, bf16[8,128,128]{2,1,0:T(8,128)(2,1)S(1)}, u32[]{:S(2)}, u32[]{:S(2)}) collective-permute-start(bf16[8,128,128]{2,1,0:T(8,128)(2,1)} %all-to-all-done.refs_0_), channel_id=1, source_target_pairs={{0,32},{8,40},{16,48},{24,56},{32,0},{40,8},{48,16},{56,24},{64,96... | collective-permute-start | bytes 786440 | tf_op jit(solution)/shard_map/ppermute | solution.py:253
  167.8 23.5 %collective-permute-start.3 = (bf16[8,256,128]{2,1,0:T(8,128)(2,1)}, bf16[8,256,128]{2,1,0:T(8,128)(2,1)S(1)}, u32[]{:S(2)}, u32[]{:S(2)}) collective-permute-start(bf16[8,256,128]{2,1,0:T(8,128)(2,1)} %all-to-all-done.1.refs_4_), channel_id=1, source_target_pairs={{0,8},{8,0},{16,24},{24,16},{32,40},{40,32},{48,56},{56,48},{64,72... | collective-permute-start | bytes 1572872 | tf_op jit(solution)/shard_map/ppermute | solution.py:253
  167.8 24.5 %collective-permute-start.5 = (bf16[8,256,128]{2,1,0:T(8,128)(2,1)}, bf16[8,256,128]{2,1,0:T(8,128)(2,1)S(1)}, u32[]{:S(2)}, u32[]{:S(2)}) collective-permute-start(bf16[8,256,128]{2,1,0:T(8,128)(2,1)} %collective-permute-done.4.refs_6_), channel_id=1, source_target_pairs={{0,8},{8,0},{16,24},{24,16},{32,40},{40,32},{48,56},{56,48},{64,72... | collective-permute-start | bytes 1572872 | tf_op jit(solution)/shard_map/ppermute | solution.py:253
  186.3 24.5 %collective-permute-start.24 = (bf16[144,1024]{1,0:T(8,128)(2,1)S(1)}, bf16[144,1024]{1,0:T(8,128)(2,1)S(1)}, u32[]{:S(2)}, u32[]{:S(2)}) collective-permute-start(bf16[144,1024]{1,0:T(8,128)(2,1)S(1)} %copy-done.35), channel_id=1, source_target_pairs={{0,48},{8,56},{16,0},{24,8},{32,16},{40,24},{48,32},{56,40},{64,11... | collective-permute-start | bytes 884744 | tf_op jit(solution)/shard_map/ppermute | solution.py:253
  187.9 24.3 %collective-permute-start.25 = (bf16[144,1024]{1,0:T(8,128)(2,1)S(1)}, bf16[144,1024]{1,0:T(8,128)(2,1)S(1)}, u32[]{:S(2)}, u32[]{:S(2)}) collective-permute-start(bf16[144,1024]{1,0:T(8,128)(2,1)S(1)} %copy-done.33), channel_id=1, source_target_pairs={{0,16},{8,24},{16,32},{24,40},{32,48},{40,56},{48,0},{56,8},{64,80... | collective-permute-start | bytes 884744 | tf_op jit(solution)/shard_map/ppermute | solution.py:253
  188.3 27.2 %collective-permute-start.26 = (bf16[144,1024]{1,0:T(8,128)(2,1)S(1)}, bf16[144,1024]{1,0:T(8,128)(2,1)S(1)}, u32[]{:S(2)}, u32[]{:S(2)}) collective-permute-start(bf16[144,1024]{1,0:T(8,128)(2,1)S(1)} %copy-done.31), channel_id=1, source_target_pairs={{0,32},{8,40},{16,48},{24,56},{32,0},{40,8},{48,16},{56,24},{64,96... | collective-permute-start | bytes 884744 | tf_op jit(solution)/shard_map/ppermute | solution.py:253
  191.3 25.0 %collective-permute-start.15 = (bf16[144,1024]{1,0:T(8,128)(2,1)S(1)}, bf16[144,1024]{1,0:T(8,128)(2,1)S(1)}, u32[]{:S(2)}, u32[]{:S(2)}) collective-permute-start(bf16[144,1024]{1,0:T(8,128)(2,1)S(1)} %get-tuple-element.30), channel_id=1, source_target_pairs={{0,48},{8,56},{16,0},{24,8},{32,16},{40,24},{48,32},{56,40},{64,11... | collective-permute-start | bytes 884744 | tf_op jit(solution)/shard_map/ppermute | solution.py:253
  192.3 62.1 %collective-permute-start.16 = (bf16[144,1024]{1,0:T(8,128)(2,1)}, bf16[144,1024]{1,0:T(8,128)(2,1)}, u32[]{:S(2)}, u32[]{:S(2)}) collective-permute-start(bf16[144,1024]{1,0:T(8,128)(2,1)} %get-tuple-element.31), channel_id=1, source_target_pairs={{0,16},{8,24},{16,32},{24,40},{32,48},{40,56},{48,0},{56,8},{64,80... | collective-permute-start | bytes 884744 | tf_op jit(solution)/shard_map/ppermute | solution.py:253
  211.5 43.0 %collective-permute-start.17 = (bf16[144,1024]{1,0:T(8,128)(2,1)}, bf16[144,1024]{1,0:T(8,128)(2,1)}, u32[]{:S(2)}, u32[]{:S(2)}) collective-permute-start(bf16[144,1024]{1,0:T(8,128)(2,1)} %get-tuple-element.32), channel_id=1, source_target_pairs={{0,32},{8,40},{16,48},{24,56},{32,0},{40,8},{48,16},{56,24},{64,96... | collective-permute-start | bytes 884744 | tf_op jit(solution)/shard_map/ppermute | solution.py:253
  212.9 41.5 %collective-permute-start.6 = (bf16[144,1024]{1,0:T(8,128)(2,1)}, bf16[144,1024]{1,0:T(8,128)(2,1)}, u32[]{:S(2)}, u32[]{:S(2)}) collective-permute-start(bf16[144,1024]{1,0:T(8,128)(2,1)} %get-tuple-element.24), channel_id=1, source_target_pairs={{0,48},{8,56},{16,0},{24,8},{32,16},{40,24},{48,32},{56,40},{64,11... | collective-permute-start | bytes 884744 | tf_op jit(solution)/shard_map/ppermute | solution.py:253
  216.3 38.2 %collective-permute-start.7 = (bf16[144,1024]{1,0:T(8,128)(2,1)}, bf16[144,1024]{1,0:T(8,128)(2,1)}, u32[]{:S(2)}, u32[]{:S(2)}) collective-permute-start(bf16[144,1024]{1,0:T(8,128)(2,1)} %get-tuple-element.25), channel_id=1, source_target_pairs={{0,16},{8,24},{16,32},{24,40},{32,48},{40,56},{48,0},{56,8},{64,80... | collective-permute-start | bytes 884744 | tf_op jit(solution)/shard_map/ppermute | solution.py:253
  217.0 37.4 %collective-permute-start.8 = (bf16[144,1024]{1,0:T(8,128)(2,1)}, bf16[144,1024]{1,0:T(8,128)(2,1)}, u32[]{:S(2)}, u32[]{:S(2)}) collective-permute-start(bf16[144,1024]{1,0:T(8,128)(2,1)} %get-tuple-element.26), channel_id=1, source_target_pairs={{0,32},{8,40},{16,48},{24,56},{32,0},{40,8},{48,16},{56,24},{64,96... | collective-permute-start | bytes 884744 | tf_op jit(solution)/shard_map/ppermute | solution.py:253
  (41 other events, 400.9 us)

commit v2 on v1

v2 whole, which is shorter than its diff:
```python
import math

import jax
import jax.numpy as jnp
from jax import lax
from jax.experimental import pallas as pl
from jax.experimental.pallas import tpu as pltpu
from jax.sharding import PartitionSpec as P

HEAD = 128
EPS = 1e-06
SCALE = math.log2(math.e) / math.sqrt(HEAD)
TILE = 512
CHUNK = 2048
EXTRA = 16
SLOT = 32


def vmem(mib):
    return pltpu.CompilerParams(vmem_limit_bytes=mib * 2**20)


def normed(ref, gain_ref, at, factor):
    x = ref[:, at].astype(jnp.float32)
    inverse = lax.rsqrt(jnp.mean(x * x, axis=-1, keepdims=True) + EPS)
    return (x * inverse * (gain_ref[:, at] * factor)).astype(jnp.bfloat16)


def pack_kernel(heads, plan, q_ref, k_ref, v_ref, qg_ref, kg_ref, *rest):
    groups = rest[-1].shape[0]
    outs = rest[2:] if plan["crossed"] else rest

    def group(n, _):
        for h, out, base in plan["heads"]:
            at = pl.ds(pl.multiple_of((n * heads + h) * HEAD, HEAD), HEAD)
            ref = outs[out]
            ref[n, base : base + HEAD, :] = normed(k_ref, kg_ref, at, 1.0)
            ref[n, base + HEAD : base + 2 * HEAD, :] = (
                v_ref[:, at].astype(jnp.float32).T.astype(jnp.bfloat16)
            )
            ref[n, base + 2 * HEAD : base + 3 * HEAD, :] = normed(q_ref, qg_ref, at, SCALE)
        for h, out, base in plan["crossed"]:
            at = pl.ds(pl.multiple_of((n * heads + h) * HEAD, HEAD), HEAD)
            outs[out][n, base : base + HEAD, :] = normed(rest[0], rest[1], at, SCALE)
        return 0

    lax.fori_loop(0, groups, group, 0)


def pack(arrays, gains, groups, heads, plan, depths):
    whole = pl.BlockSpec(memory_space=pltpu.VMEM)
    operands = list(arrays[:3]) + [gain[None, :] for gain in gains[:2]]
    if plan["crossed"]:
        operands += [arrays[3], gains[2][None, :]]
    units = 3 * len(plan["heads"]) + len(plan["crossed"])
    return pl.pallas_call(
        lambda *refs: pack_kernel(heads, plan, *refs),
        in_specs=[whole] * len(operands),
        out_specs=[whole] * len(depths),
        out_shape=[
            jax.ShapeDtypeStruct((groups, depth, HEAD), jnp.bfloat16) for depth in depths
        ],
        compiler_params=vmem(56),
        cost_estimate=pl.CostEstimate(
            flops=8 * arrays[0].size, bytes_accessed=units * 2**20, transcendentals=0
        ),
        name="pack",
    )(*operands)


def words(block):
    high = block.astype(jnp.bfloat16)
    return high, (block - high.astype(jnp.float32)).astype(jnp.bfloat16)


def feed_kernel(x_ref, gain_ref, gate_ref, up_ref, down_ref, out_ref, rows_ref, total):
    step = pl.program_id(0)

    @pl.when(step == 0)
    def _():
        x = x_ref[...].astype(jnp.float32)
        inverse = lax.rsqrt(jnp.mean(x * x, axis=-1, keepdims=True) + EPS)
        rows = x * inverse * gain_ref[...]
        spare = jnp.zeros((SLOT - x.shape[0], x.shape[1]), jnp.float32)
        rows_ref[...] = jnp.concatenate([rows, spare], axis=0).astype(jnp.bfloat16)
        total[...] = jnp.zeros_like(total)

    rows = rows_ref[...]
    gate = jnp.dot(rows, gate_ref[...], preferred_element_type=jnp.float32)
    upward = jnp.dot(rows, up_ref[...], preferred_element_type=jnp.float32)
    hidden = (jax.nn.gelu(gate, approximate=True) * upward).astype(jnp.bfloat16)
    total[...] += jnp.dot(hidden, down_ref[...], preferred_element_type=jnp.float32)

    @pl.when(step == pl.num_programs(0) - 1)
    def _():
        groups = out_ref.shape[0]
        each = total.shape[1] // groups // HEAD
        for n in range(groups):
            for j in range(each):
                at = (n * each + j) * HEAD
                high, low = words(total[:, at : at + HEAD])
                out_ref[n, j * SLOT : (j + 1) * SLOT, :] = high
                out_ref[n, (each + j) * SLOT : (each + j + 1) * SLOT, :] = low


def feed(x, gain, gate, up, down, groups, extra):
    width, hidden = gate.shape
    tile = HEAD
    return pl.pallas_call(
        feed_kernel,
        grid=(hidden // tile,),
        in_specs=[
            pl.BlockSpec(x.shape, lambda i: (0, 0)),
            pl.BlockSpec((1, width), lambda i: (0, 0)),
            pl.BlockSpec((width, tile), lambda i: (0, i)),
            pl.BlockSpec((width, tile), lambda i: (0, i)),
            pl.BlockSpec((tile, width), lambda i: (i, 0)),
        ],
        out_specs=pl.BlockSpec((groups, extra, HEAD), lambda i: (0, 0, 0)),
        out_shape=jax.ShapeDtypeStruct((groups, extra, HEAD), jnp.bfloat16),
        scratch_shapes=[
            pltpu.VMEM((SLOT, width), jnp.bfloat16),
            pltpu.VMEM((SLOT, width), jnp.float32),
        ],
        compiler_params=vmem(56),
        cost_estimate=pl.CostEstimate(
            flops=6 * SLOT * width * hidden,
            bytes_accessed=6 * width * hidden,
            transcendentals=SLOT * hidden,
        ),
        name="feed",
    )(x, gain[None, :], gate, up, down)


def fold_kernel(parts_ref, _, out_ref):
    groups, depth, _ = parts_ref.shape
    half = depth // 2
    total = jnp.zeros((half, HEAD), jnp.float32)
    for n in range(groups):
        total = total + parts_ref[n, :half, :].astype(jnp.float32)
        total = total + parts_ref[n, half:, :].astype(jnp.float32)
    high, low = words(total)
    for n in range(groups):
        out_ref[n, :half, :] = high
        out_ref[n, half:, :] = low


def fold(parts, into):
    block = pl.BlockSpec(parts.shape, lambda i: (0, 0, 0))
    return pl.pallas_call(
        fold_kernel,
        grid=(1,),
        in_specs=[block, pl.BlockSpec(memory_space=pl.ANY)],
        out_specs=block,
        out_shape=jax.ShapeDtypeStruct(into.shape, into.dtype),
        input_output_aliases={1: 0},
        compiler_params=vmem(56),
        cost_estimate=pl.CostEstimate(
            flops=2**18, bytes_accessed=2**20, transcendentals=0
        ),
        name="fold",
    )(parts, into)


def project_kernel(x_ref, parts_ref, gain_ref, key_ref, value_ref, key_gain_ref, out_ref, text):
    h = pl.program_id(0)

    @pl.when(h == 0)
    def _():
        groups, depth, _ = parts_ref.shape
        each = depth // SLOT // 2
        count = x_ref.shape[0]
        columns = []
        for n in range(groups):
            for j in range(each):
                high = parts_ref[n, j * SLOT : (j + 1) * SLOT, :].astype(jnp.float32)
                low = parts_ref[n, (each + j) * SLOT : (each + j + 1) * SLOT, :]
                columns.append((high + low.astype(jnp.float32))[:count])
        x = x_ref[...].astype(jnp.float32) + jnp.concatenate(columns, axis=1)
        inverse = lax.rsqrt(jnp.mean(x * x, axis=-1, keepdims=True) + EPS)
        rows = x * inverse * gain_ref[...]
        spare = jnp.zeros((SLOT - count, x.shape[1]), jnp.float32)
        text[...] = jnp.concatenate([rows, spare], axis=0).astype(jnp.bfloat16)

    rows = text[...]
    keys = jnp.dot(rows, key_ref[...], preferred_element_type=jnp.float32)
    inverse = lax.rsqrt(jnp.mean(keys * keys, axis=-1, keepdims=True) + EPS)
    keys = (keys * inverse * key_gain_ref[...]).astype(jnp.bfloat16)
    values = jnp.dot(rows, value_ref[...], preferred_element_type=jnp.float32)
    values = values.astype(jnp.bfloat16)
    for n in range(out_ref.shape[0]):
        out_ref[n, :SLOT, :] = keys
        out_ref[n, SLOT:, :] = values


def project(x, parts, gain, key, value, key_gain, extra, copies):
    width, part = key.shape
    heads = part // HEAD
    weight = pl.BlockSpec((width, HEAD), lambda h: (0, h))
    return pl.pallas_call(
        project_kernel,
        grid=(heads,),
        in_specs=[
            pl.BlockSpec(x.shape, lambda h: (0, 0)),
            pl.BlockSpec((parts.shape[0], extra, HEAD), lambda h: (0, 0, 0)),
            pl.BlockSpec((1, width), lambda h: (0, 0)),
            weight,
            weight,
            pl.BlockSpec((1, HEAD), lambda h: (0, h)),
        ],
        out_specs=pl.BlockSpec((copies, 2 * SLOT, HEAD), lambda h: (0, h, 0)),
        out_shape=jax.ShapeDtypeStruct((copies, heads * 2 * SLOT, HEAD), jnp.bfloat16),
        scratch_shapes=[pltpu.VMEM((SLOT, width), jnp.bfloat16)],
        compiler_params=vmem(56),
        cost_estimate=pl.CostEstimate(
            flops=4 * SLOT * width * part, bytes_accessed=4 * width * part, transcendentals=0
        ),
        name="project",
    )(x, parts, gain[None, :], key, value, key_gain[None, :])


def attend_kernel(views, nq, nkv, ring, *refs):
    inputs, outs = refs[: len(views)], refs[len(views) : -5]
    q_s, k_s, v_s, o_s, sems = refs[-5:]
    blocks = q_s.shape[0] // nq
    copies = []
    counts = [0, 0]
    for ref, (kind, start) in zip(inputs, views):
        pieces = [ref] if len(ref.shape) == 3 else [ref.at[i] for i in range(ref.shape[0])]
        for piece in pieces:
            rows = pl.ds(counts[kind] * blocks, blocks)
            counts[kind] += 1
            targets = ((0, q_s),) if kind == 0 else ((0, k_s), (HEAD, v_s))
            for offset, scratch in targets:
                copies.append((piece.at[:, pl.ds(start + offset, HEAD), :], scratch.at[rows]))
    copies = [
        pltpu.make_async_copy(src, dst, sems.at[i]) for i, (src, dst) in enumerate(copies)
    ]
    for copy in copies:
        copy.start()
    for copy in copies:
        copy.wait()
    per_q = TILE // HEAD
    per_k = CHUNK // HEAD
    per_block = blocks // per_q

    def tile(t, _):
        q = q_s[pl.ds(t * per_q, per_q)].reshape(TILE, HEAD)
        acc = jnp.zeros((HEAD, TILE), jnp.float32)
        total = jnp.zeros((8, TILE), jnp.float32)
        for j in range(nkv * blocks // per_k):
            keys = k_s[j * per_k : (j + 1) * per_k].reshape(CHUNK, HEAD)
            s = lax.dot_general(
                keys, q, (((1,), (1,)), ((), ())), preferred_element_type=jnp.float32
            )
            p = jnp.exp2(s)
            total = total + jnp.sum(p.reshape(CHUNK // 8, 8, TILE), axis=0)
            values = jnp.concatenate(
                [v_s[j * per_k + i] for i in range(per_k)], axis=1
            )
            acc = acc + jnp.dot(
                values, p.astype(jnp.bfloat16), preferred_element_type=jnp.float32
            )
        row = jnp.sum(total, axis=0, keepdims=True)
        high = row.astype(jnp.bfloat16).astype(jnp.float32)
        words = jnp.concatenate(
            [jnp.broadcast_to(high, (8, TILE)), jnp.broadcast_to(row - high, (8, TILE))], axis=0
        )
        columns = pl.ds(pl.multiple_of((t % per_block) * TILE, TILE), TILE)
        slot = t // per_block
        if ring is not None:
            slot = ring(slot)
        o_s[slot, :HEAD, columns] = acc.astype(jnp.bfloat16)
        o_s[slot, HEAD:, columns] = words.astype(jnp.bfloat16)
        return 0

    lax.fori_loop(0, nq * per_block, tile, 0)
    if ring is not None:
        copies = [pltpu.make_async_copy(o_s, outs[0], sems.at[0])]
    else:
        copies = [
            pltpu.make_async_copy(o_s.at[i], ref, sems.at[i]) for i, ref in enumerate(outs)
        ]
    for copy in copies:
        copy.start()
    for copy in copies:
        copy.wait()


def attend(queries, pairs, ring=None):
    arrays = [array for array, _ in queries + pairs]
    views = [(0, start) for _, start in queries] + [(1, start) for _, start in pairs]
    nq, nkv = (sum(math.prod(a.shape[:-3]) for a, _ in part) for part in (queries, pairs))
    blocks = arrays[0].shape[-3]
    count = blocks * HEAD
    work = nq * nkv * count * count
    shapes = [jax.ShapeDtypeStruct((HEAD + EXTRA, count), jnp.bfloat16)] * nq
    if ring is not None:
        shapes = [jax.ShapeDtypeStruct((nq, HEAD + EXTRA, count), jnp.bfloat16)]
    return pl.pallas_call(
        lambda *refs: attend_kernel(views, nq, nkv, ring, *refs),
        in_specs=[pl.BlockSpec(memory_space=pl.ANY)] * len(arrays),
        out_specs=[pl.BlockSpec(memory_space=pl.ANY)] * len(shapes),
        out_shape=shapes,
        scratch_shapes=[
            pltpu.VMEM((nq * blocks, HEAD, HEAD), jnp.bfloat16),
            pltpu.VMEM((nkv * blocks, HEAD, HEAD), jnp.bfloat16),
            pltpu.VMEM((nkv * blocks, HEAD, HEAD), jnp.bfloat16),
            pltpu.VMEM((nq, HEAD + EXTRA, count), jnp.bfloat16),
            pltpu.SemaphoreType.DMA((nq + 2 * nkv,)),
        ],
        compiler_params=vmem(56),
        cost_estimate=pl.CostEstimate(
            flops=4 * HEAD * work, bytes_accessed=6 * 2**20, transcendentals=work
        ),
        name="attend",
    )(*arrays)


def merge_kernel(sizes, *refs):
    out_ref = refs[-1]
    refs = list(refs[:-1])
    for h, size in enumerate(sizes):
        group, refs = refs[:size], refs[size:]
        if size == 1:
            group = [group[0].at[i] for i in range(group[0].shape[0])]
        weighted = sum(ref[:HEAD, :].astype(jnp.float32) for ref in group)
        pieces = sum(ref[HEAD:, :].astype(jnp.float32) for ref in group)
        total = pieces[0:1] + pieces[8:9]
        out_ref[:, h * HEAD : (h + 1) * HEAD] = (weighted / total).T.astype(jnp.bfloat16)


def merge(results):
    heads = len(results)
    arrays = [array for group in results for array in group]
    sizes = [len(group) for group in results]
    count = arrays[0].shape[-1]
    step = 256
    specs = []
    for array in arrays:
        if array.ndim == 2:
            specs.append(pl.BlockSpec((array.shape[0], step), lambda i: (0, i)))
        else:
            specs.append(pl.BlockSpec(array.shape[:2] + (step,), lambda i: (0, 0, i)))
    return pl.pallas_call(
        lambda *refs: merge_kernel(sizes, *refs),
        grid=(count // step,),
        in_specs=specs,
        out_specs=pl.BlockSpec((step, heads * HEAD), lambda i: (i, 0)),
        out_shape=jax.ShapeDtypeStruct((count, heads * HEAD), jnp.bfloat16),
        compiler_params=vmem(56),
        cost_estimate=pl.CostEstimate(
            flops=count * heads * HEAD * 8, bytes_accessed=4 * 2**20, transcendentals=0
        ),
        name="merge",
    )(*arrays)


def cross_kernel(start, per, length_ref, c_ref, kv_ref, out_ref):
    live = length_ref[0]
    blocks = c_ref.shape[0]
    sources = kv_ref.shape[0]
    count = sources * SLOT
    tile = blocks * HEAD
    row = lax.broadcasted_iota(jnp.int32, (count, tile), 0)
    source, slot = row // SLOT, row % SLOT
    alive = (slot < per) & (source * per + slot < live)
    for h in range(kv_ref.shape[1] // (2 * SLOT)):
        at = 2 * h * SLOT
        keys = kv_ref[:, at : at + SLOT, :].reshape(count, HEAD)
        values = kv_ref[:, at + SLOT : at + 2 * SLOT, :].reshape(count, HEAD)
        values = values.astype(jnp.float32).T.astype(jnp.bfloat16)
        first = start + h * HEAD
        q = c_ref[:, first : first + HEAD, :].reshape(tile, HEAD)
        s = lax.dot_general(
            keys, q, (((1,), (1,)), ((), ())), preferred_element_type=jnp.float32
        )
        p = jnp.where(alive, jnp.exp2(s), 0.0)
        total = jnp.sum(p, axis=0, keepdims=True)
        weighted = jnp.dot(values, p.astype(jnp.bfloat16), preferred_element_type=jnp.float32)
        out_ref[:, h * HEAD : (h + 1) * HEAD] = (weighted / total).T.astype(jnp.bfloat16)


def cross(lengths, c, start, kv, per):
    blocks, depth, _ = c.shape
    step = 4
    heads = kv.shape[1] // (2 * SLOT)
    return pl.pallas_call(
        lambda *refs: cross_kernel(start, per, *refs),
        grid=(blocks // step,),
        in_specs=[
            pl.BlockSpec(memory_space=pltpu.SMEM),
            pl.BlockSpec((step, depth, HEAD), lambda i: (i, 0, 0)),
            pl.BlockSpec(kv.shape, lambda i: (0, 0, 0)),
        ],
        out_specs=pl.BlockSpec((step * HEAD, heads * HEAD), lambda i: (i, 0)),
        out_shape=jax.ShapeDtypeStruct((blocks * HEAD, heads * HEAD), jnp.bfloat16),
        compiler_params=vmem(56),
        cost_estimate=pl.CostEstimate(
            flops=4 * HEAD * heads * blocks * HEAD * kv.shape[0] * SLOT,
            bytes_accessed=3 * 2**20,
            transcendentals=heads * blocks * HEAD * kv.shape[0] * SLOT,
        ),
        name="cross",
    )(lengths, c, kv)


def spot(hi, z, core):
    return hi * 8 + z * 2 + core


def wide_pairs(move):
    places = [(hi, z, core) for hi in range(2) for z in range(4) for core in range(2)]
    return [(spot(*place), spot(*move(*place))) for place in places]


UP = wide_pairs(lambda hi, z, core: (hi, (z + 1) % 4, core))
DOWN = wide_pairs(lambda hi, z, core: (hi, (z + 3) % 4, core))
ACROSS = wide_pairs(lambda hi, z, core: (hi, (z + 2) % 4, core))
OTHER_X = wide_pairs(lambda hi, z, core: (1 - hi, z, core))
OTHER_CORE = wide_pairs(lambda hi, z, core: (hi, z, 1 - core))
ALONG_Z = [[spot(hi, z, core) for z in range(4)] for hi in range(2) for core in range(2)]
ALONG_X = [[spot(hi, z, core) for hi in range(2) for core in range(2)] for z in range(4)]


def send(array, pairs):
    return lax.ppermute(array, "wide", pairs)


def collect(array, groups):
    return lax.all_gather(array, "wide", axis=0, axis_index_groups=groups)


def give_back(parts):
    own, below, above, across = parts
    return [own, send(below, DOWN), send(above, UP), send(across, ACROSS)]


def trade_back(parts):
    return lax.all_to_all(
        parts, "wide", split_axis=0, concat_axis=0, axis_index_groups=ALONG_Z, tiled=True
    )


def from_ring(block):
    z = lax.axis_index("wide") // 2 % 4
    shift = jnp.where(block == 1, 3, jnp.where(block == 2, 1, jnp.where(block == 3, 2, 0)))
    return (z + shift) % 4


def around(array):
    return [send(array, UP), send(array, DOWN), send(array, ACROSS)]


def after(arrays):
    return lax.optimization_barrier(arrays)


def trade(array):
    return lax.all_to_all(array, "narrow", split_axis=0, concat_axis=0, tiled=True)


def body(
    prompt_states,
    prompt_lengths,
    feed_gain,
    gate_weight,
    up_weight,
    down_weight,
    final_gain,
    key_weight,
    value_weight,
    prompt_key_gain,
    latent_queries,
    latent_keys,
    latent_values,
    cross_queries,
    query_gain,
    key_gain,
    cross_query_gain,
):
    groups = latent_queries.shape[1] // key_weight.shape[1]
    per, width = prompt_states.shape
    extra = width // groups // HEAD * SLOT * 2
    heads = key_weight.shape[1] // HEAD
    each = 3 * HEAD
    arrays = (latent_queries, latent_keys, latent_values, cross_queries)
    gains = (query_gain, key_gain, cross_query_gain)

    def split(traded, base):
        pair = traded[:, base : base + 2 * HEAD]
        return traded[:, base + 2 * HEAD : base + 3 * HEAD], pair

    early = {"heads": [(0, 0, 0), (1, 0, each)], "crossed": []}
    late = {
        "heads": [(2, 0, extra)],
        "crossed": [(h, 0, extra + (3 + h) * HEAD) for h in range(heads)],
    }

    def plain(queries, pairs):
        return [(a, 0) for a in queries], [(a, 0) for a in pairs]

    (packed,) = pack(arrays, gains, groups, heads, early, [2 * each])
    traded = trade(packed)
    (final,) = pack(arrays, gains, groups, heads, late, [extra + 2 * each])
    pieces = feed(prompt_states, feed_gain, gate_weight, up_weight, down_weight, groups, extra)
    traded, pieces, final = after((traded, pieces, final))
    final = fold(trade(pieces), final)

    query0, pair0 = split(traded, 0)
    pair_x0 = send(pair0, OTHER_X)
    queries0 = [query0] + around(query0)
    pairs0 = [pair0, send(pair0, OTHER_CORE)]
    query1, pair1 = split(traded, each)
    pair_x1 = send(pair1, OTHER_X)
    queries1 = [query1] + around(query1)
    pairs1 = [pair1, send(pair1, OTHER_CORE)]
    pair_x0, queries0, final = after((pair_x0, queries0, final))
    final = trade(final)
    pairs0 += [pair_x0, send(pair_x0, OTHER_CORE)]
    part0 = attend(*plain(queries0, pairs0), from_ring)

    final, part0, queries1, pair_x1 = after((final, part0, queries1, pair_x1))
    pairs1 += [pair_x1, send(pair_x1, OTHER_CORE)]
    query2, pair2 = split(final, extra)
    pair_x2 = send(pair2, OTHER_X)
    queries2 = [query2] + around(query2)
    pairs2 = [pair2, send(pair2, OTHER_CORE)]
    result0 = trade_back(part0[0])
    part1 = attend(*plain(queries1, pairs1))

    tied = (part1, queries2, pair_x2, pairs2, result0, final)
    part1, queries2, pair_x2, pairs2, result0, folded = after(tied)
    pairs2 += [pair_x2, send(pair_x2, OTHER_CORE)]
    result1 = give_back(part1)
    prompt_pair = project(
        prompt_states,
        folded,
        final_gain,
        key_weight,
        value_weight,
        prompt_key_gain,
        extra,
        lax.axis_size("wide"),
    )
    prompt_pair = lax.all_to_all(prompt_pair, "wide", split_axis=0, concat_axis=0, tiled=True)
    others = attend(*plain(queries2[1:], pairs2))
    result1, others, prompt_pair = after((result1, others, prompt_pair))
    below, above, across = others
    result2 = [send(below, DOWN), send(above, UP), send(across, ACROSS)]
    result2 += attend(*plain(queries2[:1], pairs2))
    results = [[result0], result1, result2]
    cross_out = cross(prompt_lengths, final, extra + each, prompt_pair, per)
    results, cross_out = after((results, cross_out))
    self_out = merge(results)
    return (self_out, cross_out)


def solution(mesh):
    rows = P(("wide", "narrow"), None)
    return jax.shard_map(
        body,
        mesh=mesh,
        in_specs=(
            P("wide", None),
            P(),
            P(),
            P(None, "narrow"),
            P(None, "narrow"),
            P("narrow", None),
            P(),
            P(None, "narrow"),
            P(None, "narrow"),
            P("narrow"),
            rows,
            rows,
            rows,
            rows,
            P(),
            P(),
            P(),
        ),
        out_specs=(P("wide", "narrow"), P("wide", "narrow")),
        check_vma=False,
    )
```

time: 269 us -> 193 us (0.72); the launches traced: 264 us -> 192 us
  blocking collectives: 54.9 us -> 0 us
  local copies, waits for them, and re-layouts: 37.7 us -> 8.6 us
  Pallas kernels: 61.8 us -> 88.5 us
  waiting for transfers between devices: 14.4 us -> 34.8 us
  starting transfers between devices: 75 us -> 58.2 us
  matrix products: 13.5 us -> 0 us
  other arithmetic: 5.22 us -> 0 us
    all_gather x1 -> x0, blocking collectives: 30.1 us -> none  [body(): lax.all_gather(jnp.concatenate([prompt_keys, prompt_values], axis=1), 'wi...]
    pallas_call x6 -> x11, Pallas kernels: 61.8 us -> 88.5 us  [the longest x4 53.9 us: attend(): pl.pallas_call(lambda *refs: attend_kernel(views, nq, nkv, ring, *refs),...]
    all_to_all x7 -> x3, starting transfers between devices: 42.5 us -> 16.7 us  [trade(): lax.all_to_all(array, 'narrow', split_axis=0, concat_axis=0, tiled=True)]
    all_to_all x2 -> x0, blocking collectives: 24.8 us -> none  [trade(): lax.all_to_all(array, 'narrow', split_axis=0, concat_axis=0, tiled=True)]
    unnamed x79 -> x58, local copies, waits for them, and re-layouts: 31.6 us -> 6.87 us
    ppermute x27 -> x24, waiting for transfers between devices: 0.07 us -> 23.5 us  [send(): return lax.ppermute(array, 'wide', pairs)]
    dot_general x4 -> x0, matrix products: 13.5 us -> none  [the longest x1 6.44 us: body(): jnp.dot(hidden, down_weight, preferred_element_type=jnp.float32)]
    all_to_all x0 -> x2, starting transfers between devices: none -> 10.4 us  [the longest x1 5.42 us: body(): lax.all_to_all(prompt_pair, 'wide', split_axis=0, concat_axis=0, tiled=True)]
  transfers between devices with their start and end apart: 34 -> 29, of which waited for: 3 -> 8; matrix products, arithmetic and copies ran while one was open for 11% -> 0% of each run, Pallas kernels for 21% -> 42%
where the time goes in v2:
time: 193 us; the launch traced here: 192 us
  Pallas kernels  88.5 us (46%)
  starting transfers between devices  58.2 us (30%)
  waiting for transfers between devices  34.8 us (18%)
  local copies, waits for them, and re-layouts  8.6 us (4%)
    pallas_call x4, Pallas kernels, attend(): pl.pallas_call(lambda *refs: attend_kernel(views, nq, nkv, ring, *refs),...  53.9 us
    ppermute x24, starting transfers between devices, send(): return lax.ppermute(array, 'wide', pairs)  31 us
    ppermute x24, waiting for transfers between devices, send(): return lax.ppermute(array, 'wide', pairs)  23.5 us
    all_to_all x3, starting transfers between devices, trade(): lax.all_to_all(array, 'narrow', split_axis=0, concat_axis=0, tiled=True)  16.7 us
    all_to_all x3, waiting for transfers between devices, trade(): lax.all_to_all(array, 'narrow', split_axis=0, concat_axis=0, tiled=True)  11.3 us
    pallas_call x1, Pallas kernels, feed(): pl.pallas_call(feed_kernel, grid=(hidden // tile,), in_specs=[pl.BlockSpe...  9.21 us
    pallas_call x2, Pallas kernels, pack(): pl.pallas_call(lambda *refs: pack_kernel(heads, plan, *refs), in_specs=[w...  9.2 us
    unnamed x58, local copies, waits for them, and re-layouts  6.87 us
  transfers between devices with their start and end apart: 29, of which 8 were waited for; matrix products, arithmetic and copies ran while one was open for 0% of the time, Pallas kernels for 42%

profile of v2, /device:TPU:14, one launch (start us, length us, event | category | flops | bytes accessed | tf_op | source)
XLA Modules:
  0.0 191.7 jit_solution(15676932698361650441)
XLA Ops:
  0.6 4.3 %pack.2 = bf16[8,768,128]{2,1,0:T(8,128)(2,1)} custom-call(bf16[128,3072]{1,0:T(8,128)(2,1)} %refs_0_.4, bf16[128,3072]{1,0:T(8,128)(2,1)} %refs_1_.3, bf16[128,3072]{1,0:T(8,128)(2,1)} %refs_2_.3, f32[1,3072]{1,0:T(1,128)} %bitcast.5, f32[1,3072]{1,0:T(1,128)} %bitcast.7), custom_call_target="tpu_custom_call" | custom-call | flops 3145728 | bytes 6291456 | tf_op jit(solution)/shard_map/pack/pallas_call | solution.py:56
  4.9 5.8 %all-to-all-start = ((bf16[8,768,128]{2,1,0:T(8,128)(2,1)}), bf16[8,768,128]{2,1,0:T(8,128)(2,1)S(1)}, u32[]{:S(2)}, u32[]{:S(2)}) async-start(bf16[8,768,128]{2,1,0:T(8,128)(2,1)} %pack.2), calls=%async_computation | async-start | bytes 3145728 | tf_op jit(solution)/shard_map/all_to_all | solution.py:460
  10.8 4.9 %pack.3._ = bf16[8,1024,128]{2,1,0:T(8,128)(2,1)} custom-call(bf16[128,3072]{1,0:T(8,128)(2,1)} %refs_0_.4, bf16[128,3072]{1,0:T(8,128)(2,1)} %refs_1_.3, bf16[128,3072]{1,0:T(8,128)(2,1)} %refs_2_.3, f32[1,3072]{1,0:T(1,128)} %bitcast.6, f32[1,3072]{1,0:T(1,128)} %bitcast.8, bf16[128,3072]{1,0:T(8,128)(2,1)} %refs_5_.1, f32[1,3072]{1,0:T(1,128)} %bitcast.11), custom_call_target="tpu_custom_call" | custom-call | flops 3145728 | bytes 6291456 | tf_op jit(solution)/shard_map/pack/pallas_call | solution.py:56
  15.6 9.2 %feed.1 = bf16[8,256,128]{2,1,0:T(8,128)(2,1)} custom-call(bf16[24,4096]{1,0:T(8,128)(2,1)} %x_ref.3, f32[1,4096]{1,0:T(1,128)} %bitcast.9, bf16[4096,640]{1,0:T(8,128)(2,1)} %gate_ref.1, bf16[4096,640]{1,0:T(8,128)(2,1)} %up_ref.1, bf16[640,4096]{1,0:T(8,128)(2,1)} %down_ref.1), custom_call_target="tpu_custom_call" | custom-call | flops 503316480 | bytes 15728640 | tf_op jit(solution)/shard_map/feed/pallas_call | solution.py:109
  24.8 5.2 %all-to-all-done = bf16[8,768,128]{2,1,0:T(8,128)(2,1)S(1)} async-done(((bf16[8,768,128]{2,1,0:T(8,128)(2,1)}), bf16[8,768,128]{2,1,0:T(8,128)(2,1)S(1)}, u32[]{:S(2)}, u32[]{:S(2)}) %all-to-all-start) | async-done | bytes 1572896 | tf_op jit(solution)/shard_map/all_to_all | solution.py:460
  32.3 4.9 %all-to-all-start.1 = ((bf16[8,256,128]{2,1,0:T(8,128)(2,1)}), bf16[8,256,128]{2,1,0:T(8,128)(2,1)S(1)}, u32[]{:S(2)}, u32[]{:S(2)}) async-start(bf16[8,256,128]{2,1,0:T(8,128)(2,1)} %feed.1), calls=%async_computation.1 | async-start | bytes 1048576 | tf_op jit(solution)/shard_map/all_to_all | solution.py:460
  37.3 2.0 %collective-permute-start.1 = (bf16[8,128,128]{2,1,0:T(8,128)(2,1)S(1)}, bf16[8,128,128]{2,1,0:T(8,128)(2,1)S(1)}, u32[]{:S(2)}, u32[]{:S(2)}) collective-permute-start(bf16[8,128,128]{2,1,0:T(8,128)(2,1)S(1)} %get-tuple-element.60.refs_0_), channel_id=1, source_target_pairs={{0,16},{8,24},{16,32},{24,40},{32,48},{40,56},{48,0},{56,8},{64,80... | collective-permute-start | bytes 786440 | tf_op jit(solution)/shard_map/ppermute | solution.py:427
  39.3 2.2 %collective-permute-start.2 = (bf16[8,128,128]{2,1,0:T(8,128)(2,1)S(1)}, bf16[8,128,128]{2,1,0:T(8,128)(2,1)S(1)}, u32[]{:S(2)}, u32[]{:S(2)}) collective-permute-start(bf16[8,128,128]{2,1,0:T(8,128)(2,1)S(1)} %get-tuple-element.60.refs_0_), channel_id=1, source_target_pairs={{0,48},{8,56},{16,0},{24,8},{32,16},{40,24},{48,32},{56,40},{64,11... | collective-permute-start | bytes 786440 | tf_op jit(solution)/shard_map/ppermute | solution.py:427
  43.3 6.1 %all-to-all-done.1.parts_ref = bf16[8,256,128]{2,1,0:T(8,128)(2,1)S(1)} async-done(((bf16[8,256,128]{2,1,0:T(8,128)(2,1)}), bf16[8,256,128]{2,1,0:T(8,128)(2,1)S(1)}, u32[]{:S(2)}, u32[]{:S(2)}) %all-to-all-start.1) | async-done | bytes 524320 | tf_op jit(solution)/shard_map/all_to_all | solution.py:460
  50.2 2.0 %fold.1 = bf16[8,1024,128]{2,1,0:T(8,128)(2,1)} custom-call(bf16[8,256,128]{2,1,0:T(8,128)(2,1)} %copy-done.3, bf16[8,1024,128]{2,1,0:T(8,128)(2,1)} %pack.3._), custom_call_target="tpu_custom_call", output_to_operand_aliasing={{}: (1, {})} | custom-call | flops 262144 | bytes 1048576 | tf_op jit(solution)/shard_map/fold/pallas_call | solution.py:150
  54.4 6.0 %all-to-all-start.2 = ((bf16[8,1024,128]{2,1,0:T(8,128)(2,1)}), bf16[8,1024,128]{2,1,0:T(8,128)(2,1)S(1)}, u32[]{:S(2)}, u32[]{:S(2)}) async-start(bf16[8,1024,128]{2,1,0:T(8,128)(2,1)} %fold.1), calls=%async_computation.2 | async-start | bytes 4194304 | tf_op jit(solution)/shard_map/all_to_all | solution.py:460
  61.0 1.9 %collective-permute-start.6 = (bf16[8,128,128]{2,1,0:T(8,128)(2,1)S(1)}, bf16[8,128,128]{2,1,0:T(8,128)(2,1)S(1)}, u32[]{:S(2)}, u32[]{:S(2)}) collective-permute-start(bf16[8,128,128]{2,1,0:T(8,128)(2,1)S(1)} %get-tuple-element.65.refs_0_), channel_id=1, source_target_pairs={{0,16},{8,24},{16,32},{24,40},{32,48},{40,56},{48,0},{56,8},{64,80... | collective-permute-start | bytes 786440 | tf_op jit(solution)/shard_map/ppermute | solution.py:427
  62.9 2.1 %collective-permute-start.7 = (bf16[8,128,128]{2,1,0:T(8,128)(2,1)S(1)}, bf16[8,128,128]{2,1,0:T(8,128)(2,1)S(1)}, u32[]{:S(2)}, u32[]{:S(2)}) collective-permute-start(bf16[8,128,128]{2,1,0:T(8,128)(2,1)S(1)} %get-tuple-element.65.refs_0_), channel_id=1, source_target_pairs={{0,48},{8,56},{16,0},{24,8},{32,16},{40,24},{48,32},{56,40},{64,11... | collective-permute-start | bytes 786440 | tf_op jit(solution)/shard_map/ppermute | solution.py:427
  65.0 1.9 collective-permute-start.8
  66.9 2.1 %collective-permute-start.9 = (bf16[8,256,128]{2,1,0:T(8,128)(2,1)}, bf16[8,256,128]{2,1,0:T(8,128)(2,1)}, u32[]{:S(2)}, u32[]{:S(2)}) collective-permute-start(bf16[8,256,128]{2,1,0:T(8,128)(2,1)} %get-tuple-element.110.refs_4_), channel_id=1, source_target_pairs={{0,64},{8,72},{16,80},{24,88},{32,96},{40,104},{48,112},{56,120},{... | collective-permute-start | bytes 1572872 | tf_op jit(solution)/shard_map/ppermute | solution.py:427
  69.8 17.3 %attend.4 = bf16[4,144,1024]{2,1,0:T(8,128)(2,1)} custom-call(bf16[8,128,128]{2,1,0:T(8,128)(2,1)} %copy-done.14, bf16[8,128,128]{2,1,0:T(8,128)(2,1)} %copy-done.24, bf16[8,128,128]{2,1,0:T(8,128)(2,1)} %copy-done.26, bf16[8,128,128]{2,1,0:T(8,128)(2,1)} %copy-done.27, bf16[8,256,128]{2,1,0:T(8,128)(2,1)} %copy-done.5, bf16[8,256,128]{2,1,0:T(8,128)(2,1)} %copy-done.17, ...), custom_call_target="tpu_custom_call" | custom-call | flops 8589934592 | bytes 6291456 | tf_op jit(solution)/shard_map/attend/pallas_call | solution.py:300
  88.7 7.7 %collective-permute-done.9.refs_6_ = bf16[8,256,128]{2,1,0:T(8,128)(2,1)} collective-permute-done((bf16[8,256,128]{2,1,0:T(8,128)(2,1)}, bf16[8,256,128]{2,1,0:T(8,128)(2,1)}, u32[]{:S(2)}, u32[]{:S(2)}) %collective-permute-start.9) | collective-permute-done | bytes 524320 | tf_op jit(solution)/shard_map/ppermute | solution.py:427
  96.4 5.0 %all-to-all-start.3 = ((bf16[4,144,1024]{2,1,0:T(8,128)(2,1)}), bf16[4,144,1024]{2,1,0:T(8,128)(2,1)S(1)}, u32[]{:S(2)}, u32[]{:S(2)}) async-start(bf16[4,144,1024]{2,1,0:T(8,128)(2,1)} %attend.4), calls=%async_computation.3 | async-start | bytes 2359296 | tf_op jit(solution)/shard_map/all_to_all | solution.py:440
  103.0 2.1 %collective-permute-start.12 = (bf16[8,128,128]{2,1,0:T(8,128)(2,1)S(1)}, bf16[8,128,128]{2,1,0:T(8,128)(2,1)S(1)}, u32[]{:S(2)}, u32[]{:S(2)}) collective-permute-start(bf16[8,128,128]{2,1,0:T(8,128)(2,1)S(1)} %slice.22.refs_0_), channel_id=1, source_target_pairs={{0,16},{8,24},{16,32},{24,40},{32,48},{40,56},{48,0},{56,8},{64,80... | collective-permute-start | bytes 786440 | tf_op jit(solution)/shard_map/ppermute | solution.py:427
  106.4 2.2 %collective-permute-start.14 = (bf16[8,128,128]{2,1,0:T(8,128)(2,1)S(1)}, bf16[8,128,128]{2,1,0:T(8,128)(2,1)S(1)}, u32[]{:S(2)}, u32[]{:S(2)}) collective-permute-start(bf16[8,128,128]{2,1,0:T(8,128)(2,1)S(1)} %slice.22.refs_0_), channel_id=1, source_target_pairs={{0,32},{8,40},{16,48},{24,56},{32,0},{40,8},{48,16},{56,24},{64,96... | collective-permute-start | bytes 786440 | tf_op jit(solution)/shard_map/ppermute | solution.py:427
  108.6 17.2 %attend.5 = (bf16[144,1024]{1,0:T(8,128)(2,1)}, bf16[144,1024]{1,0:T(8,128)(2,1)}, bf16[144,1024]{1,0:T(8,128)(2,1)}, bf16[144,1024]{1,0:T(8,128)(2,1)}) custom-call(bf16[8,128,128]{2,1,0:T(8,128)(2,1)} %copy-done.13, bf16[8,128,128]{2,1,0:T(8,128)(2,1)} %copy-done.20, bf16[8,128,128]{2,1,0:T(8,128)(2,1)} %copy-done.21, bf16[8,128,128]{2,1,0:T(8,128)(2,1)} %copy-done.22, ...), custom_call_target="tpu_custom_call" | custom-call | flops 8589934592 | bytes 6291456 | tf_op jit(solution)/shard_map/attend/pallas_call | solution.py:300
  125.9 3.9 %collective-permute-done.14.refs_2_ = bf16[8,128,128]{2,1,0:T(8,128)(2,1)S(1)} collective-permute-done((bf16[8,128,128]{2,1,0:T(8,128)(2,1)S(1)}, bf16[8,128,128]{2,1,0:T(8,128)(2,1)S(1)}, u32[]{:S(2)}, u32[]{:S(2)}) %collective-permute-start.14) | collective-permute-done | bytes 262176 | tf_op jit(solution)/shard_map/ppermute | solution.py:427
  132.4 5.3 %project.1 = bf16[16,192,128]{2,1,0:T(8,128)(2,1)} custom-call(bf16[24,4096]{1,0:T(8,128)(2,1)} %x_ref.3, bf16[8,1024,128]{2,1,0:T(8,128)(2,1)} %copy-done, f32[1,4096]{1,0:T(1,128)} %bitcast.10, bf16[4096,384]{1,0:T(8,128)(2,1)} %key_ref.1, bf16[4096,384]{1,0:T(8,128)(2,1)} %value_ref.1, f32[1,384]{1,0:T(1,128)} %broadcast_in_dim.25.key_gain_ref), custom_call_target="tpu_custom_call" | custom-call | flops 201326592 | bytes 6291456 | tf_op jit(solution)/shard_map/project/pallas_call | solution.py:200
  137.7 5.4 %all-to-all-start.4 = ((bf16[16,192,128]{2,1,0:T(8,128)(2,1)}), bf16[16,192,128]{2,1,0:T(8,128)(2,1)S(1)}, u32[]{:S(2)}, u32[]{:S(2)}) async-start(bf16[16,192,128]{2,1,0:T(8,128)(2,1)} %project.1), calls=%async_computation.4 | async-start | bytes 1572864 | tf_op jit(solution)/shard_map/all_to_all | solution.py:546
  143.2 2.7 %collective-permute-start.17 = (bf16[144,1024]{1,0:T(8,128)(2,1)}, bf16[144,1024]{1,0:T(8,128)(2,1)S(1)}, u32[]{:S(2)}, u32[]{:S(2)}) collective-permute-start(bf16[144,1024]{1,0:T(8,128)(2,1)} %get-tuple-element.78), channel_id=1, source_target_pairs={{0,48},{8,56},{16,0},{24,8},{32,16},{40,24},{48,32},{56,40},{64,11... | collective-permute-start | bytes 884744 | tf_op jit(solution)/shard_map/ppermute | solution.py:427
  145.9 2.3 %collective-permute-start.19 = (bf16[144,1024]{1,0:T(8,128)(2,1)S(1)}, bf16[144,1024]{1,0:T(8,128)(2,1)S(1)}, u32[]{:S(2)}, u32[]{:S(2)}) collective-permute-start(bf16[144,1024]{1,0:T(8,128)(2,1)S(1)} %copy-done.19), channel_id=1, source_target_pairs={{0,32},{8,40},{16,48},{24,56},{32,0},{40,8},{48,16},{56,24},{64,96... | collective-permute-start | bytes 884744 | tf_op jit(solution)/shard_map/ppermute | solution.py:427
  148.2 13.5 %attend.6 = (bf16[144,1024]{1,0:T(8,128)(2,1)}, bf16[144,1024]{1,0:T(8,128)(2,1)}, bf16[144,1024]{1,0:T(8,128)(2,1)}) custom-call(bf16[8,128,128]{2,1,0:T(8,128)(2,1)} %copy-done.23, bf16[8,128,128]{2,1,0:T(8,128)(2,1)} %copy-done.25, bf16[8,128,128]{2,1,0:T(8,128)(2,1)} %copy-done.28, bf16[8,256,128]{2,1,0:T(8,128)(2,1)} %copy-done.4, ...), custom_call_target="tpu_custom_call" | custom-call | flops 6442450944 | bytes 6291456 | tf_op jit(solution)/shard_map/attend/pallas_call | solution.py:300
  161.8 6.7 %collective-permute-done.19.refs_4_ = bf16[144,1024]{1,0:T(8,128)(2,1)S(1)} collective-permute-done((bf16[144,1024]{1,0:T(8,128)(2,1)S(1)}, bf16[144,1024]{1,0:T(8,128)(2,1)S(1)}, u32[]{:S(2)}, u32[]{:S(2)}) %collective-permute-start.19) | collective-permute-done | bytes 294944 | tf_op jit(solution)/shard_map/ppermute | solution.py:427
  171.8 6.0 %attend.7.refs_8_ = bf16[144,1024]{1,0:T(8,128)(2,1)} custom-call(bf16[8,128,128]{2,1,0:T(8,128)(2,1)} %copy-done.12, bf16[8,256,128]{2,1,0:T(8,128)(2,1)} %copy-done.4, bf16[8,256,128]{2,1,0:T(8,128)(2,1)} %collective-permute-done.16.refs_4_.refs_2_, bf16[8,256,128]{2,1,0:T(8,128)(2,1)} %copy-done.16, ...), custom_call_target="tpu_custom_call" | custom-call | flops 2147483648 | bytes 6291456 | tf_op jit(solution)/shard_map/attend/pallas_call | solution.py:300
  177.9 4.7 %cross.1 = bf16[1024,384]{1,0:T(8,128)(2,1)} custom-call(s32[1]{0:T(128)S(6)} %copy.21.refs_0_, bf16[8,1024,128]{2,1,0:T(8,128)(2,1)} %copy-done, bf16[16,192,128]{2,1,0:T(8,128)(2,1)} %copy-done.2), custom_call_target="tpu_custom_call" | custom-call | flops 805306368 | bytes 3145728 | tf_op jit(solution)/shard_map/cross/pallas_call | solution.py:388
  182.6 3.5 %collective-permute-done.22.refs_6_ = bf16[144,1024]{1,0:T(8,128)(2,1)S(1)} collective-permute-done((bf16[144,1024]{1,0:T(8,128)(2,1)}, bf16[144,1024]{1,0:T(8,128)(2,1)S(1)}, u32[]{:S(2)}, u32[]{:S(2)}) %collective-permute-start.22) | collective-permute-done | bytes 294944 | tf_op jit(solution)/shard_map/ppermute | solution.py:427
  187.5 4.2 %merge.1 = bf16[1024,384]{1,0:T(8,128)(2,1)} custom-call(bf16[4,144,1024]{2,1,0:T(8,128)(2,1)} %copy-done.1, bf16[144,1024]{1,0:T(8,128)(2,1)} %get-tuple-element.101.refs_1_, bf16[144,1024]{1,0:T(8,128)(2,1)} %copy-done.6, bf16[144,1024]{1,0:T(8,128)(2,1)} %copy-done.7, bf16[144,1024]{1,0:T(8,128)(2,1)} %copy-done.8, bf16[144,1024]{1,0:T(8,128)(2,1)} %copy-done.9, ...), custom_call_target="tpu_custom_call" | custom-call | flops 3145728 | bytes 4194304 | tf_op jit(solution)/shard_map/merge/pallas_call | solution.py:345
  (100 shorter events, 19.8 us)
Async XLA Ops:
  4.9 25.1 %all-to-all-start = ((bf16[8,768,128]{2,1,0:T(8,128)(2,1)}), bf16[8,768,128]{2,1,0:T(8,128)(2,1)S(1)}, u32[]{:S(2)}, u32[]{:S(2)}) async-start(bf16[8,768,128]{2,1,0:T(8,128)(2,1)} %pack.2), calls=%async_computation | async-start | bytes 3145728 | tf_op jit(solution)/shard_map/all_to_all | solution.py:460
  30.9 29.6 %copy-start.5 = (bf16[8,256,128]{2,1,0:T(8,128)(2,1)}, bf16[8,256,128]{2,1,0:T(8,128)(2,1)S(1)}, u32[]{:S(2)}) copy-start(bf16[8,256,128]{2,1,0:T(8,128)(2,1)S(1)} %get-tuple-element.111.refs_4_) | copy-start | bytes 1572868
  30.9 22.8 %collective-permute-start = (bf16[8,256,128]{2,1,0:T(8,128)(2,1)S(1)}, bf16[8,256,128]{2,1,0:T(8,128)(2,1)}, u32[]{:S(2)}, u32[]{:S(2)}) collective-permute-start(bf16[8,256,128]{2,1,0:T(8,128)(2,1)S(1)} %get-tuple-element.111.refs_4_), channel_id=1, source_target_pairs={{0,64},{8,72},{16,80},{24,88},{32,96},{40,104},{48,112},{56,120},{... | collective-permute-start | bytes 1572872 | tf_op jit(solution)/shard_map/ppermute | solution.py:427
  32.3 17.1 %all-to-all-start.1 = ((bf16[8,256,128]{2,1,0:T(8,128)(2,1)}), bf16[8,256,128]{2,1,0:T(8,128)(2,1)S(1)}, u32[]{:S(2)}, u32[]{:S(2)}) async-start(bf16[8,256,128]{2,1,0:T(8,128)(2,1)} %feed.1), calls=%async_computation.1 | async-start | bytes 1048576 | tf_op jit(solution)/shard_map/all_to_all | solution.py:460
  37.3 31.7 %copy-start.14 = (bf16[8,128,128]{2,1,0:T(8,128)(2,1)}, bf16[8,128,128]{2,1,0:T(8,128)(2,1)S(1)}, u32[]{:S(2)}) copy-start(bf16[8,128,128]{2,1,0:T(8,128)(2,1)S(1)} %get-tuple-element.60.refs_0_) | copy-start | bytes 786436
  37.3 49.8 %copy-start.13 = (bf16[8,128,128]{2,1,0:T(8,128)(2,1)}, bf16[8,128,128]{2,1,0:T(8,128)(2,1)S(1)}, u32[]{:S(2)}) copy-start(bf16[8,128,128]{2,1,0:T(8,128)(2,1)S(1)} %get-tuple-element.65.refs_0_) | copy-start | bytes 786436
  37.3 14.9 %collective-permute-start.1 = (bf16[8,128,128]{2,1,0:T(8,128)(2,1)S(1)}, bf16[8,128,128]{2,1,0:T(8,128)(2,1)S(1)}, u32[]{:S(2)}, u32[]{:S(2)}) collective-permute-start(bf16[8,128,128]{2,1,0:T(8,128)(2,1)S(1)} %get-tuple-element.60.refs_0_), channel_id=1, source_target_pairs={{0,16},{8,24},{16,32},{24,40},{32,48},{40,56},{48,0},{56,8},{64,80... | collective-permute-start | bytes 786440 | tf_op jit(solution)/shard_map/ppermute | solution.py:427
  39.3 12.9 %collective-permute-start.2 = (bf16[8,128,128]{2,1,0:T(8,128)(2,1)S(1)}, bf16[8,128,128]{2,1,0:T(8,128)(2,1)S(1)}, u32[]{:S(2)}, u32[]{:S(2)}) collective-permute-start(bf16[8,128,128]{2,1,0:T(8,128)(2,1)S(1)} %get-tuple-element.60.refs_0_), channel_id=1, source_target_pairs={{0,48},{8,56},{16,0},{24,8},{32,16},{40,24},{48,32},{56,40},{64,11... | collective-permute-start | bytes 786440 | tf_op jit(solution)/shard_map/ppermute | solution.py:427
  41.5 12.2 %collective-permute-start.3 = (bf16[8,128,128]{2,1,0:T(8,128)(2,1)S(1)}, bf16[8,128,128]{2,1,0:T(8,128)(2,1)S(1)}, u32[]{:S(2)}, u32[]{:S(2)}) collective-permute-start(bf16[8,128,128]{2,1,0:T(8,128)(2,1)S(1)} %get-tuple-element.60.refs_0_), channel_id=1, source_target_pairs={{0,32},{8,40},{16,48},{24,56},{32,0},{40,8},{48,16},{56,24},{64,96... | collective-permute-start | bytes 786440 | tf_op jit(solution)/shard_map/ppermute | solution.py:427
  54.4 41.9 %all-to-all-start.2 = ((bf16[8,1024,128]{2,1,0:T(8,128)(2,1)}), bf16[8,1024,128]{2,1,0:T(8,128)(2,1)S(1)}, u32[]{:S(2)}, u32[]{:S(2)}) async-start(bf16[8,1024,128]{2,1,0:T(8,128)(2,1)} %fold.1), calls=%async_computation.2 | async-start | bytes 4194304 | tf_op jit(solution)/shard_map/all_to_all | solution.py:460
  60.4 6.4 %collective-permute-start.4 = (bf16[8,256,128]{2,1,0:T(8,128)(2,1)S(1)}, bf16[8,256,128]{2,1,0:T(8,128)(2,1)S(1)}, u32[]{:S(2)}, u32[]{:S(2)}) collective-permute-start(bf16[8,256,128]{2,1,0:T(8,128)(2,1)S(1)} %get-tuple-element.111.refs_4_), channel_id=1, source_target_pairs={{0,8},{8,0},{16,24},{24,16},{32,40},{40,32},{48,56},{56,48},{64,72... | collective-permute-start | bytes 1572872 | tf_op jit(solution)/shard_map/ppermute | solution.py:427
  60.5 8.5 %collective-permute-start.5 = (bf16[8,256,128]{2,1,0:T(8,128)(2,1)}, bf16[8,256,128]{2,1,0:T(8,128)(2,1)S(1)}, u32[]{:S(2)}, u32[]{:S(2)}) collective-permute-start(bf16[8,256,128]{2,1,0:T(8,128)(2,1)} %collective-permute-done.refs_6_), channel_id=1, source_target_pairs={{0,8},{8,0},{16,24},{24,16},{32,40},{40,32},{48,56},{56,48},{64,72... | collective-permute-start | bytes 1572872 | tf_op jit(solution)/shard_map/ppermute | solution.py:427
  61.0 26.2 %collective-permute-start.6 = (bf16[8,128,128]{2,1,0:T(8,128)(2,1)S(1)}, bf16[8,128,128]{2,1,0:T(8,128)(2,1)S(1)}, u32[]{:S(2)}, u32[]{:S(2)}) collective-permute-start(bf16[8,128,128]{2,1,0:T(8,128)(2,1)S(1)} %get-tuple-element.65.refs_0_), channel_id=1, source_target_pairs={{0,16},{8,24},{16,32},{24,40},{32,48},{40,56},{48,0},{56,8},{64,80... | collective-permute-start | bytes 786440 | tf_op jit(solution)/shard_map/ppermute | solution.py:427
  62.9 24.3 %collective-permute-start.7 = (bf16[8,128,128]{2,1,0:T(8,128)(2,1)S(1)}, bf16[8,128,128]{2,1,0:T(8,128)(2,1)S(1)}, u32[]{:S(2)}, u32[]{:S(2)}) collective-permute-start(bf16[8,128,128]{2,1,0:T(8,128)(2,1)S(1)} %get-tuple-element.65.refs_0_), channel_id=1, source_target_pairs={{0,48},{8,56},{16,0},{24,8},{32,16},{40,24},{48,32},{56,40},{64,11... | collective-permute-start | bytes 786440 | tf_op jit(solution)/shard_map/ppermute | solution.py:427
  65.0 22.2 %collective-permute-start.8 = (bf16[8,128,128]{2,1,0:T(8,128)(2,1)S(1)}, bf16[8,128,128]{2,1,0:T(8,128)(2,1)S(1)}, u32[]{:S(2)}, u32[]{:S(2)}) collective-permute-start(bf16[8,128,128]{2,1,0:T(8,128)(2,1)S(1)} %get-tuple-element.65.refs_0_), channel_id=1, source_target_pairs={{0,32},{8,40},{16,48},{24,56},{32,0},{40,8},{48,16},{56,24},{64,96... | collective-permute-start | bytes 786440 | tf_op jit(solution)/shard_map/ppermute | solution.py:427
  66.9 29.5 %collective-permute-start.9 = (bf16[8,256,128]{2,1,0:T(8,128)(2,1)}, bf16[8,256,128]{2,1,0:T(8,128)(2,1)}, u32[]{:S(2)}, u32[]{:S(2)}) collective-permute-start(bf16[8,256,128]{2,1,0:T(8,128)(2,1)} %get-tuple-element.110.refs_4_), channel_id=1, source_target_pairs={{0,64},{8,72},{16,80},{24,88},{32,96},{40,104},{48,112},{56,120},{... | collective-permute-start | bytes 1572872 | tf_op jit(solution)/shard_map/ppermute | solution.py:427
  69.0 36.1 %collective-permute-start.10 = (bf16[8,256,128]{2,1,0:T(8,128)(2,1)}, bf16[8,256,128]{2,1,0:T(8,128)(2,1)}, u32[]{:S(2)}, u32[]{:S(2)}) collective-permute-start(bf16[8,256,128]{2,1,0:T(8,128)(2,1)} %get-tuple-element.110.refs_4_), channel_id=1, source_target_pairs={{0,8},{8,0},{16,24},{24,16},{32,40},{40,32},{48,56},{56,48},{64,72... | collective-permute-start | bytes 1572872 | tf_op jit(solution)/shard_map/ppermute | solution.py:427
  96.4 10.0 %collective-permute-start.11 = (bf16[8,256,128]{2,1,0:T(8,128)(2,1)}, bf16[8,256,128]{2,1,0:T(8,128)(2,1)}, u32[]{:S(2)}, u32[]{:S(2)}) collective-permute-start(bf16[8,256,128]{2,1,0:T(8,128)(2,1)} %collective-permute-done.9.refs_6_), channel_id=1, source_target_pairs={{0,8},{8,0},{16,24},{24,16},{32,40},{40,32},{48,56},{56,48},{64,72... | collective-permute-start | bytes 1572872 | tf_op jit(solution)/shard_map/ppermute | solution.py:427
  96.4 35.0 %all-to-all-start.3 = ((bf16[4,144,1024]{2,1,0:T(8,128)(2,1)}), bf16[4,144,1024]{2,1,0:T(8,128)(2,1)S(1)}, u32[]{:S(2)}, u32[]{:S(2)}) async-start(bf16[4,144,1024]{2,1,0:T(8,128)(2,1)} %attend.4), calls=%async_computation.3 | async-start | bytes 2359296 | tf_op jit(solution)/shard_map/all_to_all | solution.py:440
  101.5 28.4 %collective-permute-start.15 = (bf16[8,256,128]{2,1,0:T(8,128)(2,1)S(1)}, bf16[8,256,128]{2,1,0:T(8,128)(2,1)S(1)}, u32[]{:S(2)}, u32[]{:S(2)}) collective-permute-start(bf16[8,256,128]{2,1,0:T(8,128)(2,1)S(1)} %slice.23.refs_3_.refs_1_), channel_id=1, source_target_pairs={{0,64},{8,72},{16,80},{24,88},{32,96},{40,104},{48,112},{56,120},{... | collective-permute-start | bytes 1572872 | tf_op jit(solution)/shard_map/ppermute | solution.py:427
  102.9 28.5 %collective-permute-start.16 = (bf16[8,256,128]{2,1,0:T(8,128)(2,1)S(1)}, bf16[8,256,128]{2,1,0:T(8,128)(2,1)}, u32[]{:S(2)}, u32[]{:S(2)}) collective-permute-start(bf16[8,256,128]{2,1,0:T(8,128)(2,1)S(1)} %slice.23.refs_3_.refs_1_), channel_id=1, source_target_pairs={{0,8},{8,0},{16,24},{24,16},{32,40},{40,32},{48,56},{56,48},{64,72... | collective-permute-start | bytes 1572872 | tf_op jit(solution)/shard_map/ppermute | solution.py:427
  103.0 22.9 %collective-permute-start.12 = (bf16[8,128,128]{2,1,0:T(8,128)(2,1)S(1)}, bf16[8,128,128]{2,1,0:T(8,128)(2,1)S(1)}, u32[]{:S(2)}, u32[]{:S(2)}) collective-permute-start(bf16[8,128,128]{2,1,0:T(8,128)(2,1)S(1)} %slice.22.refs_0_), channel_id=1, source_target_pairs={{0,16},{8,24},{16,32},{24,40},{32,48},{40,56},{48,0},{56,8},{64,80... | collective-permute-start | bytes 786440 | tf_op jit(solution)/shard_map/ppermute | solution.py:427
  105.1 20.8 %collective-permute-start.13 = (bf16[8,128,128]{2,1,0:T(8,128)(2,1)S(1)}, bf16[8,128,128]{2,1,0:T(8,128)(2,1)S(1)}, u32[]{:S(2)}, u32[]{:S(2)}) collective-permute-start(bf16[8,128,128]{2,1,0:T(8,128)(2,1)S(1)} %slice.22.refs_0_), channel_id=1, source_target_pairs={{0,48},{8,56},{16,0},{24,8},{32,16},{40,24},{48,32},{56,40},{64,11... | collective-permute-start | bytes 786440 | tf_op jit(solution)/shard_map/ppermute | solution.py:427
  106.4 23.5 %collective-permute-start.14 = (bf16[8,128,128]{2,1,0:T(8,128)(2,1)S(1)}, bf16[8,128,128]{2,1,0:T(8,128)(2,1)S(1)}, u32[]{:S(2)}, u32[]{:S(2)}) collective-permute-start(bf16[8,128,128]{2,1,0:T(8,128)(2,1)S(1)} %slice.22.refs_0_), channel_id=1, source_target_pairs={{0,32},{8,40},{16,48},{24,56},{32,0},{40,8},{48,16},{56,24},{64,96... | collective-permute-start | bytes 786440 | tf_op jit(solution)/shard_map/ppermute | solution.py:427
  131.4 16.8 %collective-permute-start.20 = (bf16[8,256,128]{2,1,0:T(8,128)(2,1)}, bf16[8,256,128]{2,1,0:T(8,128)(2,1)}, u32[]{:S(2)}, u32[]{:S(2)}) collective-permute-start(bf16[8,256,128]{2,1,0:T(8,128)(2,1)} %copy-done.16), channel_id=1, source_target_pairs={{0,8},{8,0},{16,24},{24,16},{32,40},{40,32},{48,56},{56,48},{64,72... | collective-permute-start | bytes 1572872 | tf_op jit(solution)/shard_map/ppermute | solution.py:427
  137.7 30.7 %all-to-all-start.4 = ((bf16[16,192,128]{2,1,0:T(8,128)(2,1)}), bf16[16,192,128]{2,1,0:T(8,128)(2,1)S(1)}, u32[]{:S(2)}, u32[]{:S(2)}) async-start(bf16[16,192,128]{2,1,0:T(8,128)(2,1)} %project.1), calls=%async_computation.4 | async-start | bytes 1572864 | tf_op jit(solution)/shard_map/all_to_all | solution.py:546
  143.2 18.5 %collective-permute-start.17 = (bf16[144,1024]{1,0:T(8,128)(2,1)}, bf16[144,1024]{1,0:T(8,128)(2,1)S(1)}, u32[]{:S(2)}, u32[]{:S(2)}) collective-permute-start(bf16[144,1024]{1,0:T(8,128)(2,1)} %get-tuple-element.78), channel_id=1, source_target_pairs={{0,48},{8,56},{16,0},{24,8},{32,16},{40,24},{48,32},{56,40},{64,11... | collective-permute-start | bytes 884744 | tf_op jit(solution)/shard_map/ppermute | solution.py:427
  145.8 15.9 %collective-permute-start.18 = (bf16[144,1024]{1,0:T(8,128)(2,1)}, bf16[144,1024]{1,0:T(8,128)(2,1)S(1)}, u32[]{:S(2)}, u32[]{:S(2)}) collective-permute-start(bf16[144,1024]{1,0:T(8,128)(2,1)} %get-tuple-element.79), channel_id=1, source_target_pairs={{0,16},{8,24},{16,32},{24,40},{32,48},{40,56},{48,0},{56,8},{64,80... | collective-permute-start | bytes 884744 | tf_op jit(solution)/shard_map/ppermute | solution.py:427
  145.9 22.6 %collective-permute-start.19 = (bf16[144,1024]{1,0:T(8,128)(2,1)S(1)}, bf16[144,1024]{1,0:T(8,128)(2,1)S(1)}, u32[]{:S(2)}, u32[]{:S(2)}) collective-permute-start(bf16[144,1024]{1,0:T(8,128)(2,1)S(1)} %copy-done.19), channel_id=1, source_target_pairs={{0,32},{8,40},{16,48},{24,56},{32,0},{40,8},{48,16},{56,24},{64,96... | collective-permute-start | bytes 884744 | tf_op jit(solution)/shard_map/ppermute | solution.py:427
  168.5 14.1 %collective-permute-start.21 = (bf16[144,1024]{1,0:T(8,128)(2,1)}, bf16[144,1024]{1,0:T(8,128)(2,1)S(1)}, u32[]{:S(2)}, u32[]{:S(2)}) collective-permute-start(bf16[144,1024]{1,0:T(8,128)(2,1)} %get-tuple-element.95), channel_id=1, source_target_pairs={{0,48},{8,56},{16,0},{24,8},{32,16},{40,24},{48,32},{56,40},{64,11... | collective-permute-start | bytes 884744 | tf_op jit(solution)/shard_map/ppermute | solution.py:427
  169.6 16.4 %collective-permute-start.22 = (bf16[144,1024]{1,0:T(8,128)(2,1)}, bf16[144,1024]{1,0:T(8,128)(2,1)S(1)}, u32[]{:S(2)}, u32[]{:S(2)}) collective-permute-start(bf16[144,1024]{1,0:T(8,128)(2,1)} %get-tuple-element.96), channel_id=1, source_target_pairs={{0,16},{8,24},{16,32},{24,40},{32,48},{40,56},{48,0},{56,8},{64,80... | collective-permute-start | bytes 884744 | tf_op jit(solution)/shard_map/ppermute | solution.py:427
  170.5 15.5 %collective-permute-start.23 = (bf16[144,1024]{1,0:T(8,128)(2,1)}, bf16[144,1024]{1,0:T(8,128)(2,1)S(1)}, u32[]{:S(2)}, u32[]{:S(2)}) collective-permute-start(bf16[144,1024]{1,0:T(8,128)(2,1)} %get-tuple-element.97), channel_id=1, source_target_pairs={{0,32},{8,40},{16,48},{24,56},{32,0},{40,8},{48,16},{56,24},{64,96... | collective-permute-start | bytes 884744 | tf_op jit(solution)/shard_map/ppermute | solution.py:427
  (26 other events, 201.2 us)

commit v3 on v2

--- a/solution.py
+++ b/solution.py
@@ -31,14 +31,14 @@
     outs = rest[2:] if plan["crossed"] else rest
 
     def group(n, _):
-        for h, out, base in plan["heads"]:
+        for h, out, pair, query in plan["heads"]:
             at = pl.ds(pl.multiple_of((n * heads + h) * HEAD, HEAD), HEAD)
             ref = outs[out]
-            ref[n, base : base + HEAD, :] = normed(k_ref, kg_ref, at, 1.0)
-            ref[n, base + HEAD : base + 2 * HEAD, :] = (
+            ref[n, pair : pair + HEAD, :] = normed(k_ref, kg_ref, at, 1.0)
+            ref[n, pair + HEAD : pair + 2 * HEAD, :] = (
                 v_ref[:, at].astype(jnp.float32).T.astype(jnp.bfloat16)
             )
-            ref[n, base + 2 * HEAD : base + 3 * HEAD, :] = normed(q_ref, qg_ref, at, SCALE)
+            ref[n, query : query + HEAD, :] = normed(q_ref, qg_ref, at, SCALE)
         for h, out, base in plan["crossed"]:
             at = pl.ds(pl.multiple_of((n * heads + h) * HEAD, HEAD), HEAD)
             outs[out][n, base : base + HEAD, :] = normed(rest[0], rest[1], at, SCALE)
@@ -319,7 +319,7 @@
 
 def merge_kernel(sizes, *refs):
     out_ref = refs[-1]
-    refs = list(refs[:-1])
+    refs = list(refs[: sum(sizes)])
     for h, size in enumerate(sizes):
         group, refs = refs[:size], refs[size:]
         if size == 1:
@@ -330,7 +330,7 @@
         out_ref[:, h * HEAD : (h + 1) * HEAD] = (weighted / total).T.astype(jnp.bfloat16)
 
 
-def merge(results):
+def merge(results, width, column, into=None):
     heads = len(results)
     arrays = [array for group in results for array in group]
     sizes = [len(group) for group in results]
@@ -342,15 +342,21 @@
             specs.append(pl.BlockSpec((array.shape[0], step), lambda i: (0, i)))
         else:
             specs.append(pl.BlockSpec(array.shape[:2] + (step,), lambda i: (0, 0, i)))
+    aliases = {}
+    if into is not None:
+        aliases = {len(arrays): 0}
+        arrays.append(into)
+        specs.append(pl.BlockSpec(memory_space=pl.ANY))
     return pl.pallas_call(
         lambda *refs: merge_kernel(sizes, *refs),
         grid=(count // step,),
         in_specs=specs,
-        out_specs=pl.BlockSpec((step, heads * HEAD), lambda i: (i, 0)),
-        out_shape=jax.ShapeDtypeStruct((count, heads * HEAD), jnp.bfloat16),
-        compiler_params=vmem(56),
-        cost_estimate=pl.CostEstimate(
-            flops=count * heads * HEAD * 8, bytes_accessed=4 * 2**20, transcendentals=0
+        out_specs=pl.BlockSpec((step, heads * HEAD), lambda i: (i, column)),
+        out_shape=jax.ShapeDtypeStruct((count, width), jnp.bfloat16),
+        input_output_aliases=aliases,
+        compiler_params=vmem(56),
+        cost_estimate=pl.CostEstimate(
+            flops=count * heads * HEAD * 8, bytes_accessed=heads * 2**21, transcendentals=0
         ),
         name="merge",
     )(*arrays)
@@ -484,50 +490,47 @@
     extra = width // groups // HEAD * SLOT * 2
     heads = key_weight.shape[1] // HEAD
     each = 3 * HEAD
+    last = heads - 1
     arrays = (latent_queries, latent_keys, latent_values, cross_queries)
     gains = (query_gain, key_gain, cross_query_gain)
 
-    def split(traded, base):
-        pair = traded[:, base : base + 2 * HEAD]
-        return traded[:, base + 2 * HEAD : base + 3 * HEAD], pair
-
-    early = {"heads": [(0, 0, 0), (1, 0, each)], "crossed": []}
+    def split(traded, base, count):
+        middle, end = base + 2 * count * HEAD, base + 3 * count * HEAD
+        return traded[:, middle:end], traded[:, base:middle]
+
+    early = {
+        "heads": [(0, 0, 0, 4 * HEAD), (1, 0, 2 * HEAD, 5 * HEAD)],
+        "crossed": [],
+    }
     late = {
-        "heads": [(2, 0, extra)],
+        "heads": [(2, 0, extra, extra + 2 * HEAD)],
         "crossed": [(h, 0, extra + (3 + h) * HEAD) for h in range(heads)],
     }
 
-    def plain(queries, pairs):
-        return [(a, 0) for a in queries], [(a, 0) for a in pairs]
+    def views(queries, pairs, h=0):
+        return [(a, h * HEAD) for a in queries], [(a, 2 * h * HEAD) for a in pairs]
 
     (packed,) = pack(arrays, gains, groups, heads, early, [2 * each])
     traded = trade(packed)
     (final,) = pack(arrays, gains, groups, heads, late, [extra + 2 * each])
     pieces = feed(prompt_states, feed_gain, gate_weight, up_weight, down_weight, groups, extra)
     traded, pieces, final = after((traded, pieces, final))
+    query, pair = split(traded, 0, 2)
+    pair_x = send(pair, OTHER_X)
+    queries = [query] + around(query)
+    pairs = [pair, send(pair, OTHER_CORE)]
     final = fold(trade(pieces), final)
-
-    query0, pair0 = split(traded, 0)
-    pair_x0 = send(pair0, OTHER_X)
-    queries0 = [query0] + around(query0)
-    pairs0 = [pair0, send(pair0, OTHER_CORE)]
-    query1, pair1 = split(traded, each)
-    pair_x1 = send(pair1, OTHER_X)
-    queries1 = [query1] + around(query1)
-    pairs1 = [pair1, send(pair1, OTHER_CORE)]
-    pair_x0, queries0, final = after((pair_x0, queries0, final))
+    pair_x, queries, token = after((pair_x, queries, final[:1, :16]))
     final = trade(final)
-    pairs0 += [pair_x0, send(pair_x0, OTHER_CORE)]
-    part0 = attend(*plain(queries0, pairs0), from_ring)
-
-    final, part0, queries1, pair_x1 = after((final, part0, queries1, pair_x1))
-    pairs1 += [pair_x1, send(pair_x1, OTHER_CORE)]
-    query2, pair2 = split(final, extra)
+    pairs += [pair_x, send(pair_x, OTHER_CORE)]
+    part0 = attend(*views(queries, pairs), from_ring)
+    final, part0 = after((final, part0))
+    query2, pair2 = split(final, extra, 1)
     pair_x2 = send(pair2, OTHER_X)
     queries2 = [query2] + around(query2)
     pairs2 = [pair2, send(pair2, OTHER_CORE)]
     result0 = trade_back(part0[0])
-    part1 = attend(*plain(queries1, pairs1))
+    part1 = attend(*views(queries, pairs, 1))
 
     tied = (part1, queries2, pair_x2, pairs2, result0, final)
     part1, queries2, pair_x2, pairs2, result0, folded = after(tied)
@@ -544,15 +547,15 @@
         lax.axis_size("wide"),
     )
     prompt_pair = lax.all_to_all(prompt_pair, "wide", split_axis=0, concat_axis=0, tiled=True)
-    others = attend(*plain(queries2[1:], pairs2))
-    result1, others, prompt_pair = after((result1, others, prompt_pair))
+    others = attend(*views(queries2[1:], pairs2))
+    result1[:3], others, prompt_pair = after((result1[:3], others, prompt_pair))
     below, above, across = others
     result2 = [send(below, DOWN), send(above, UP), send(across, ACROSS)]
-    result2 += attend(*plain(queries2[:1], pairs2))
-    results = [[result0], result1, result2]
+    result2 += attend(*views(queries2[:1], pairs2))
     cross_out = cross(prompt_lengths, final, extra + each, prompt_pair, per)
-    results, cross_out = after((results, cross_out))
-    self_out = merge(results)
+    self_out = merge([[result0], result1], heads * HEAD, 0)
+    result2, cross_out, self_out = after((result2, cross_out, self_out))
+    self_out = merge([result2], heads * HEAD, last, self_out)
     return (self_out, cross_out)
 
 

time: 193 us -> 187 us (0.969)
  starting transfers between devices: 58.2 us -> 53.8 us
  Pallas kernels: 88.5 us -> 91.8 us
  waiting for transfers between devices: 34.8 us -> 31.9 us
    ppermute x24 -> x18, starting transfers between devices: 31 us -> 24.5 us  [send(): return lax.ppermute(array, 'wide', pairs)]
    ppermute x24 -> x18, waiting for transfers between devices: 23.5 us -> 19.2 us  [send(): return lax.ppermute(array, 'wide', pairs)]
    pallas_call x1 -> x2, Pallas kernels: 4.17 us -> 7.33 us  [merge(): pl.pallas_call(lambda *refs: merge_kernel(sizes, *refs), grid=(count // s...]
    unnamed x58 -> x50, local copies, waits for them, and re-layouts: 6.87 us -> 5.42 us
  transfers between devices with their start and end apart: 29 -> 23, of which waited for: 8 -> 7; matrix products, arithmetic and copies ran while one was open for 0% -> 0% of each run, Pallas kernels for 42% -> 45%
where the time goes in v3:
time: 187 us; the launch traced here: 186 us
  Pallas kernels  91.8 us (49%)
  starting transfers between devices  53.8 us (29%)
  waiting for transfers between devices  31.9 us (17%)
  local copies, waits for them, and re-layouts  7.23 us (4%)
    pallas_call x4, Pallas kernels, attend(): pl.pallas_call(lambda *refs: attend_kernel(views, nq, nkv, ring, *refs),...  54 us
    ppermute x18, starting transfers between devices, send(): return lax.ppermute(array, 'wide', pairs)  24.5 us
    ppermute x18, waiting for transfers between devices, send(): return lax.ppermute(array, 'wide', pairs)  19.2 us
    all_to_all x3, starting transfers between devices, trade(): lax.all_to_all(array, 'narrow', split_axis=0, concat_axis=0, tiled=True)  18.1 us
    all_to_all x3, waiting for transfers between devices, trade(): lax.all_to_all(array, 'narrow', split_axis=0, concat_axis=0, tiled=True)  12.6 us
    pallas_call x1, Pallas kernels, feed(): pl.pallas_call(feed_kernel, grid=(hidden // tile,), in_specs=[pl.BlockSpe...  9.2 us
    pallas_call x2, Pallas kernels, pack(): pl.pallas_call(lambda *refs: pack_kernel(heads, plan, *refs), in_specs=[w...  9.19 us
    pallas_call x2, Pallas kernels, merge(): pl.pallas_call(lambda *refs: merge_kernel(sizes, *refs), grid=(count // s...  7.33 us
  transfers between devices with their start and end apart: 23, of which 7 were waited for; matrix products, arithmetic and copies ran while one was open for 0% of the time, Pallas kernels for 45%

profile of v3, /device:TPU:14, one launch (start us, length us, event | category | flops | bytes accessed | tf_op | source)
XLA Modules:
  0.0 186.3 jit_solution(10515235684187792430)
XLA Ops:
  0.6 4.3 %pack.2 = bf16[8,768,128]{2,1,0:T(8,128)(2,1)} custom-call(bf16[128,3072]{1,0:T(8,128)(2,1)} %refs_0_.4, bf16[128,3072]{1,0:T(8,128)(2,1)} %refs_1_.3, bf16[128,3072]{1,0:T(8,128)(2,1)} %refs_2_.3, f32[1,3072]{1,0:T(1,128)} %bitcast.5, f32[1,3072]{1,0:T(1,128)} %bitcast.7), custom_call_target="tpu_custom_call" | custom-call | flops 3145728 | bytes 6291456 | tf_op jit(solution)/shard_map/pack/pallas_call | solution.py:56
  4.9 5.8 %all-to-all-start = ((bf16[8,768,128]{2,1,0:T(8,128)(2,1)}), bf16[8,768,128]{2,1,0:T(8,128)(2,1)S(1)}, u32[]{:S(2)}, u32[]{:S(2)}) async-start(bf16[8,768,128]{2,1,0:T(8,128)(2,1)} %pack.2), calls=%async_computation | async-start | bytes 3145728 | tf_op jit(solution)/shard_map/all_to_all | solution.py:466
  10.8 4.9 %pack.3._ = bf16[8,1024,128]{2,1,0:T(8,128)(2,1)} custom-call(bf16[128,3072]{1,0:T(8,128)(2,1)} %refs_0_.4, bf16[128,3072]{1,0:T(8,128)(2,1)} %refs_1_.3, bf16[128,3072]{1,0:T(8,128)(2,1)} %refs_2_.3, f32[1,3072]{1,0:T(1,128)} %bitcast.6, f32[1,3072]{1,0:T(1,128)} %bitcast.8, bf16[128,3072]{1,0:T(8,128)(2,1)} %refs_5_.1, f32[1,3072]{1,0:T(1,128)} %bitcast.11), custom_call_target="tpu_custom_call" | custom-call | flops 3145728 | bytes 6291456 | tf_op jit(solution)/shard_map/pack/pallas_call | solution.py:56
  15.6 9.2 %feed.1 = bf16[8,256,128]{2,1,0:T(8,128)(2,1)} custom-call(bf16[24,4096]{1,0:T(8,128)(2,1)} %x_ref.3, f32[1,4096]{1,0:T(1,128)} %bitcast.9, bf16[4096,640]{1,0:T(8,128)(2,1)} %gate_ref.1, bf16[4096,640]{1,0:T(8,128)(2,1)} %up_ref.1, bf16[640,4096]{1,0:T(8,128)(2,1)} %down_ref.1), custom_call_target="tpu_custom_call" | custom-call | flops 503316480 | bytes 15728640 | tf_op jit(solution)/shard_map/feed/pallas_call | solution.py:109
  24.8 5.2 %all-to-all-done = bf16[8,768,128]{2,1,0:T(8,128)(2,1)S(1)} async-done(((bf16[8,768,128]{2,1,0:T(8,128)(2,1)}), bf16[8,768,128]{2,1,0:T(8,128)(2,1)S(1)}, u32[]{:S(2)}, u32[]{:S(2)}) %all-to-all-start) | async-done | bytes 1572896 | tf_op jit(solution)/shard_map/all_to_all | solution.py:466
  31.1 1.4 collective-permute-start
  32.5 4.0 %collective-permute-start.3 = (bf16[8,256,128]{2,1,0:T(8,128)(2,1)S(1)}, bf16[8,256,128]{2,1,0:T(8,128)(2,1)S(1)}, u32[]{:S(2)}, u32[]{:S(2)}) collective-permute-start(bf16[8,256,128]{2,1,0:T(8,128)(2,1)S(1)} %slice.14.refs_0_), channel_id=1, source_target_pairs={{0,32},{8,40},{16,48},{24,56},{32,0},{40,8},{48,16},{56,24},{64,96... | collective-permute-start | bytes 1572872 | tf_op jit(solution)/shard_map/ppermute | solution.py:433
  37.2 1.3 collective-permute-start.1
  38.5 4.9 %all-to-all-start.1 = ((bf16[8,256,128]{2,1,0:T(8,128)(2,1)}), bf16[8,256,128]{2,1,0:T(8,128)(2,1)S(1)}, u32[]{:S(2)}, u32[]{:S(2)}) async-start(bf16[8,256,128]{2,1,0:T(8,128)(2,1)} %feed.1), calls=%async_computation.1 | async-start | bytes 1048576 | tf_op jit(solution)/shard_map/all_to_all | solution.py:466
  43.4 5.9 %collective-permute-done.3.refs_3_ = bf16[8,256,128]{2,1,0:T(8,128)(2,1)S(1)} collective-permute-done((bf16[8,256,128]{2,1,0:T(8,128)(2,1)S(1)}, bf16[8,256,128]{2,1,0:T(8,128)(2,1)S(1)}, u32[]{:S(2)}, u32[]{:S(2)}) %collective-permute-start.3) | collective-permute-done | bytes 524320 | tf_op jit(solution)/shard_map/ppermute | solution.py:433
  49.3 11.0 %collective-permute-done.2.refs_2_ = bf16[8,256,128]{2,1,0:T(8,128)(2,1)S(1)} collective-permute-done((bf16[8,256,128]{2,1,0:T(8,128)(2,1)S(1)}, bf16[8,256,128]{2,1,0:T(8,128)(2,1)S(1)}, u32[]{:S(2)}, u32[]{:S(2)}) %collective-permute-start.2) | collective-permute-done | bytes 524320 | tf_op jit(solution)/shard_map/ppermute | solution.py:433
  61.8 1.9 %fold.1 = bf16[8,1024,128]{2,1,0:T(8,128)(2,1)} custom-call(bf16[8,256,128]{2,1,0:T(8,128)(2,1)} %copy-done.3, bf16[8,1024,128]{2,1,0:T(8,128)(2,1)} %pack.3._), custom_call_target="tpu_custom_call", output_to_operand_aliasing={{}: (1, {})} | custom-call | flops 262144 | bytes 1048576 | tf_op jit(solution)/shard_map/fold/pallas_call | solution.py:150
  63.7 7.4 %all-to-all-start.2 = ((bf16[8,1024,128]{2,1,0:T(8,128)(2,1)}), bf16[8,1024,128]{2,1,0:T(8,128)(2,1)S(1)}, u32[]{:S(2)}, u32[]{:S(2)}) async-start(bf16[8,1024,128]{2,1,0:T(8,128)(2,1)} %fold.1), calls=%async_computation.2 | async-start | bytes 4194304 | tf_op jit(solution)/shard_map/all_to_all | solution.py:466
  71.2 17.3 %attend.5 = bf16[4,144,1024]{2,1,0:T(8,128)(2,1)} custom-call(bf16[8,256,128]{2,1,0:T(8,128)(2,1)} %copy-done.5, bf16[8,256,128]{2,1,0:T(8,128)(2,1)} %copy-done.17, bf16[8,256,128]{2,1,0:T(8,128)(2,1)} %copy-done.16, bf16[8,256,128]{2,1,0:T(8,128)(2,1)} %copy-done.15, bf16[8,512,128]{2,1,0:T(8,128)(2,1)} %slice.13.refs_4_, ...), custom_call_target="tpu_custom_call" | custom-call | flops 8589934592 | bytes 6291456 | tf_op jit(solution)/shard_map/attend/pallas_call | solution.py:300
  88.5 6.9 %all-to-all-done.2.parts_ref.refs_1_ = bf16[8,1024,128]{2,1,0:T(8,128)(2,1)S(1)} async-done(((bf16[8,1024,128]{2,1,0:T(8,128)(2,1)}), bf16[8,1024,128]{2,1,0:T(8,128)(2,1)S(1)}, u32[]{:S(2)}, u32[]{:S(2)}) %all-to-all-start.2) | async-done | bytes 2097184 | tf_op jit(solution)/shard_map/all_to_all | solution.py:466
  95.4 5.3 %all-to-all-start.3 = ((bf16[4,144,1024]{2,1,0:T(8,128)(2,1)}), bf16[4,144,1024]{2,1,0:T(8,128)(2,1)S(1)}, u32[]{:S(2)}, u32[]{:S(2)}) async-start(bf16[4,144,1024]{2,1,0:T(8,128)(2,1)} %attend.5), calls=%async_computation.3 | async-start | bytes 2359296 | tf_op jit(solution)/shard_map/all_to_all | solution.py:446
  100.7 3.6 %collective-permute-start.8 = (bf16[8,128,128]{2,1,0:T(8,128)(2,1)S(1)}, bf16[8,128,128]{2,1,0:T(8,128)(2,1)S(1)}, u32[]{:S(2)}, u32[]{:S(2)}) collective-permute-start(bf16[8,128,128]{2,1,0:T(8,128)(2,1)S(1)} %slice.15.refs_0_), channel_id=1, source_target_pairs={{0,32},{8,40},{16,48},{24,56},{32,0},{40,8},{48,16},{56,24},{64,96... | collective-permute-start | bytes 786440 | tf_op jit(solution)/shard_map/ppermute | solution.py:433
  104.3 1.2 collective-permute-start.7
  106.5 2.2 %collective-permute-start.9 = (bf16[8,256,128]{2,1,0:T(8,128)(2,1)S(1)}, bf16[8,256,128]{2,1,0:T(8,128)(2,1)}, u32[]{:S(2)}, u32[]{:S(2)}) collective-permute-start(bf16[8,256,128]{2,1,0:T(8,128)(2,1)S(1)} %slice.16.refs_3_.refs_1_), channel_id=1, source_target_pairs={{0,64},{8,72},{16,80},{24,88},{32,96},{40,104},{48,112},{56,120},{... | collective-permute-start | bytes 1572872 | tf_op jit(solution)/shard_map/ppermute | solution.py:433
  108.7 17.2 %attend.4 = (bf16[144,1024]{1,0:T(8,128)(2,1)}, bf16[144,1024]{1,0:T(8,128)(2,1)}, bf16[144,1024]{1,0:T(8,128)(2,1)}, bf16[144,1024]{1,0:T(8,128)(2,1)}) custom-call(bf16[8,256,128]{2,1,0:T(8,128)(2,1)} %copy-done.5, bf16[8,256,128]{2,1,0:T(8,128)(2,1)} %copy-done.17, bf16[8,256,128]{2,1,0:T(8,128)(2,1)} %copy-done.16, bf16[8,256,128]{2,1,0:T(8,128)(2,1)} %copy-done.15, ...), custom_call_target="tpu_custom_call" | custom-call | flops 8589934592 | bytes 6291456 | tf_op jit(solution)/shard_map/attend/pallas_call | solution.py:300
  127.1 1.2 collective-permute-done.6.refs_0_
  130.6 5.3 %project.1 = bf16[16,192,128]{2,1,0:T(8,128)(2,1)} custom-call(bf16[24,4096]{1,0:T(8,128)(2,1)} %x_ref.3, bf16[8,1024,128]{2,1,0:T(8,128)(2,1)} %copy-done, f32[1,4096]{1,0:T(1,128)} %bitcast.10, bf16[4096,384]{1,0:T(8,128)(2,1)} %key_ref.1, bf16[4096,384]{1,0:T(8,128)(2,1)} %value_ref.1, f32[1,384]{1,0:T(1,128)} %broadcast_in_dim.25.key_gain_ref), custom_call_target="tpu_custom_call" | custom-call | flops 201326592 | bytes 6291456 | tf_op jit(solution)/shard_map/project/pallas_call | solution.py:200
  135.9 5.9 %all-to-all-start.4 = ((bf16[16,192,128]{2,1,0:T(8,128)(2,1)}), bf16[16,192,128]{2,1,0:T(8,128)(2,1)S(1)}, u32[]{:S(2)}, u32[]{:S(2)}) async-start(bf16[16,192,128]{2,1,0:T(8,128)(2,1)} %project.1), calls=%async_computation.4 | async-start | bytes 1572864 | tf_op jit(solution)/shard_map/all_to_all | solution.py:549
  141.8 2.7 %collective-permute-start.11 = (bf16[144,1024]{1,0:T(8,128)(2,1)S(1)}, bf16[144,1024]{1,0:T(8,128)(2,1)S(1)}, u32[]{:S(2)}, u32[]{:S(2)}) collective-permute-start(bf16[144,1024]{1,0:T(8,128)(2,1)S(1)} %copy-done.21), channel_id=1, source_target_pairs={{0,48},{8,56},{16,0},{24,8},{32,16},{40,24},{48,32},{56,40},{64,11... | collective-permute-start | bytes 884744 | tf_op jit(solution)/shard_map/ppermute | solution.py:433
  144.6 2.3 %collective-permute-start.17 = (bf16[144,1024]{1,0:T(8,128)(2,1)S(1)}, bf16[144,1024]{1,0:T(8,128)(2,1)S(1)}, u32[]{:S(2)}, u32[]{:S(2)}) collective-permute-start(bf16[144,1024]{1,0:T(8,128)(2,1)S(1)} %copy-done.19), channel_id=1, source_target_pairs={{0,32},{8,40},{16,48},{24,56},{32,0},{40,8},{48,16},{56,24},{64,96... | collective-permute-start | bytes 884744 | tf_op jit(solution)/shard_map/ppermute | solution.py:433
  147.7 13.6 %attend.6 = (bf16[144,1024]{1,0:T(8,128)(2,1)}, bf16[144,1024]{1,0:T(8,128)(2,1)}, bf16[144,1024]{1,0:T(8,128)(2,1)}) custom-call(bf16[8,128,128]{2,1,0:T(8,128)(2,1)} %copy-done.24, bf16[8,128,128]{2,1,0:T(8,128)(2,1)} %copy-done.23, bf16[8,128,128]{2,1,0:T(8,128)(2,1)} %copy-done.22, bf16[8,256,128]{2,1,0:T(8,128)(2,1)} %copy-done.4, ...), custom_call_target="tpu_custom_call" | custom-call | flops 6442450944 | bytes 6291456 | tf_op jit(solution)/shard_map/attend/pallas_call | solution.py:300
  161.4 1.2 collective-permute-start.14
  163.5 1.8 collective-permute-start.16
  165.9 5.9 %attend.7.refs_3_ = bf16[144,1024]{1,0:T(8,128)(2,1)} custom-call(bf16[8,128,128]{2,1,0:T(8,128)(2,1)} %copy-done.12, bf16[8,256,128]{2,1,0:T(8,128)(2,1)} %copy-done.4, bf16[8,256,128]{2,1,0:T(8,128)(2,1)} %copy-done.14, bf16[8,256,128]{2,1,0:T(8,128)(2,1)} %collective-permute-done.9.refs_5_.refs_3_, bf16[8,256,128]{2,1,0:T(8,128)(2,1)} %copy-done.18), custom_call_target="tpu_custom_call" | custom-call | flops 2147483648 | bytes 6291456 | tf_op jit(solution)/shard_map/attend/pallas_call | solution.py:300
  172.6 3.8 %merge.2.refs_4_ = bf16[1024,384]{1,0:T(8,128)(2,1)} custom-call(bf16[4,144,1024]{2,1,0:T(8,128)(2,1)} %copy-done.1, bf16[144,1024]{1,0:T(8,128)(2,1)} %get-tuple-element.78.refs_1_, bf16[144,1024]{1,0:T(8,128)(2,1)} %copy-done.6, bf16[144,1024]{1,0:T(8,128)(2,1)} %copy-done.7, bf16[144,1024]{1,0:T(8,128)(2,1)} %copy-done.8), custom_call_target="tpu_custom_call" | custom-call | flops 2097152 | bytes 4194304 | tf_op jit(solution)/shard_map/merge/pallas_call | solution.py:350
  176.5 4.7 %cross.1 = bf16[1024,384]{1,0:T(8,128)(2,1)} custom-call(s32[1]{0:T(128)S(6)} %copy.23.refs_0_, bf16[8,1024,128]{2,1,0:T(8,128)(2,1)} %copy-done, bf16[16,192,128]{2,1,0:T(8,128)(2,1)} %copy-done.2), custom_call_target="tpu_custom_call" | custom-call | flops 805306368 | bytes 3145728 | tf_op jit(solution)/shard_map/cross/pallas_call | solution.py:394
  182.7 3.5 %merge.3 = bf16[1024,384]{1,0:T(8,128)(2,1)} custom-call(bf16[144,1024]{1,0:T(8,128)(2,1)} %copy-done.9, bf16[144,1024]{1,0:T(8,128)(2,1)} %copy-done.10, bf16[144,1024]{1,0:T(8,128)(2,1)} %copy-done.11, bf16[144,1024]{1,0:T(8,128)(2,1)} %attend.7.refs_3_, bf16[1024,384]{1,0:T(8,128)(2,1)} %merge.2.refs_4_), custom_call_target="tpu_custom_call", output_to_operand_aliasing={{}: (4, {})} | custom-call | flops 1048576 | bytes 2097152 | tf_op jit(solution)/shard_map/merge/pallas_call | solution.py:350
  (81 shorter events, 11.7 us)
Async XLA Ops:
  4.9 25.1 %all-to-all-start = ((bf16[8,768,128]{2,1,0:T(8,128)(2,1)}), bf16[8,768,128]{2,1,0:T(8,128)(2,1)S(1)}, u32[]{:S(2)}, u32[]{:S(2)}) async-start(bf16[8,768,128]{2,1,0:T(8,128)(2,1)} %pack.2), calls=%async_computation | async-start | bytes 3145728 | tf_op jit(solution)/shard_map/all_to_all | solution.py:466
  31.1 29.3 %collective-permute-start = (bf16[8,512,128]{2,1,0:T(8,128)(2,1)}, bf16[8,512,128]{2,1,0:T(8,128)(2,1)}, u32[]{:S(2)}, u32[]{:S(2)}) collective-permute-start(bf16[8,512,128]{2,1,0:T(8,128)(2,1)} %slice.13.refs_4_), channel_id=1, source_target_pairs={{0,64},{8,72},{16,80},{24,88},{32,96},{40,104},{48,112},{56,120},{... | collective-permute-start | bytes 3145736 | tf_op jit(solution)/shard_map/ppermute | solution.py:433
  32.5 31.2 %copy-start.5 = (bf16[8,256,128]{2,1,0:T(8,128)(2,1)}, bf16[8,256,128]{2,1,0:T(8,128)(2,1)S(1)}, u32[]{:S(2)}) copy-start(bf16[8,256,128]{2,1,0:T(8,128)(2,1)S(1)} %slice.14.refs_0_) | copy-start | bytes 1572868
  32.5 16.8 %collective-permute-start.3 = (bf16[8,256,128]{2,1,0:T(8,128)(2,1)S(1)}, bf16[8,256,128]{2,1,0:T(8,128)(2,1)S(1)}, u32[]{:S(2)}, u32[]{:S(2)}) collective-permute-start(bf16[8,256,128]{2,1,0:T(8,128)(2,1)S(1)} %slice.14.refs_0_), channel_id=1, source_target_pairs={{0,32},{8,40},{16,48},{24,56},{32,0},{40,8},{48,16},{56,24},{64,96... | collective-permute-start | bytes 1572872 | tf_op jit(solution)/shard_map/ppermute | solution.py:433
  36.5 23.8 %collective-permute-start.2 = (bf16[8,256,128]{2,1,0:T(8,128)(2,1)S(1)}, bf16[8,256,128]{2,1,0:T(8,128)(2,1)S(1)}, u32[]{:S(2)}, u32[]{:S(2)}) collective-permute-start(bf16[8,256,128]{2,1,0:T(8,128)(2,1)S(1)} %slice.14.refs_0_), channel_id=1, source_target_pairs={{0,48},{8,56},{16,0},{24,8},{32,16},{40,24},{48,32},{56,40},{64,11... | collective-permute-start | bytes 1572872 | tf_op jit(solution)/shard_map/ppermute | solution.py:433
  37.2 23.1 %collective-permute-start.1 = (bf16[8,256,128]{2,1,0:T(8,128)(2,1)S(1)}, bf16[8,256,128]{2,1,0:T(8,128)(2,1)S(1)}, u32[]{:S(2)}, u32[]{:S(2)}) collective-permute-start(bf16[8,256,128]{2,1,0:T(8,128)(2,1)S(1)} %slice.14.refs_0_), channel_id=1, source_target_pairs={{0,16},{8,24},{16,32},{24,40},{32,48},{40,56},{48,0},{56,8},{64,80... | collective-permute-start | bytes 1572872 | tf_op jit(solution)/shard_map/ppermute | solution.py:433
  38.5 22.5 %all-to-all-start.1 = ((bf16[8,256,128]{2,1,0:T(8,128)(2,1)}), bf16[8,256,128]{2,1,0:T(8,128)(2,1)S(1)}, u32[]{:S(2)}, u32[]{:S(2)}) async-start(bf16[8,256,128]{2,1,0:T(8,128)(2,1)} %feed.1), calls=%async_computation.1 | async-start | bytes 1048576 | tf_op jit(solution)/shard_map/all_to_all | solution.py:466
  43.4 27.7 %collective-permute-start.4 = (bf16[8,512,128]{2,1,0:T(8,128)(2,1)}, bf16[8,512,128]{2,1,0:T(8,128)(2,1)}, u32[]{:S(2)}, u32[]{:S(2)}) collective-permute-start(bf16[8,512,128]{2,1,0:T(8,128)(2,1)} %slice.13.refs_4_), channel_id=1, source_target_pairs={{0,8},{8,0},{16,24},{24,16},{32,40},{40,32},{48,56},{56,48},{64,72... | collective-permute-start | bytes 3145736 | tf_op jit(solution)/shard_map/ppermute | solution.py:433
  49.3 21.9 %copy-start.15 = (bf16[8,256,128]{2,1,0:T(8,128)(2,1)}, bf16[8,256,128]{2,1,0:T(8,128)(2,1)S(1)}, u32[]{:S(2)}) copy-start(bf16[8,256,128]{2,1,0:T(8,128)(2,1)S(1)} %collective-permute-done.3.refs_3_) | copy-start | bytes 1572868
  60.3 10.8 %collective-permute-start.5 = (bf16[8,512,128]{2,1,0:T(8,128)(2,1)}, bf16[8,512,128]{2,1,0:T(8,128)(2,1)}, u32[]{:S(2)}, u32[]{:S(2)}) collective-permute-start(bf16[8,512,128]{2,1,0:T(8,128)(2,1)} %collective-permute-done.refs_6_), channel_id=1, source_target_pairs={{0,8},{8,0},{16,24},{24,16},{32,40},{40,32},{48,56},{56,48},{64,72... | collective-permute-start | bytes 3145736 | tf_op jit(solution)/shard_map/ppermute | solution.py:433
  63.7 31.6 %all-to-all-start.2 = ((bf16[8,1024,128]{2,1,0:T(8,128)(2,1)}), bf16[8,1024,128]{2,1,0:T(8,128)(2,1)S(1)}, u32[]{:S(2)}, u32[]{:S(2)}) async-start(bf16[8,1024,128]{2,1,0:T(8,128)(2,1)} %fold.1), calls=%async_computation.2 | async-start | bytes 4194304 | tf_op jit(solution)/shard_map/all_to_all | solution.py:466
  95.4 30.6 %copy-start = (bf16[8,1024,128]{2,1,0:T(8,128)(2,1)}, bf16[8,1024,128]{2,1,0:T(8,128)(2,1)S(1)}, u32[]{:S(2)}) copy-start(bf16[8,1024,128]{2,1,0:T(8,128)(2,1)S(1)} %all-to-all-done.2.parts_ref.refs_1_) | copy-start | bytes 6291460
  95.4 34.4 %all-to-all-start.3 = ((bf16[4,144,1024]{2,1,0:T(8,128)(2,1)}), bf16[4,144,1024]{2,1,0:T(8,128)(2,1)S(1)}, u32[]{:S(2)}, u32[]{:S(2)}) async-start(bf16[4,144,1024]{2,1,0:T(8,128)(2,1)} %attend.5), calls=%async_computation.3 | async-start | bytes 2359296 | tf_op jit(solution)/shard_map/all_to_all | solution.py:446
  100.7 25.3 %copy-start.12 = (bf16[8,128,128]{2,1,0:T(8,128)(2,1)}, bf16[8,128,128]{2,1,0:T(8,128)(2,1)S(1)}, u32[]{:S(2)}) copy-start(bf16[8,128,128]{2,1,0:T(8,128)(2,1)S(1)} %slice.15.refs_0_) | copy-start | bytes 786436
  100.7 25.3 %collective-permute-start.8 = (bf16[8,128,128]{2,1,0:T(8,128)(2,1)S(1)}, bf16[8,128,128]{2,1,0:T(8,128)(2,1)S(1)}, u32[]{:S(2)}, u32[]{:S(2)}) collective-permute-start(bf16[8,128,128]{2,1,0:T(8,128)(2,1)S(1)} %slice.15.refs_0_), channel_id=1, source_target_pairs={{0,32},{8,40},{16,48},{24,56},{32,0},{40,8},{48,16},{56,24},{64,96... | collective-permute-start | bytes 786440 | tf_op jit(solution)/shard_map/ppermute | solution.py:433
  104.3 22.8 %collective-permute-start.7 = (bf16[8,128,128]{2,1,0:T(8,128)(2,1)S(1)}, bf16[8,128,128]{2,1,0:T(8,128)(2,1)S(1)}, u32[]{:S(2)}, u32[]{:S(2)}) collective-permute-start(bf16[8,128,128]{2,1,0:T(8,128)(2,1)S(1)} %slice.15.refs_0_), channel_id=1, source_target_pairs={{0,48},{8,56},{16,0},{24,8},{32,16},{40,24},{48,32},{56,40},{64,11... | collective-permute-start | bytes 786440 | tf_op jit(solution)/shard_map/ppermute | solution.py:433
  105.5 22.8 %collective-permute-start.6 = (bf16[8,128,128]{2,1,0:T(8,128)(2,1)S(1)}, bf16[8,128,128]{2,1,0:T(8,128)(2,1)S(1)}, u32[]{:S(2)}, u32[]{:S(2)}) collective-permute-start(bf16[8,128,128]{2,1,0:T(8,128)(2,1)S(1)} %slice.15.refs_0_), channel_id=1, source_target_pairs={{0,16},{8,24},{16,32},{24,40},{32,48},{40,56},{48,0},{56,8},{64,80... | collective-permute-start | bytes 786440 | tf_op jit(solution)/shard_map/ppermute | solution.py:433
  106.4 19.6 %copy-start.4 = (bf16[8,256,128]{2,1,0:T(8,128)(2,1)}, bf16[8,256,128]{2,1,0:T(8,128)(2,1)S(1)}, u32[]{:S(2)}) copy-start(bf16[8,256,128]{2,1,0:T(8,128)(2,1)S(1)} %slice.16.refs_3_.refs_1_) | copy-start | bytes 1572868
  106.4 23.5 %copy-start.13 = (f32[384]{0:T(512)S(1)}, f32[384]{0:T(512)}, u32[]{:S(2)}) copy-start(f32[384]{0:T(512)} %param.26) | copy-start | bytes 4612
  106.4 21.9 %collective-permute-start.10 = (bf16[8,256,128]{2,1,0:T(8,128)(2,1)S(1)}, bf16[8,256,128]{2,1,0:T(8,128)(2,1)S(1)}, u32[]{:S(2)}, u32[]{:S(2)}) collective-permute-start(bf16[8,256,128]{2,1,0:T(8,128)(2,1)S(1)} %slice.16.refs_3_.refs_1_), channel_id=1, source_target_pairs={{0,8},{8,0},{16,24},{24,16},{32,40},{40,32},{48,56},{56,48},{64,72... | collective-permute-start | bytes 1572872 | tf_op jit(solution)/shard_map/ppermute | solution.py:433
  106.5 23.3 %collective-permute-start.9 = (bf16[8,256,128]{2,1,0:T(8,128)(2,1)S(1)}, bf16[8,256,128]{2,1,0:T(8,128)(2,1)}, u32[]{:S(2)}, u32[]{:S(2)}) collective-permute-start(bf16[8,256,128]{2,1,0:T(8,128)(2,1)S(1)} %slice.16.refs_3_.refs_1_), channel_id=1, source_target_pairs={{0,64},{8,72},{16,80},{24,88},{32,96},{40,104},{48,112},{56,120},{... | collective-permute-start | bytes 1572872 | tf_op jit(solution)/shard_map/ppermute | solution.py:433
  129.8 17.1 %collective-permute-start.13 = (bf16[8,256,128]{2,1,0:T(8,128)(2,1)}, bf16[8,256,128]{2,1,0:T(8,128)(2,1)S(1)}, u32[]{:S(2)}, u32[]{:S(2)}) collective-permute-start(bf16[8,256,128]{2,1,0:T(8,128)(2,1)} %collective-permute-done.9.refs_5_.refs_3_), channel_id=1, source_target_pairs={{0,8},{8,0},{16,24},{24,16},{32,40},{40,32},{48,56},{56,48},{64,72... | collective-permute-start | bytes 1572872 | tf_op jit(solution)/shard_map/ppermute | solution.py:433
  130.6 11.3 %copy-start.21 = (bf16[144,1024]{1,0:T(8,128)(2,1)S(1)}, bf16[144,1024]{1,0:T(8,128)(2,1)}, u32[]{:S(2)}) copy-start(bf16[144,1024]{1,0:T(8,128)(2,1)} %get-tuple-element.60) | copy-start | bytes 884740
  130.6 14.0 %copy-start.20 = (bf16[144,1024]{1,0:T(8,128)(2,1)S(1)}, bf16[144,1024]{1,0:T(8,128)(2,1)}, u32[]{:S(2)}) copy-start(bf16[144,1024]{1,0:T(8,128)(2,1)} %get-tuple-element.61) | copy-start | bytes 884740
  130.6 14.0 %copy-start.19 = (bf16[144,1024]{1,0:T(8,128)(2,1)S(1)}, bf16[144,1024]{1,0:T(8,128)(2,1)}, u32[]{:S(2)}) copy-start(bf16[144,1024]{1,0:T(8,128)(2,1)} %get-tuple-element.81) | copy-start | bytes 884740
  135.9 25.4 %all-to-all-start.4 = ((bf16[16,192,128]{2,1,0:T(8,128)(2,1)}), bf16[16,192,128]{2,1,0:T(8,128)(2,1)S(1)}, u32[]{:S(2)}, u32[]{:S(2)}) async-start(bf16[16,192,128]{2,1,0:T(8,128)(2,1)} %project.1), calls=%async_computation.4 | async-start | bytes 1572864 | tf_op jit(solution)/shard_map/all_to_all | solution.py:549
  141.8 19.5 %collective-permute-start.11 = (bf16[144,1024]{1,0:T(8,128)(2,1)S(1)}, bf16[144,1024]{1,0:T(8,128)(2,1)S(1)}, u32[]{:S(2)}, u32[]{:S(2)}) collective-permute-start(bf16[144,1024]{1,0:T(8,128)(2,1)S(1)} %copy-done.21), channel_id=1, source_target_pairs={{0,48},{8,56},{16,0},{24,8},{32,16},{40,24},{48,32},{56,40},{64,11... | collective-permute-start | bytes 884744 | tf_op jit(solution)/shard_map/ppermute | solution.py:433
  144.6 16.8 %collective-permute-start.12 = (bf16[144,1024]{1,0:T(8,128)(2,1)S(1)}, bf16[144,1024]{1,0:T(8,128)(2,1)S(1)}, u32[]{:S(2)}, u32[]{:S(2)}) collective-permute-start(bf16[144,1024]{1,0:T(8,128)(2,1)S(1)} %copy-done.20), channel_id=1, source_target_pairs={{0,16},{8,24},{16,32},{24,40},{32,48},{40,56},{48,0},{56,8},{64,80... | collective-permute-start | bytes 884744 | tf_op jit(solution)/shard_map/ppermute | solution.py:433
  144.6 27.3 %collective-permute-start.17 = (bf16[144,1024]{1,0:T(8,128)(2,1)S(1)}, bf16[144,1024]{1,0:T(8,128)(2,1)S(1)}, u32[]{:S(2)}, u32[]{:S(2)}) collective-permute-start(bf16[144,1024]{1,0:T(8,128)(2,1)S(1)} %copy-done.19), channel_id=1, source_target_pairs={{0,32},{8,40},{16,48},{24,56},{32,0},{40,8},{48,16},{56,24},{64,96... | collective-permute-start | bytes 884744 | tf_op jit(solution)/shard_map/ppermute | solution.py:433
  161.4 19.8 %collective-permute-start.14 = (bf16[144,1024]{1,0:T(8,128)(2,1)}, bf16[144,1024]{1,0:T(8,128)(2,1)S(1)}, u32[]{:S(2)}, u32[]{:S(2)}) collective-permute-start(bf16[144,1024]{1,0:T(8,128)(2,1)} %get-tuple-element.72), channel_id=1, source_target_pairs={{0,48},{8,56},{16,0},{24,8},{32,16},{40,24},{48,32},{56,40},{64,11... | collective-permute-start | bytes 884744 | tf_op jit(solution)/shard_map/ppermute | solution.py:433
  162.6 18.6 %collective-permute-start.15 = (bf16[144,1024]{1,0:T(8,128)(2,1)}, bf16[144,1024]{1,0:T(8,128)(2,1)S(1)}, u32[]{:S(2)}, u32[]{:S(2)}) collective-permute-start(bf16[144,1024]{1,0:T(8,128)(2,1)} %get-tuple-element.73), channel_id=1, source_target_pairs={{0,16},{8,24},{16,32},{24,40},{32,48},{40,56},{48,0},{56,8},{64,80... | collective-permute-start | bytes 884744 | tf_op jit(solution)/shard_map/ppermute | solution.py:433
  163.5 17.7 %collective-permute-start.16 = (bf16[144,1024]{1,0:T(8,128)(2,1)}, bf16[144,1024]{1,0:T(8,128)(2,1)S(1)}, u32[]{:S(2)}, u32[]{:S(2)}) collective-permute-start(bf16[144,1024]{1,0:T(8,128)(2,1)} %get-tuple-element.74), channel_id=1, source_target_pairs={{0,32},{8,40},{16,48},{24,56},{32,0},{40,8},{48,16},{56,24},{64,96... | collective-permute-start | bytes 884744 | tf_op jit(solution)/shard_map/ppermute | solution.py:433
  (16 other events, 54.3 us)

commit v4 on v3

--- a/solution.py
+++ b/solution.py
@@ -236,19 +236,23 @@
     copies = [
         pltpu.make_async_copy(src, dst, sems.at[i]) for i, (src, dst) in enumerate(copies)
     ]
-    for copy in copies:
+    q_copies, kv_copies = copies[:nq], copies[nq:]
+    for copy in q_copies[:1] + kv_copies + q_copies[1:]:
         copy.start()
-    for copy in copies:
-        copy.wait()
+    q_copies[0].wait()
     per_q = TILE // HEAD
     per_k = CHUNK // HEAD
     per_block = blocks // per_q
-
-    def tile(t, _):
+    chunk_copies = 2 * per_k // blocks
+
+    def tile(t, first):
         q = q_s[pl.ds(t * per_q, per_q)].reshape(TILE, HEAD)
         acc = jnp.zeros((HEAD, TILE), jnp.float32)
         total = jnp.zeros((8, TILE), jnp.float32)
         for j in range(nkv * blocks // per_k):
+            if first is True:
+                for copy in kv_copies[j * chunk_copies : (j + 1) * chunk_copies]:
+                    copy.wait()
             keys = k_s[j * per_k : (j + 1) * per_k].reshape(CHUNK, HEAD)
             s = lax.dot_general(
                 keys, q, (((1,), (1,)), ((), ())), preferred_element_type=jnp.float32
@@ -274,7 +278,10 @@
         o_s[slot, HEAD:, columns] = words.astype(jnp.bfloat16)
         return 0
 
-    lax.fori_loop(0, nq * per_block, tile, 0)
+    tile(0, True)
+    for copy in q_copies[1:]:
+        copy.wait()
+    lax.fori_loop(1, nq * per_block, tile, 0)
     if ring is not None:
         copies = [pltpu.make_async_copy(o_s, outs[0], sems.at[0])]
     else:
@@ -335,7 +342,7 @@
     arrays = [array for group in results for array in group]
     sizes = [len(group) for group in results]
     count = arrays[0].shape[-1]
-    step = 256
+    step = 512
     specs = []
     for array in arrays:
         if array.ndim == 2:

time: 187 us -> 184 us (0.984)
  Pallas kernels: 91.8 us -> 87.8 us
    pallas_call x2, Pallas kernels: 7.33 us -> 4.72 us  [merge(): pl.pallas_call(lambda *refs: merge_kernel(sizes, *refs), grid=(count // s...]
  transfers between devices with their start and end apart: 23 -> 23, of which waited for: 7 -> 8; matrix products, arithmetic and copies ran while one was open for 0% -> 0% of each run, Pallas kernels for 45% -> 44%
where the time goes in v4:
time: 184 us; the launch traced here: 183 us
  Pallas kernels  87.8 us (48%)
  starting transfers between devices  54 us (29%)
  waiting for transfers between devices  32.9 us (18%)
  local copies, waits for them, and re-layouts  6.84 us (4%)
    pallas_call x4, Pallas kernels, attend(): pl.pallas_call(lambda *refs: attend_kernel(views, nq, nkv, ring, *refs),...  52.7 us
    ppermute x18, starting transfers between devices, send(): return lax.ppermute(array, 'wide', pairs)  24.7 us
    ppermute x18, waiting for transfers between devices, send(): return lax.ppermute(array, 'wide', pairs)  19.8 us
    all_to_all x3, starting transfers between devices, trade(): lax.all_to_all(array, 'narrow', split_axis=0, concat_axis=0, tiled=True)  18.1 us
    all_to_all x3, waiting for transfers between devices, trade(): lax.all_to_all(array, 'narrow', split_axis=0, concat_axis=0, tiled=True)  13 us
    pallas_call x1, Pallas kernels, feed(): pl.pallas_call(feed_kernel, grid=(hidden // tile,), in_specs=[pl.BlockSpe...  9.2 us
    pallas_call x2, Pallas kernels, pack(): pl.pallas_call(lambda *refs: pack_kernel(heads, plan, *refs), in_specs=[w...  9.19 us
    all_to_all x1, starting transfers between devices, body(): lax.all_to_all(prompt_pair, 'wide', split_axis=0, concat_axis=0, tiled=True)  5.9 us
  transfers between devices with their start and end apart: 23, of which 8 were waited for; matrix products, arithmetic and copies ran while one was open for 0% of the time, Pallas kernels for 44%

profile of v4, /device:TPU:14, one launch (start us, length us, event | category | flops | bytes accessed | tf_op | source)
XLA Modules:
  0.0 183.1 jit_solution(15533317665862625462)
XLA Ops:
  0.6 4.3 %pack.2 = bf16[8,768,128]{2,1,0:T(8,128)(2,1)} custom-call(bf16[128,3072]{1,0:T(8,128)(2,1)} %refs_0_.4, bf16[128,3072]{1,0:T(8,128)(2,1)} %refs_1_.3, bf16[128,3072]{1,0:T(8,128)(2,1)} %refs_2_.3, f32[1,3072]{1,0:T(1,128)} %bitcast.5, f32[1,3072]{1,0:T(1,128)} %bitcast.7), custom_call_target="tpu_custom_call" | custom-call | flops 3145728 | bytes 6291456 | tf_op jit(solution)/shard_map/pack/pallas_call | solution.py:56
  4.9 5.8 %all-to-all-start = ((bf16[8,768,128]{2,1,0:T(8,128)(2,1)}), bf16[8,768,128]{2,1,0:T(8,128)(2,1)S(1)}, u32[]{:S(2)}, u32[]{:S(2)}) async-start(bf16[8,768,128]{2,1,0:T(8,128)(2,1)} %pack.2), calls=%async_computation | async-start | bytes 3145728 | tf_op jit(solution)/shard_map/all_to_all | solution.py:473
  10.8 4.9 %pack.3._ = bf16[8,1024,128]{2,1,0:T(8,128)(2,1)} custom-call(bf16[128,3072]{1,0:T(8,128)(2,1)} %refs_0_.4, bf16[128,3072]{1,0:T(8,128)(2,1)} %refs_1_.3, bf16[128,3072]{1,0:T(8,128)(2,1)} %refs_2_.3, f32[1,3072]{1,0:T(1,128)} %bitcast.6, f32[1,3072]{1,0:T(1,128)} %bitcast.8, bf16[128,3072]{1,0:T(8,128)(2,1)} %refs_5_.1, f32[1,3072]{1,0:T(1,128)} %bitcast.11), custom_call_target="tpu_custom_call" | custom-call | flops 3145728 | bytes 6291456 | tf_op jit(solution)/shard_map/pack/pallas_call | solution.py:56
  15.6 9.2 %feed.1 = bf16[8,256,128]{2,1,0:T(8,128)(2,1)} custom-call(bf16[24,4096]{1,0:T(8,128)(2,1)} %x_ref.3, f32[1,4096]{1,0:T(1,128)} %bitcast.9, bf16[4096,640]{1,0:T(8,128)(2,1)} %gate_ref.1, bf16[4096,640]{1,0:T(8,128)(2,1)} %up_ref.1, bf16[640,4096]{1,0:T(8,128)(2,1)} %down_ref.1), custom_call_target="tpu_custom_call" | custom-call | flops 503316480 | bytes 15728640 | tf_op jit(solution)/shard_map/feed/pallas_call | solution.py:109
  24.8 5.2 %all-to-all-done = bf16[8,768,128]{2,1,0:T(8,128)(2,1)S(1)} async-done(((bf16[8,768,128]{2,1,0:T(8,128)(2,1)}), bf16[8,768,128]{2,1,0:T(8,128)(2,1)S(1)}, u32[]{:S(2)}, u32[]{:S(2)}) %all-to-all-start) | async-done | bytes 1572896 | tf_op jit(solution)/shard_map/all_to_all | solution.py:473
  31.1 1.4 collective-permute-start
  32.5 4.0 %collective-permute-start.3 = (bf16[8,256,128]{2,1,0:T(8,128)(2,1)S(1)}, bf16[8,256,128]{2,1,0:T(8,128)(2,1)S(1)}, u32[]{:S(2)}, u32[]{:S(2)}) collective-permute-start(bf16[8,256,128]{2,1,0:T(8,128)(2,1)S(1)} %slice.14.refs_0_), channel_id=1, source_target_pairs={{0,32},{8,40},{16,48},{24,56},{32,0},{40,8},{48,16},{56,24},{64,96... | collective-permute-start | bytes 1572872 | tf_op jit(solution)/shard_map/ppermute | solution.py:440
  37.2 1.3 collective-permute-start.1
  38.5 4.9 %all-to-all-start.1 = ((bf16[8,256,128]{2,1,0:T(8,128)(2,1)}), bf16[8,256,128]{2,1,0:T(8,128)(2,1)S(1)}, u32[]{:S(2)}, u32[]{:S(2)}) async-start(bf16[8,256,128]{2,1,0:T(8,128)(2,1)} %feed.1), calls=%async_computation.1 | async-start | bytes 1048576 | tf_op jit(solution)/shard_map/all_to_all | solution.py:473
  43.4 5.9 %collective-permute-done.3.refs_3_ = bf16[8,256,128]{2,1,0:T(8,128)(2,1)S(1)} collective-permute-done((bf16[8,256,128]{2,1,0:T(8,128)(2,1)S(1)}, bf16[8,256,128]{2,1,0:T(8,128)(2,1)S(1)}, u32[]{:S(2)}, u32[]{:S(2)}) %collective-permute-start.3) | collective-permute-done | bytes 524320 | tf_op jit(solution)/shard_map/ppermute | solution.py:440
  49.3 11.0 %collective-permute-done.2.refs_2_ = bf16[8,256,128]{2,1,0:T(8,128)(2,1)S(1)} collective-permute-done((bf16[8,256,128]{2,1,0:T(8,128)(2,1)S(1)}, bf16[8,256,128]{2,1,0:T(8,128)(2,1)S(1)}, u32[]{:S(2)}, u32[]{:S(2)}) %collective-permute-start.2) | collective-permute-done | bytes 524320 | tf_op jit(solution)/shard_map/ppermute | solution.py:440
  61.8 1.9 %fold.1 = bf16[8,1024,128]{2,1,0:T(8,128)(2,1)} custom-call(bf16[8,256,128]{2,1,0:T(8,128)(2,1)} %copy-done.3, bf16[8,1024,128]{2,1,0:T(8,128)(2,1)} %pack.3._), custom_call_target="tpu_custom_call", output_to_operand_aliasing={{}: (1, {})} | custom-call | flops 262144 | bytes 1048576 | tf_op jit(solution)/shard_map/fold/pallas_call | solution.py:150
  63.7 7.4 %all-to-all-start.2 = ((bf16[8,1024,128]{2,1,0:T(8,128)(2,1)}), bf16[8,1024,128]{2,1,0:T(8,128)(2,1)S(1)}, u32[]{:S(2)}, u32[]{:S(2)}) async-start(bf16[8,1024,128]{2,1,0:T(8,128)(2,1)} %fold.1), calls=%async_computation.2 | async-start | bytes 4194304 | tf_op jit(solution)/shard_map/all_to_all | solution.py:473
  71.2 16.9 %attend.5 = bf16[4,144,1024]{2,1,0:T(8,128)(2,1)} custom-call(bf16[8,256,128]{2,1,0:T(8,128)(2,1)} %copy-done.5, bf16[8,256,128]{2,1,0:T(8,128)(2,1)} %copy-done.17, bf16[8,256,128]{2,1,0:T(8,128)(2,1)} %copy-done.16, bf16[8,256,128]{2,1,0:T(8,128)(2,1)} %copy-done.15, bf16[8,512,128]{2,1,0:T(8,128)(2,1)} %slice.13.refs_4_, ...), custom_call_target="tpu_custom_call" | custom-call | flops 8589934592 | bytes 6291456 | tf_op jit(solution)/shard_map/attend/pallas_call | solution.py:307
  88.1 7.3 %all-to-all-done.2.parts_ref.refs_1_ = bf16[8,1024,128]{2,1,0:T(8,128)(2,1)S(1)} async-done(((bf16[8,1024,128]{2,1,0:T(8,128)(2,1)}), bf16[8,1024,128]{2,1,0:T(8,128)(2,1)S(1)}, u32[]{:S(2)}, u32[]{:S(2)}) %all-to-all-start.2) | async-done | bytes 2097184 | tf_op jit(solution)/shard_map/all_to_all | solution.py:473
  95.4 5.3 %all-to-all-start.3 = ((bf16[4,144,1024]{2,1,0:T(8,128)(2,1)}), bf16[4,144,1024]{2,1,0:T(8,128)(2,1)S(1)}, u32[]{:S(2)}, u32[]{:S(2)}) async-start(bf16[4,144,1024]{2,1,0:T(8,128)(2,1)} %attend.5), calls=%async_computation.3 | async-start | bytes 2359296 | tf_op jit(solution)/shard_map/all_to_all | solution.py:453
  100.7 3.6 %collective-permute-start.8 = (bf16[8,128,128]{2,1,0:T(8,128)(2,1)S(1)}, bf16[8,128,128]{2,1,0:T(8,128)(2,1)S(1)}, u32[]{:S(2)}, u32[]{:S(2)}) collective-permute-start(bf16[8,128,128]{2,1,0:T(8,128)(2,1)S(1)} %slice.15.refs_0_), channel_id=1, source_target_pairs={{0,32},{8,40},{16,48},{24,56},{32,0},{40,8},{48,16},{56,24},{64,96... | collective-permute-start | bytes 786440 | tf_op jit(solution)/shard_map/ppermute | solution.py:440
  104.3 1.2 collective-permute-start.7
  106.5 2.4 %collective-permute-start.9 = (bf16[8,256,128]{2,1,0:T(8,128)(2,1)S(1)}, bf16[8,256,128]{2,1,0:T(8,128)(2,1)}, u32[]{:S(2)}, u32[]{:S(2)}) collective-permute-start(bf16[8,256,128]{2,1,0:T(8,128)(2,1)S(1)} %slice.16.refs_3_.refs_1_), channel_id=1, source_target_pairs={{0,64},{8,72},{16,80},{24,88},{32,96},{40,104},{48,112},{56,120},{... | collective-permute-start | bytes 1572872 | tf_op jit(solution)/shard_map/ppermute | solution.py:440
  108.9 16.9 %attend.4 = (bf16[144,1024]{1,0:T(8,128)(2,1)}, bf16[144,1024]{1,0:T(8,128)(2,1)}, bf16[144,1024]{1,0:T(8,128)(2,1)}, bf16[144,1024]{1,0:T(8,128)(2,1)}) custom-call(bf16[8,256,128]{2,1,0:T(8,128)(2,1)} %copy-done.5, bf16[8,256,128]{2,1,0:T(8,128)(2,1)} %copy-done.17, bf16[8,256,128]{2,1,0:T(8,128)(2,1)} %copy-done.16, bf16[8,256,128]{2,1,0:T(8,128)(2,1)} %copy-done.15, ...), custom_call_target="tpu_custom_call" | custom-call | flops 8589934592 | bytes 6291456 | tf_op jit(solution)/shard_map/attend/pallas_call | solution.py:307
  125.8 1.3 collective-permute-done.7.refs_1_
  130.6 5.3 %project.1 = bf16[16,192,128]{2,1,0:T(8,128)(2,1)} custom-call(bf16[24,4096]{1,0:T(8,128)(2,1)} %x_ref.3, bf16[8,1024,128]{2,1,0:T(8,128)(2,1)} %copy-done, f32[1,4096]{1,0:T(1,128)} %bitcast.10, bf16[4096,384]{1,0:T(8,128)(2,1)} %key_ref.1, bf16[4096,384]{1,0:T(8,128)(2,1)} %value_ref.1, f32[1,384]{1,0:T(1,128)} %broadcast_in_dim.25.key_gain_ref), custom_call_target="tpu_custom_call" | custom-call | flops 201326592 | bytes 6291456 | tf_op jit(solution)/shard_map/project/pallas_call | solution.py:200
  135.9 5.9 %all-to-all-start.4 = ((bf16[16,192,128]{2,1,0:T(8,128)(2,1)}), bf16[16,192,128]{2,1,0:T(8,128)(2,1)S(1)}, u32[]{:S(2)}, u32[]{:S(2)}) async-start(bf16[16,192,128]{2,1,0:T(8,128)(2,1)} %project.1), calls=%async_computation.4 | async-start | bytes 1572864 | tf_op jit(solution)/shard_map/all_to_all | solution.py:556
  141.8 2.7 %collective-permute-start.11 = (bf16[144,1024]{1,0:T(8,128)(2,1)S(1)}, bf16[144,1024]{1,0:T(8,128)(2,1)S(1)}, u32[]{:S(2)}, u32[]{:S(2)}) collective-permute-start(bf16[144,1024]{1,0:T(8,128)(2,1)S(1)} %copy-done.21), channel_id=1, source_target_pairs={{0,48},{8,56},{16,0},{24,8},{32,16},{40,24},{48,32},{56,40},{64,11... | collective-permute-start | bytes 884744 | tf_op jit(solution)/shard_map/ppermute | solution.py:440
  144.6 2.3 %collective-permute-start.17 = (bf16[144,1024]{1,0:T(8,128)(2,1)S(1)}, bf16[144,1024]{1,0:T(8,128)(2,1)S(1)}, u32[]{:S(2)}, u32[]{:S(2)}) collective-permute-start(bf16[144,1024]{1,0:T(8,128)(2,1)S(1)} %copy-done.19), channel_id=1, source_target_pairs={{0,32},{8,40},{16,48},{24,56},{32,0},{40,8},{48,16},{56,24},{64,96... | collective-permute-start | bytes 884744 | tf_op jit(solution)/shard_map/ppermute | solution.py:440
  147.7 13.3 %attend.6 = (bf16[144,1024]{1,0:T(8,128)(2,1)}, bf16[144,1024]{1,0:T(8,128)(2,1)}, bf16[144,1024]{1,0:T(8,128)(2,1)}) custom-call(bf16[8,128,128]{2,1,0:T(8,128)(2,1)} %copy-done.24, bf16[8,128,128]{2,1,0:T(8,128)(2,1)} %copy-done.23, bf16[8,128,128]{2,1,0:T(8,128)(2,1)} %copy-done.22, bf16[8,256,128]{2,1,0:T(8,128)(2,1)} %copy-done.4, ...), custom_call_target="tpu_custom_call" | custom-call | flops 6442450944 | bytes 6291456 | tf_op jit(solution)/shard_map/attend/pallas_call | solution.py:307
  161.1 1.2 collective-permute-start.14
  163.2 1.8 %collective-permute-start.16 = (bf16[144,1024]{1,0:T(8,128)(2,1)}, bf16[144,1024]{1,0:T(8,128)(2,1)S(1)}, u32[]{:S(2)}, u32[]{:S(2)}) collective-permute-start(bf16[144,1024]{1,0:T(8,128)(2,1)} %get-tuple-element.74), channel_id=1, source_target_pairs={{0,32},{8,40},{16,48},{24,56},{32,0},{40,8},{48,16},{56,24},{64,96... | collective-permute-start | bytes 884744 | tf_op jit(solution)/shard_map/ppermute | solution.py:440
  165.7 5.6 %attend.7.refs_3_ = bf16[144,1024]{1,0:T(8,128)(2,1)} custom-call(bf16[8,128,128]{2,1,0:T(8,128)(2,1)} %copy-done.12, bf16[8,256,128]{2,1,0:T(8,128)(2,1)} %copy-done.4, bf16[8,256,128]{2,1,0:T(8,128)(2,1)} %copy-done.14, bf16[8,256,128]{2,1,0:T(8,128)(2,1)} %collective-permute-done.9.refs_5_.refs_3_, bf16[8,256,128]{2,1,0:T(8,128)(2,1)} %copy-done.18), custom_call_target="tpu_custom_call" | custom-call | flops 2147483648 | bytes 6291456 | tf_op jit(solution)/shard_map/attend/pallas_call | solution.py:307
  172.0 2.6 %merge.2.refs_4_ = bf16[1024,384]{1,0:T(8,128)(2,1)} custom-call(bf16[4,144,1024]{2,1,0:T(8,128)(2,1)} %copy-done.1, bf16[144,1024]{1,0:T(8,128)(2,1)} %get-tuple-element.78.refs_1_, bf16[144,1024]{1,0:T(8,128)(2,1)} %copy-done.6, bf16[144,1024]{1,0:T(8,128)(2,1)} %copy-done.7, bf16[144,1024]{1,0:T(8,128)(2,1)} %copy-done.8), custom_call_target="tpu_custom_call" | custom-call | flops 2097152 | bytes 4194304 | tf_op jit(solution)/shard_map/merge/pallas_call | solution.py:357
  174.6 4.7 %cross.1 = bf16[1024,384]{1,0:T(8,128)(2,1)} custom-call(s32[1]{0:T(128)S(6)} %copy.23.refs_0_, bf16[8,1024,128]{2,1,0:T(8,128)(2,1)} %copy-done, bf16[16,192,128]{2,1,0:T(8,128)(2,1)} %copy-done.2), custom_call_target="tpu_custom_call" | custom-call | flops 805306368 | bytes 3145728 | tf_op jit(solution)/shard_map/cross/pallas_call | solution.py:401
  180.9 2.1 %merge.3 = bf16[1024,384]{1,0:T(8,128)(2,1)} custom-call(bf16[144,1024]{1,0:T(8,128)(2,1)} %copy-done.9, bf16[144,1024]{1,0:T(8,128)(2,1)} %copy-done.10, bf16[144,1024]{1,0:T(8,128)(2,1)} %copy-done.11, bf16[144,1024]{1,0:T(8,128)(2,1)} %attend.7.refs_3_, bf16[1024,384]{1,0:T(8,128)(2,1)} %merge.2.refs_4_), custom_call_target="tpu_custom_call", output_to_operand_aliasing={{}: (4, {})} | custom-call | flops 1048576 | bytes 2097152 | tf_op jit(solution)/shard_map/merge/pallas_call | solution.py:357
  (81 shorter events, 11.7 us)
Async XLA Ops:
  4.9 25.1 %all-to-all-start = ((bf16[8,768,128]{2,1,0:T(8,128)(2,1)}), bf16[8,768,128]{2,1,0:T(8,128)(2,1)S(1)}, u32[]{:S(2)}, u32[]{:S(2)}) async-start(bf16[8,768,128]{2,1,0:T(8,128)(2,1)} %pack.2), calls=%async_computation | async-start | bytes 3145728 | tf_op jit(solution)/shard_map/all_to_all | solution.py:473
  31.1 29.3 %collective-permute-start = (bf16[8,512,128]{2,1,0:T(8,128)(2,1)}, bf16[8,512,128]{2,1,0:T(8,128)(2,1)}, u32[]{:S(2)}, u32[]{:S(2)}) collective-permute-start(bf16[8,512,128]{2,1,0:T(8,128)(2,1)} %slice.13.refs_4_), channel_id=1, source_target_pairs={{0,64},{8,72},{16,80},{24,88},{32,96},{40,104},{48,112},{56,120},{... | collective-permute-start | bytes 3145736 | tf_op jit(solution)/shard_map/ppermute | solution.py:440
  32.5 31.2 %copy-start.5 = (bf16[8,256,128]{2,1,0:T(8,128)(2,1)}, bf16[8,256,128]{2,1,0:T(8,128)(2,1)S(1)}, u32[]{:S(2)}) copy-start(bf16[8,256,128]{2,1,0:T(8,128)(2,1)S(1)} %slice.14.refs_0_) | copy-start | bytes 1572868
  32.5 16.8 %collective-permute-start.3 = (bf16[8,256,128]{2,1,0:T(8,128)(2,1)S(1)}, bf16[8,256,128]{2,1,0:T(8,128)(2,1)S(1)}, u32[]{:S(2)}, u32[]{:S(2)}) collective-permute-start(bf16[8,256,128]{2,1,0:T(8,128)(2,1)S(1)} %slice.14.refs_0_), channel_id=1, source_target_pairs={{0,32},{8,40},{16,48},{24,56},{32,0},{40,8},{48,16},{56,24},{64,96... | collective-permute-start | bytes 1572872 | tf_op jit(solution)/shard_map/ppermute | solution.py:440
  36.5 23.8 %collective-permute-start.2 = (bf16[8,256,128]{2,1,0:T(8,128)(2,1)S(1)}, bf16[8,256,128]{2,1,0:T(8,128)(2,1)S(1)}, u32[]{:S(2)}, u32[]{:S(2)}) collective-permute-start(bf16[8,256,128]{2,1,0:T(8,128)(2,1)S(1)} %slice.14.refs_0_), channel_id=1, source_target_pairs={{0,48},{8,56},{16,0},{24,8},{32,16},{40,24},{48,32},{56,40},{64,11... | collective-permute-start | bytes 1572872 | tf_op jit(solution)/shard_map/ppermute | solution.py:440
  37.2 23.1 %collective-permute-start.1 = (bf16[8,256,128]{2,1,0:T(8,128)(2,1)S(1)}, bf16[8,256,128]{2,1,0:T(8,128)(2,1)S(1)}, u32[]{:S(2)}, u32[]{:S(2)}) collective-permute-start(bf16[8,256,128]{2,1,0:T(8,128)(2,1)S(1)} %slice.14.refs_0_), channel_id=1, source_target_pairs={{0,16},{8,24},{16,32},{24,40},{32,48},{40,56},{48,0},{56,8},{64,80... | collective-permute-start | bytes 1572872 | tf_op jit(solution)/shard_map/ppermute | solution.py:440
  38.5 22.5 %all-to-all-start.1 = ((bf16[8,256,128]{2,1,0:T(8,128)(2,1)}), bf16[8,256,128]{2,1,0:T(8,128)(2,1)S(1)}, u32[]{:S(2)}, u32[]{:S(2)}) async-start(bf16[8,256,128]{2,1,0:T(8,128)(2,1)} %feed.1), calls=%async_computation.1 | async-start | bytes 1048576 | tf_op jit(solution)/shard_map/all_to_all | solution.py:473
  43.4 27.7 %collective-permute-start.4 = (bf16[8,512,128]{2,1,0:T(8,128)(2,1)}, bf16[8,512,128]{2,1,0:T(8,128)(2,1)}, u32[]{:S(2)}, u32[]{:S(2)}) collective-permute-start(bf16[8,512,128]{2,1,0:T(8,128)(2,1)} %slice.13.refs_4_), channel_id=1, source_target_pairs={{0,8},{8,0},{16,24},{24,16},{32,40},{40,32},{48,56},{56,48},{64,72... | collective-permute-start | bytes 3145736 | tf_op jit(solution)/shard_map/ppermute | solution.py:440
  49.3 21.9 %copy-start.15 = (bf16[8,256,128]{2,1,0:T(8,128)(2,1)}, bf16[8,256,128]{2,1,0:T(8,128)(2,1)S(1)}, u32[]{:S(2)}) copy-start(bf16[8,256,128]{2,1,0:T(8,128)(2,1)S(1)} %collective-permute-done.3.refs_3_) | copy-start | bytes 1572868
  60.3 10.8 %collective-permute-start.5 = (bf16[8,512,128]{2,1,0:T(8,128)(2,1)}, bf16[8,512,128]{2,1,0:T(8,128)(2,1)}, u32[]{:S(2)}, u32[]{:S(2)}) collective-permute-start(bf16[8,512,128]{2,1,0:T(8,128)(2,1)} %collective-permute-done.refs_6_), channel_id=1, source_target_pairs={{0,8},{8,0},{16,24},{24,16},{32,40},{40,32},{48,56},{56,48},{64,72... | collective-permute-start | bytes 3145736 | tf_op jit(solution)/shard_map/ppermute | solution.py:440
  63.7 31.6 %all-to-all-start.2 = ((bf16[8,1024,128]{2,1,0:T(8,128)(2,1)}), bf16[8,1024,128]{2,1,0:T(8,128)(2,1)S(1)}, u32[]{:S(2)}, u32[]{:S(2)}) async-start(bf16[8,1024,128]{2,1,0:T(8,128)(2,1)} %fold.1), calls=%async_computation.2 | async-start | bytes 4194304 | tf_op jit(solution)/shard_map/all_to_all | solution.py:473
  95.4 30.4 %copy-start = (bf16[8,1024,128]{2,1,0:T(8,128)(2,1)}, bf16[8,1024,128]{2,1,0:T(8,128)(2,1)S(1)}, u32[]{:S(2)}) copy-start(bf16[8,1024,128]{2,1,0:T(8,128)(2,1)S(1)} %all-to-all-done.2.parts_ref.refs_1_) | copy-start | bytes 6291460
  95.4 34.4 %all-to-all-start.3 = ((bf16[4,144,1024]{2,1,0:T(8,128)(2,1)}), bf16[4,144,1024]{2,1,0:T(8,128)(2,1)S(1)}, u32[]{:S(2)}, u32[]{:S(2)}) async-start(bf16[4,144,1024]{2,1,0:T(8,128)(2,1)} %attend.5), calls=%async_computation.3 | async-start | bytes 2359296 | tf_op jit(solution)/shard_map/all_to_all | solution.py:453
  100.7 25.1 %copy-start.12 = (bf16[8,128,128]{2,1,0:T(8,128)(2,1)}, bf16[8,128,128]{2,1,0:T(8,128)(2,1)S(1)}, u32[]{:S(2)}) copy-start(bf16[8,128,128]{2,1,0:T(8,128)(2,1)S(1)} %slice.15.refs_0_) | copy-start | bytes 786436
  100.7 25.1 %collective-permute-start.8 = (bf16[8,128,128]{2,1,0:T(8,128)(2,1)S(1)}, bf16[8,128,128]{2,1,0:T(8,128)(2,1)S(1)}, u32[]{:S(2)}, u32[]{:S(2)}) collective-permute-start(bf16[8,128,128]{2,1,0:T(8,128)(2,1)S(1)} %slice.15.refs_0_), channel_id=1, source_target_pairs={{0,32},{8,40},{16,48},{24,56},{32,0},{40,8},{48,16},{56,24},{64,96... | collective-permute-start | bytes 786440 | tf_op jit(solution)/shard_map/ppermute | solution.py:440
  104.3 22.8 %collective-permute-start.7 = (bf16[8,128,128]{2,1,0:T(8,128)(2,1)S(1)}, bf16[8,128,128]{2,1,0:T(8,128)(2,1)S(1)}, u32[]{:S(2)}, u32[]{:S(2)}) collective-permute-start(bf16[8,128,128]{2,1,0:T(8,128)(2,1)S(1)} %slice.15.refs_0_), channel_id=1, source_target_pairs={{0,48},{8,56},{16,0},{24,8},{32,16},{40,24},{48,32},{56,40},{64,11... | collective-permute-start | bytes 786440 | tf_op jit(solution)/shard_map/ppermute | solution.py:440
  105.5 22.8 %collective-permute-start.6 = (bf16[8,128,128]{2,1,0:T(8,128)(2,1)S(1)}, bf16[8,128,128]{2,1,0:T(8,128)(2,1)S(1)}, u32[]{:S(2)}, u32[]{:S(2)}) collective-permute-start(bf16[8,128,128]{2,1,0:T(8,128)(2,1)S(1)} %slice.15.refs_0_), channel_id=1, source_target_pairs={{0,16},{8,24},{16,32},{24,40},{32,48},{40,56},{48,0},{56,8},{64,80... | collective-permute-start | bytes 786440 | tf_op jit(solution)/shard_map/ppermute | solution.py:440
  106.4 19.4 %copy-start.4 = (bf16[8,256,128]{2,1,0:T(8,128)(2,1)}, bf16[8,256,128]{2,1,0:T(8,128)(2,1)S(1)}, u32[]{:S(2)}) copy-start(bf16[8,256,128]{2,1,0:T(8,128)(2,1)S(1)} %slice.16.refs_3_.refs_1_) | copy-start | bytes 1572868
  106.4 23.5 %copy-start.13 = (f32[384]{0:T(512)S(1)}, f32[384]{0:T(512)}, u32[]{:S(2)}) copy-start(f32[384]{0:T(512)} %param.26) | copy-start | bytes 4612
  106.4 21.9 %collective-permute-start.10 = (bf16[8,256,128]{2,1,0:T(8,128)(2,1)S(1)}, bf16[8,256,128]{2,1,0:T(8,128)(2,1)S(1)}, u32[]{:S(2)}, u32[]{:S(2)}) collective-permute-start(bf16[8,256,128]{2,1,0:T(8,128)(2,1)S(1)} %slice.16.refs_3_.refs_1_), channel_id=1, source_target_pairs={{0,8},{8,0},{16,24},{24,16},{32,40},{40,32},{48,56},{56,48},{64,72... | collective-permute-start | bytes 1572872 | tf_op jit(solution)/shard_map/ppermute | solution.py:440
  106.5 23.3 %collective-permute-start.9 = (bf16[8,256,128]{2,1,0:T(8,128)(2,1)S(1)}, bf16[8,256,128]{2,1,0:T(8,128)(2,1)}, u32[]{:S(2)}, u32[]{:S(2)}) collective-permute-start(bf16[8,256,128]{2,1,0:T(8,128)(2,1)S(1)} %slice.16.refs_3_.refs_1_), channel_id=1, source_target_pairs={{0,64},{8,72},{16,80},{24,88},{32,96},{40,104},{48,112},{56,120},{... | collective-permute-start | bytes 1572872 | tf_op jit(solution)/shard_map/ppermute | solution.py:440
  129.8 17.1 %collective-permute-start.13 = (bf16[8,256,128]{2,1,0:T(8,128)(2,1)}, bf16[8,256,128]{2,1,0:T(8,128)(2,1)S(1)}, u32[]{:S(2)}, u32[]{:S(2)}) collective-permute-start(bf16[8,256,128]{2,1,0:T(8,128)(2,1)} %collective-permute-done.9.refs_5_.refs_3_), channel_id=1, source_target_pairs={{0,8},{8,0},{16,24},{24,16},{32,40},{40,32},{48,56},{56,48},{64,72... | collective-permute-start | bytes 1572872 | tf_op jit(solution)/shard_map/ppermute | solution.py:440
  130.6 11.3 %copy-start.21 = (bf16[144,1024]{1,0:T(8,128)(2,1)S(1)}, bf16[144,1024]{1,0:T(8,128)(2,1)}, u32[]{:S(2)}) copy-start(bf16[144,1024]{1,0:T(8,128)(2,1)} %get-tuple-element.60) | copy-start | bytes 884740
  130.6 14.0 %copy-start.20 = (bf16[144,1024]{1,0:T(8,128)(2,1)S(1)}, bf16[144,1024]{1,0:T(8,128)(2,1)}, u32[]{:S(2)}) copy-start(bf16[144,1024]{1,0:T(8,128)(2,1)} %get-tuple-element.61) | copy-start | bytes 884740
  130.6 14.0 %copy-start.19 = (bf16[144,1024]{1,0:T(8,128)(2,1)S(1)}, bf16[144,1024]{1,0:T(8,128)(2,1)}, u32[]{:S(2)}) copy-start(bf16[144,1024]{1,0:T(8,128)(2,1)} %get-tuple-element.81) | copy-start | bytes 884740
  135.9 25.1 %all-to-all-start.4 = ((bf16[16,192,128]{2,1,0:T(8,128)(2,1)}), bf16[16,192,128]{2,1,0:T(8,128)(2,1)S(1)}, u32[]{:S(2)}, u32[]{:S(2)}) async-start(bf16[16,192,128]{2,1,0:T(8,128)(2,1)} %project.1), calls=%async_computation.4 | async-start | bytes 1572864 | tf_op jit(solution)/shard_map/all_to_all | solution.py:556
  141.8 19.2 %collective-permute-start.11 = (bf16[144,1024]{1,0:T(8,128)(2,1)S(1)}, bf16[144,1024]{1,0:T(8,128)(2,1)S(1)}, u32[]{:S(2)}, u32[]{:S(2)}) collective-permute-start(bf16[144,1024]{1,0:T(8,128)(2,1)S(1)} %copy-done.21), channel_id=1, source_target_pairs={{0,48},{8,56},{16,0},{24,8},{32,16},{40,24},{48,32},{56,40},{64,11... | collective-permute-start | bytes 884744 | tf_op jit(solution)/shard_map/ppermute | solution.py:440
  144.6 16.5 %collective-permute-start.12 = (bf16[144,1024]{1,0:T(8,128)(2,1)S(1)}, bf16[144,1024]{1,0:T(8,128)(2,1)S(1)}, u32[]{:S(2)}, u32[]{:S(2)}) collective-permute-start(bf16[144,1024]{1,0:T(8,128)(2,1)S(1)} %copy-done.20), channel_id=1, source_target_pairs={{0,16},{8,24},{16,32},{24,40},{32,48},{40,56},{48,0},{56,8},{64,80... | collective-permute-start | bytes 884744 | tf_op jit(solution)/shard_map/ppermute | solution.py:440
  144.6 26.7 %collective-permute-start.17 = (bf16[144,1024]{1,0:T(8,128)(2,1)S(1)}, bf16[144,1024]{1,0:T(8,128)(2,1)S(1)}, u32[]{:S(2)}, u32[]{:S(2)}) collective-permute-start(bf16[144,1024]{1,0:T(8,128)(2,1)S(1)} %copy-done.19), channel_id=1, source_target_pairs={{0,32},{8,40},{16,48},{24,56},{32,0},{40,8},{48,16},{56,24},{64,96... | collective-permute-start | bytes 884744 | tf_op jit(solution)/shard_map/ppermute | solution.py:440
  161.1 18.3 %collective-permute-start.14 = (bf16[144,1024]{1,0:T(8,128)(2,1)}, bf16[144,1024]{1,0:T(8,128)(2,1)S(1)}, u32[]{:S(2)}, u32[]{:S(2)}) collective-permute-start(bf16[144,1024]{1,0:T(8,128)(2,1)} %get-tuple-element.72), channel_id=1, source_target_pairs={{0,48},{8,56},{16,0},{24,8},{32,16},{40,24},{48,32},{56,40},{64,11... | collective-permute-start | bytes 884744 | tf_op jit(solution)/shard_map/ppermute | solution.py:440
  162.3 17.0 %collective-permute-start.15 = (bf16[144,1024]{1,0:T(8,128)(2,1)}, bf16[144,1024]{1,0:T(8,128)(2,1)S(1)}, u32[]{:S(2)}, u32[]{:S(2)}) collective-permute-start(bf16[144,1024]{1,0:T(8,128)(2,1)} %get-tuple-element.73), channel_id=1, source_target_pairs={{0,16},{8,24},{16,32},{24,40},{32,48},{40,56},{48,0},{56,8},{64,80... | collective-permute-start | bytes 884744 | tf_op jit(solution)/shard_map/ppermute | solution.py:440
  163.2 16.6 %collective-permute-start.16 = (bf16[144,1024]{1,0:T(8,128)(2,1)}, bf16[144,1024]{1,0:T(8,128)(2,1)S(1)}, u32[]{:S(2)}, u32[]{:S(2)}) collective-permute-start(bf16[144,1024]{1,0:T(8,128)(2,1)} %get-tuple-element.74), channel_id=1, source_target_pairs={{0,32},{8,40},{16,48},{24,56},{32,0},{40,8},{48,16},{56,24},{64,96... | collective-permute-start | bytes 884744 | tf_op jit(solution)/shard_map/ppermute | solution.py:440
  (16 other events, 53.5 us)

commit v5 on v4

--- a/solution.py
+++ b/solution.py
@@ -342,7 +342,7 @@
     arrays = [array for group in results for array in group]
     sizes = [len(group) for group in results]
     count = arrays[0].shape[-1]
-    step = 512
+    step = 1024
     specs = []
     for array in arrays:
         if array.ndim == 2:
@@ -369,22 +369,22 @@
     )(*arrays)
 
 
-def cross_kernel(start, per, length_ref, c_ref, kv_ref, out_ref):
+def cross_kernel(per, length_ref, *refs):
+    c_refs, (kv_ref, out_ref) = refs[:-2], refs[-2:]
     live = length_ref[0]
-    blocks = c_ref.shape[0]
+    blocks = c_refs[0].shape[0]
     sources = kv_ref.shape[0]
     count = sources * SLOT
     tile = blocks * HEAD
     row = lax.broadcasted_iota(jnp.int32, (count, tile), 0)
     source, slot = row // SLOT, row % SLOT
     alive = (slot < per) & (source * per + slot < live)
-    for h in range(kv_ref.shape[1] // (2 * SLOT)):
+    for h, c_ref in enumerate(c_refs):
         at = 2 * h * SLOT
         keys = kv_ref[:, at : at + SLOT, :].reshape(count, HEAD)
         values = kv_ref[:, at + SLOT : at + 2 * SLOT, :].reshape(count, HEAD)
         values = values.astype(jnp.float32).T.astype(jnp.bfloat16)
-        first = start + h * HEAD
-        q = c_ref[:, first : first + HEAD, :].reshape(tile, HEAD)
+        q = c_ref[...].reshape(tile, HEAD)
         s = lax.dot_general(
             keys, q, (((1,), (1,)), ((), ())), preferred_element_type=jnp.float32
         )
@@ -398,12 +398,16 @@
     blocks, depth, _ = c.shape
     step = 4
     heads = kv.shape[1] // (2 * SLOT)
-    return pl.pallas_call(
-        lambda *refs: cross_kernel(start, per, *refs),
+
+    def part(row):
+        return pl.BlockSpec((step, HEAD, HEAD), lambda i: (i, row, 0))
+
+    return pl.pallas_call(
+        lambda *refs: cross_kernel(per, *refs),
         grid=(blocks // step,),
         in_specs=[
             pl.BlockSpec(memory_space=pltpu.SMEM),
-            pl.BlockSpec((step, depth, HEAD), lambda i: (i, 0, 0)),
+            *[part(start // HEAD + h) for h in range(heads)],
             pl.BlockSpec(kv.shape, lambda i: (0, 0, 0)),
         ],
         out_specs=pl.BlockSpec((step * HEAD, heads * HEAD), lambda i: (i, 0)),
@@ -415,7 +419,7 @@
             transcendentals=heads * blocks * HEAD * kv.shape[0] * SLOT,
         ),
         name="cross",
-    )(lengths, c, kv)
+    )(lengths, *[c] * heads, kv)
 
 
 def spot(hi, z, core):

time: 184 us -> 184 us (level)
  no operation moved by 1% of the time
where the time goes in v5:
time: 184 us; the launch traced here: 183 us
  Pallas kernels  87.9 us (48%)
  starting transfers between devices  54 us (29%)
  waiting for transfers between devices  32.7 us (18%)
  local copies, waits for them, and re-layouts  6.97 us (4%)
    pallas_call x4, Pallas kernels, attend(): pl.pallas_call(lambda *refs: attend_kernel(views, nq, nkv, ring, *refs),...  52.7 us
    ppermute x18, starting transfers between devices, send(): return lax.ppermute(array, 'wide', pairs)  24.7 us
    ppermute x18, waiting for transfers between devices, send(): return lax.ppermute(array, 'wide', pairs)  19.7 us
    all_to_all x3, starting transfers between devices, trade(): lax.all_to_all(array, 'narrow', split_axis=0, concat_axis=0, tiled=True)  18.1 us
    all_to_all x3, waiting for transfers between devices, trade(): lax.all_to_all(array, 'narrow', split_axis=0, concat_axis=0, tiled=True)  13 us
    pallas_call x1, Pallas kernels, feed(): pl.pallas_call(feed_kernel, grid=(hidden // tile,), in_specs=[pl.BlockSpe...  9.2 us
    pallas_call x2, Pallas kernels, pack(): pl.pallas_call(lambda *refs: pack_kernel(heads, plan, *refs), in_specs=[w...  9.19 us
    all_to_all x1, starting transfers between devices, body(): lax.all_to_all(prompt_pair, 'wide', split_axis=0, concat_axis=0, tiled=True)  5.9 us
  transfers between devices with their start and end apart: 23, of which 8 were waited for; matrix products, arithmetic and copies ran while one was open for 0% of the time, Pallas kernels for 44%

profile of v5, /device:TPU:14, one launch (start us, length us, event | category | flops | bytes accessed | tf_op | source)
XLA Modules:
  0.0 183.2 jit_solution(16608821914972752963)
XLA Ops:
  0.6 4.3 %pack.2 = bf16[8,768,128]{2,1,0:T(8,128)(2,1)} custom-call(bf16[128,3072]{1,0:T(8,128)(2,1)} %refs_0_.4, bf16[128,3072]{1,0:T(8,128)(2,1)} %refs_1_.3, bf16[128,3072]{1,0:T(8,128)(2,1)} %refs_2_.3, f32[1,3072]{1,0:T(1,128)} %bitcast.5, f32[1,3072]{1,0:T(1,128)} %bitcast.7), custom_call_target="tpu_custom_call" | custom-call | flops 3145728 | bytes 6291456 | tf_op jit(solution)/shard_map/pack/pallas_call | solution.py:56
  4.9 5.8 %all-to-all-start = ((bf16[8,768,128]{2,1,0:T(8,128)(2,1)}), bf16[8,768,128]{2,1,0:T(8,128)(2,1)S(1)}, u32[]{:S(2)}, u32[]{:S(2)}) async-start(bf16[8,768,128]{2,1,0:T(8,128)(2,1)} %pack.2), calls=%async_computation | async-start | bytes 3145728 | tf_op jit(solution)/shard_map/all_to_all | solution.py:477
  10.8 4.9 %pack.3._ = bf16[8,1024,128]{2,1,0:T(8,128)(2,1)} custom-call(bf16[128,3072]{1,0:T(8,128)(2,1)} %refs_0_.4, bf16[128,3072]{1,0:T(8,128)(2,1)} %refs_1_.3, bf16[128,3072]{1,0:T(8,128)(2,1)} %refs_2_.3, f32[1,3072]{1,0:T(1,128)} %bitcast.6, f32[1,3072]{1,0:T(1,128)} %bitcast.8, bf16[128,3072]{1,0:T(8,128)(2,1)} %refs_5_.1, f32[1,3072]{1,0:T(1,128)} %bitcast.11), custom_call_target="tpu_custom_call" | custom-call | flops 3145728 | bytes 6291456 | tf_op jit(solution)/shard_map/pack/pallas_call | solution.py:56
  15.6 9.2 %feed.1 = bf16[8,256,128]{2,1,0:T(8,128)(2,1)} custom-call(bf16[24,4096]{1,0:T(8,128)(2,1)} %x_ref.3, f32[1,4096]{1,0:T(1,128)} %bitcast.9, bf16[4096,640]{1,0:T(8,128)(2,1)} %gate_ref.1, bf16[4096,640]{1,0:T(8,128)(2,1)} %up_ref.1, bf16[640,4096]{1,0:T(8,128)(2,1)} %down_ref.1), custom_call_target="tpu_custom_call" | custom-call | flops 503316480 | bytes 15728640 | tf_op jit(solution)/shard_map/feed/pallas_call | solution.py:109
  24.8 5.2 %all-to-all-done = bf16[8,768,128]{2,1,0:T(8,128)(2,1)S(1)} async-done(((bf16[8,768,128]{2,1,0:T(8,128)(2,1)}), bf16[8,768,128]{2,1,0:T(8,128)(2,1)S(1)}, u32[]{:S(2)}, u32[]{:S(2)}) %all-to-all-start) | async-done | bytes 1572896 | tf_op jit(solution)/shard_map/all_to_all | solution.py:477
  31.1 1.4 collective-permute-start
  32.5 4.0 %collective-permute-start.3 = (bf16[8,256,128]{2,1,0:T(8,128)(2,1)S(1)}, bf16[8,256,128]{2,1,0:T(8,128)(2,1)S(1)}, u32[]{:S(2)}, u32[]{:S(2)}) collective-permute-start(bf16[8,256,128]{2,1,0:T(8,128)(2,1)S(1)} %slice.14.refs_0_), channel_id=1, source_target_pairs={{0,32},{8,40},{16,48},{24,56},{32,0},{40,8},{48,16},{56,24},{64,96... | collective-permute-start | bytes 1572872 | tf_op jit(solution)/shard_map/ppermute | solution.py:444
  37.2 1.3 collective-permute-start.1
  38.5 4.9 %all-to-all-start.1 = ((bf16[8,256,128]{2,1,0:T(8,128)(2,1)}), bf16[8,256,128]{2,1,0:T(8,128)(2,1)S(1)}, u32[]{:S(2)}, u32[]{:S(2)}) async-start(bf16[8,256,128]{2,1,0:T(8,128)(2,1)} %feed.1), calls=%async_computation.1 | async-start | bytes 1048576 | tf_op jit(solution)/shard_map/all_to_all | solution.py:477
  43.4 5.9 %collective-permute-done.3.refs_3_ = bf16[8,256,128]{2,1,0:T(8,128)(2,1)S(1)} collective-permute-done((bf16[8,256,128]{2,1,0:T(8,128)(2,1)S(1)}, bf16[8,256,128]{2,1,0:T(8,128)(2,1)S(1)}, u32[]{:S(2)}, u32[]{:S(2)}) %collective-permute-start.3) | collective-permute-done | bytes 524320 | tf_op jit(solution)/shard_map/ppermute | solution.py:444
  49.3 11.0 %collective-permute-done.2.refs_2_ = bf16[8,256,128]{2,1,0:T(8,128)(2,1)S(1)} collective-permute-done((bf16[8,256,128]{2,1,0:T(8,128)(2,1)S(1)}, bf16[8,256,128]{2,1,0:T(8,128)(2,1)S(1)}, u32[]{:S(2)}, u32[]{:S(2)}) %collective-permute-start.2) | collective-permute-done | bytes 524320 | tf_op jit(solution)/shard_map/ppermute | solution.py:444
  61.8 1.9 %fold.1 = bf16[8,1024,128]{2,1,0:T(8,128)(2,1)} custom-call(bf16[8,256,128]{2,1,0:T(8,128)(2,1)} %copy-done.3, bf16[8,1024,128]{2,1,0:T(8,128)(2,1)} %pack.3._), custom_call_target="tpu_custom_call", output_to_operand_aliasing={{}: (1, {})} | custom-call | flops 262144 | bytes 1048576 | tf_op jit(solution)/shard_map/fold/pallas_call | solution.py:150
  63.7 7.4 %all-to-all-start.2 = ((bf16[8,1024,128]{2,1,0:T(8,128)(2,1)}), bf16[8,1024,128]{2,1,0:T(8,128)(2,1)S(1)}, u32[]{:S(2)}, u32[]{:S(2)}) async-start(bf16[8,1024,128]{2,1,0:T(8,128)(2,1)} %fold.1), calls=%async_computation.2 | async-start | bytes 4194304 | tf_op jit(solution)/shard_map/all_to_all | solution.py:477
  71.2 16.9 %attend.5 = bf16[4,144,1024]{2,1,0:T(8,128)(2,1)} custom-call(bf16[8,256,128]{2,1,0:T(8,128)(2,1)} %copy-done.5, bf16[8,256,128]{2,1,0:T(8,128)(2,1)} %copy-done.17, bf16[8,256,128]{2,1,0:T(8,128)(2,1)} %copy-done.16, bf16[8,256,128]{2,1,0:T(8,128)(2,1)} %copy-done.15, bf16[8,512,128]{2,1,0:T(8,128)(2,1)} %slice.13.refs_4_, ...), custom_call_target="tpu_custom_call" | custom-call | flops 8589934592 | bytes 6291456 | tf_op jit(solution)/shard_map/attend/pallas_call | solution.py:307
  88.1 7.3 %all-to-all-done.2.parts_ref.refs_1_.refs_2_.refs_3_ = bf16[8,1024,128]{2,1,0:T(8,128)(2,1)S(1)} async-done(((bf16[8,1024,128]{2,1,0:T(8,128)(2,1)}), bf16[8,1024,128]{2,1,0:T(8,128)(2,1)S(1)}, u32[]{:S(2)}, u32[]{:S(2)}) %all-to-all-start.2) | async-done | bytes 2097184 | tf_op jit(solution)/shard_map/all_to_all | solution.py:477
  95.4 5.3 %all-to-all-start.3 = ((bf16[4,144,1024]{2,1,0:T(8,128)(2,1)}), bf16[4,144,1024]{2,1,0:T(8,128)(2,1)S(1)}, u32[]{:S(2)}, u32[]{:S(2)}) async-start(bf16[4,144,1024]{2,1,0:T(8,128)(2,1)} %attend.5), calls=%async_computation.3 | async-start | bytes 2359296 | tf_op jit(solution)/shard_map/all_to_all | solution.py:457
  100.7 3.6 %collective-permute-start.8 = (bf16[8,128,128]{2,1,0:T(8,128)(2,1)S(1)}, bf16[8,128,128]{2,1,0:T(8,128)(2,1)S(1)}, u32[]{:S(2)}, u32[]{:S(2)}) collective-permute-start(bf16[8,128,128]{2,1,0:T(8,128)(2,1)S(1)} %slice.15.refs_0_), channel_id=1, source_target_pairs={{0,32},{8,40},{16,48},{24,56},{32,0},{40,8},{48,16},{56,24},{64,96... | collective-permute-start | bytes 786440 | tf_op jit(solution)/shard_map/ppermute | solution.py:444
  104.3 1.2 collective-permute-start.7
  106.5 2.4 %collective-permute-start.9 = (bf16[8,256,128]{2,1,0:T(8,128)(2,1)S(1)}, bf16[8,256,128]{2,1,0:T(8,128)(2,1)}, u32[]{:S(2)}, u32[]{:S(2)}) collective-permute-start(bf16[8,256,128]{2,1,0:T(8,128)(2,1)S(1)} %slice.16.refs_3_.refs_1_), channel_id=1, source_target_pairs={{0,64},{8,72},{16,80},{24,88},{32,96},{40,104},{48,112},{56,120},{... | collective-permute-start | bytes 1572872 | tf_op jit(solution)/shard_map/ppermute | solution.py:444
  108.9 16.9 %attend.4 = (bf16[144,1024]{1,0:T(8,128)(2,1)}, bf16[144,1024]{1,0:T(8,128)(2,1)}, bf16[144,1024]{1,0:T(8,128)(2,1)}, bf16[144,1024]{1,0:T(8,128)(2,1)}) custom-call(bf16[8,256,128]{2,1,0:T(8,128)(2,1)} %copy-done.5, bf16[8,256,128]{2,1,0:T(8,128)(2,1)} %copy-done.17, bf16[8,256,128]{2,1,0:T(8,128)(2,1)} %copy-done.16, bf16[8,256,128]{2,1,0:T(8,128)(2,1)} %copy-done.15, ...), custom_call_target="tpu_custom_call" | custom-call | flops 8589934592 | bytes 6291456 | tf_op jit(solution)/shard_map/attend/pallas_call | solution.py:307
  125.8 1.3 collective-permute-done.7.refs_1_
  130.6 5.3 %project.1 = bf16[16,192,128]{2,1,0:T(8,128)(2,1)} custom-call(bf16[24,4096]{1,0:T(8,128)(2,1)} %x_ref.3, bf16[8,1024,128]{2,1,0:T(8,128)(2,1)} %copy-done, f32[1,4096]{1,0:T(1,128)} %bitcast.10, bf16[4096,384]{1,0:T(8,128)(2,1)} %key_ref.1, bf16[4096,384]{1,0:T(8,128)(2,1)} %value_ref.1, f32[1,384]{1,0:T(1,128)} %broadcast_in_dim.25.key_gain_ref), custom_call_target="tpu_custom_call" | custom-call | flops 201326592 | bytes 6291456 | tf_op jit(solution)/shard_map/project/pallas_call | solution.py:200
  135.9 5.9 %all-to-all-start.4 = ((bf16[16,192,128]{2,1,0:T(8,128)(2,1)}), bf16[16,192,128]{2,1,0:T(8,128)(2,1)S(1)}, u32[]{:S(2)}, u32[]{:S(2)}) async-start(bf16[16,192,128]{2,1,0:T(8,128)(2,1)} %project.1), calls=%async_computation.4 | async-start | bytes 1572864 | tf_op jit(solution)/shard_map/all_to_all | solution.py:560
  141.8 2.7 %collective-permute-start.11 = (bf16[144,1024]{1,0:T(8,128)(2,1)S(1)}, bf16[144,1024]{1,0:T(8,128)(2,1)S(1)}, u32[]{:S(2)}, u32[]{:S(2)}) collective-permute-start(bf16[144,1024]{1,0:T(8,128)(2,1)S(1)} %copy-done.21), channel_id=1, source_target_pairs={{0,48},{8,56},{16,0},{24,8},{32,16},{40,24},{48,32},{56,40},{64,11... | collective-permute-start | bytes 884744 | tf_op jit(solution)/shard_map/ppermute | solution.py:444
  144.6 2.3 %collective-permute-start.17 = (bf16[144,1024]{1,0:T(8,128)(2,1)S(1)}, bf16[144,1024]{1,0:T(8,128)(2,1)S(1)}, u32[]{:S(2)}, u32[]{:S(2)}) collective-permute-start(bf16[144,1024]{1,0:T(8,128)(2,1)S(1)} %copy-done.19), channel_id=1, source_target_pairs={{0,32},{8,40},{16,48},{24,56},{32,0},{40,8},{48,16},{56,24},{64,96... | collective-permute-start | bytes 884744 | tf_op jit(solution)/shard_map/ppermute | solution.py:444
  147.7 13.3 %attend.6 = (bf16[144,1024]{1,0:T(8,128)(2,1)}, bf16[144,1024]{1,0:T(8,128)(2,1)}, bf16[144,1024]{1,0:T(8,128)(2,1)}) custom-call(bf16[8,128,128]{2,1,0:T(8,128)(2,1)} %copy-done.24, bf16[8,128,128]{2,1,0:T(8,128)(2,1)} %copy-done.23, bf16[8,128,128]{2,1,0:T(8,128)(2,1)} %copy-done.22, bf16[8,256,128]{2,1,0:T(8,128)(2,1)} %copy-done.4, ...), custom_call_target="tpu_custom_call" | custom-call | flops 6442450944 | bytes 6291456 | tf_op jit(solution)/shard_map/attend/pallas_call | solution.py:307
  161.1 1.2 collective-permute-start.14
  163.2 1.8 collective-permute-start.16
  165.7 5.6 %attend.7.refs_3_ = bf16[144,1024]{1,0:T(8,128)(2,1)} custom-call(bf16[8,128,128]{2,1,0:T(8,128)(2,1)} %copy-done.12, bf16[8,256,128]{2,1,0:T(8,128)(2,1)} %copy-done.4, bf16[8,256,128]{2,1,0:T(8,128)(2,1)} %copy-done.14, bf16[8,256,128]{2,1,0:T(8,128)(2,1)} %collective-permute-done.9.refs_5_.refs_3_, bf16[8,256,128]{2,1,0:T(8,128)(2,1)} %copy-done.18), custom_call_target="tpu_custom_call" | custom-call | flops 2147483648 | bytes 6291456 | tf_op jit(solution)/shard_map/attend/pallas_call | solution.py:307
  172.0 2.8 %merge.2.refs_4_ = bf16[1024,384]{1,0:T(8,128)(2,1)} custom-call(bf16[4,144,1024]{2,1,0:T(8,128)(2,1)} %copy-done.1, bf16[144,1024]{1,0:T(8,128)(2,1)} %get-tuple-element.78.refs_1_, bf16[144,1024]{1,0:T(8,128)(2,1)} %copy-done.6, bf16[144,1024]{1,0:T(8,128)(2,1)} %copy-done.7, bf16[144,1024]{1,0:T(8,128)(2,1)} %copy-done.8), custom_call_target="tpu_custom_call" | custom-call | flops 2097152 | bytes 4194304 | tf_op jit(solution)/shard_map/merge/pallas_call | solution.py:357
  174.9 4.6 %cross.1 = bf16[1024,384]{1,0:T(8,128)(2,1)} custom-call(s32[1]{0:T(128)S(6)} %copy.23.refs_0_, bf16[8,1024,128]{2,1,0:T(8,128)(2,1)} %copy-done, bf16[8,1024,128]{2,1,0:T(8,128)(2,1)} %copy-done, bf16[8,1024,128]{2,1,0:T(8,128)(2,1)} %copy-done, bf16[16,192,128]{2,1,0:T(8,128)(2,1)} %copy-done.2), custom_call_target="tpu_custom_call" | custom-call | flops 805306368 | bytes 3145728 | tf_op jit(solution)/shard_map/cross/pallas_call | solution.py:405
  181.0 2.2 %merge.3 = bf16[1024,384]{1,0:T(8,128)(2,1)} custom-call(bf16[144,1024]{1,0:T(8,128)(2,1)} %copy-done.9, bf16[144,1024]{1,0:T(8,128)(2,1)} %copy-done.10, bf16[144,1024]{1,0:T(8,128)(2,1)} %copy-done.11, bf16[144,1024]{1,0:T(8,128)(2,1)} %attend.7.refs_3_, bf16[1024,384]{1,0:T(8,128)(2,1)} %merge.2.refs_4_), custom_call_target="tpu_custom_call", output_to_operand_aliasing={{}: (4, {})} | custom-call | flops 1048576 | bytes 2097152 | tf_op jit(solution)/shard_map/merge/pallas_call | solution.py:357
  (81 shorter events, 11.7 us)
Async XLA Ops:
  4.9 25.1 %all-to-all-start = ((bf16[8,768,128]{2,1,0:T(8,128)(2,1)}), bf16[8,768,128]{2,1,0:T(8,128)(2,1)S(1)}, u32[]{:S(2)}, u32[]{:S(2)}) async-start(bf16[8,768,128]{2,1,0:T(8,128)(2,1)} %pack.2), calls=%async_computation | async-start | bytes 3145728 | tf_op jit(solution)/shard_map/all_to_all | solution.py:477
  31.1 29.3 %collective-permute-start = (bf16[8,512,128]{2,1,0:T(8,128)(2,1)}, bf16[8,512,128]{2,1,0:T(8,128)(2,1)}, u32[]{:S(2)}, u32[]{:S(2)}) collective-permute-start(bf16[8,512,128]{2,1,0:T(8,128)(2,1)} %slice.13.refs_4_), channel_id=1, source_target_pairs={{0,64},{8,72},{16,80},{24,88},{32,96},{40,104},{48,112},{56,120},{... | collective-permute-start | bytes 3145736 | tf_op jit(solution)/shard_map/ppermute | solution.py:444
  32.5 31.2 %copy-start.5 = (bf16[8,256,128]{2,1,0:T(8,128)(2,1)}, bf16[8,256,128]{2,1,0:T(8,128)(2,1)S(1)}, u32[]{:S(2)}) copy-start(bf16[8,256,128]{2,1,0:T(8,128)(2,1)S(1)} %slice.14.refs_0_) | copy-start | bytes 1572868
  32.5 16.8 %collective-permute-start.3 = (bf16[8,256,128]{2,1,0:T(8,128)(2,1)S(1)}, bf16[8,256,128]{2,1,0:T(8,128)(2,1)S(1)}, u32[]{:S(2)}, u32[]{:S(2)}) collective-permute-start(bf16[8,256,128]{2,1,0:T(8,128)(2,1)S(1)} %slice.14.refs_0_), channel_id=1, source_target_pairs={{0,32},{8,40},{16,48},{24,56},{32,0},{40,8},{48,16},{56,24},{64,96... | collective-permute-start | bytes 1572872 | tf_op jit(solution)/shard_map/ppermute | solution.py:444
  36.5 23.8 %collective-permute-start.2 = (bf16[8,256,128]{2,1,0:T(8,128)(2,1)S(1)}, bf16[8,256,128]{2,1,0:T(8,128)(2,1)S(1)}, u32[]{:S(2)}, u32[]{:S(2)}) collective-permute-start(bf16[8,256,128]{2,1,0:T(8,128)(2,1)S(1)} %slice.14.refs_0_), channel_id=1, source_target_pairs={{0,48},{8,56},{16,0},{24,8},{32,16},{40,24},{48,32},{56,40},{64,11... | collective-permute-start | bytes 1572872 | tf_op jit(solution)/shard_map/ppermute | solution.py:444
  37.2 23.1 %collective-permute-start.1 = (bf16[8,256,128]{2,1,0:T(8,128)(2,1)S(1)}, bf16[8,256,128]{2,1,0:T(8,128)(2,1)S(1)}, u32[]{:S(2)}, u32[]{:S(2)}) collective-permute-start(bf16[8,256,128]{2,1,0:T(8,128)(2,1)S(1)} %slice.14.refs_0_), channel_id=1, source_target_pairs={{0,16},{8,24},{16,32},{24,40},{32,48},{40,56},{48,0},{56,8},{64,80... | collective-permute-start | bytes 1572872 | tf_op jit(solution)/shard_map/ppermute | solution.py:444
  38.5 22.5 %all-to-all-start.1 = ((bf16[8,256,128]{2,1,0:T(8,128)(2,1)}), bf16[8,256,128]{2,1,0:T(8,128)(2,1)S(1)}, u32[]{:S(2)}, u32[]{:S(2)}) async-start(bf16[8,256,128]{2,1,0:T(8,128)(2,1)} %feed.1), calls=%async_computation.1 | async-start | bytes 1048576 | tf_op jit(solution)/shard_map/all_to_all | solution.py:477
  43.4 27.7 %collective-permute-start.4 = (bf16[8,512,128]{2,1,0:T(8,128)(2,1)}, bf16[8,512,128]{2,1,0:T(8,128)(2,1)}, u32[]{:S(2)}, u32[]{:S(2)}) collective-permute-start(bf16[8,512,128]{2,1,0:T(8,128)(2,1)} %slice.13.refs_4_), channel_id=1, source_target_pairs={{0,8},{8,0},{16,24},{24,16},{32,40},{40,32},{48,56},{56,48},{64,72... | collective-permute-start | bytes 3145736 | tf_op jit(solution)/shard_map/ppermute | solution.py:444
  49.3 21.9 %copy-start.15 = (bf16[8,256,128]{2,1,0:T(8,128)(2,1)}, bf16[8,256,128]{2,1,0:T(8,128)(2,1)S(1)}, u32[]{:S(2)}) copy-start(bf16[8,256,128]{2,1,0:T(8,128)(2,1)S(1)} %collective-permute-done.3.refs_3_) | copy-start | bytes 1572868
  60.3 10.8 %collective-permute-start.5 = (bf16[8,512,128]{2,1,0:T(8,128)(2,1)}, bf16[8,512,128]{2,1,0:T(8,128)(2,1)}, u32[]{:S(2)}, u32[]{:S(2)}) collective-permute-start(bf16[8,512,128]{2,1,0:T(8,128)(2,1)} %collective-permute-done.refs_6_), channel_id=1, source_target_pairs={{0,8},{8,0},{16,24},{24,16},{32,40},{40,32},{48,56},{56,48},{64,72... | collective-permute-start | bytes 3145736 | tf_op jit(solution)/shard_map/ppermute | solution.py:444
  63.7 31.6 %all-to-all-start.2 = ((bf16[8,1024,128]{2,1,0:T(8,128)(2,1)}), bf16[8,1024,128]{2,1,0:T(8,128)(2,1)S(1)}, u32[]{:S(2)}, u32[]{:S(2)}) async-start(bf16[8,1024,128]{2,1,0:T(8,128)(2,1)} %fold.1), calls=%async_computation.2 | async-start | bytes 4194304 | tf_op jit(solution)/shard_map/all_to_all | solution.py:477
  95.4 30.4 %copy-start = (bf16[8,1024,128]{2,1,0:T(8,128)(2,1)}, bf16[8,1024,128]{2,1,0:T(8,128)(2,1)S(1)}, u32[]{:S(2)}) copy-start(bf16[8,1024,128]{2,1,0:T(8,128)(2,1)S(1)} %all-to-all-done.2.parts_ref.refs_1_.refs_2_.refs_3_) | copy-start | bytes 6291460
  95.4 34.4 %all-to-all-start.3 = ((bf16[4,144,1024]{2,1,0:T(8,128)(2,1)}), bf16[4,144,1024]{2,1,0:T(8,128)(2,1)S(1)}, u32[]{:S(2)}, u32[]{:S(2)}) async-start(bf16[4,144,1024]{2,1,0:T(8,128)(2,1)} %attend.5), calls=%async_computation.3 | async-start | bytes 2359296 | tf_op jit(solution)/shard_map/all_to_all | solution.py:457
  100.7 25.1 %copy-start.12 = (bf16[8,128,128]{2,1,0:T(8,128)(2,1)}, bf16[8,128,128]{2,1,0:T(8,128)(2,1)S(1)}, u32[]{:S(2)}) copy-start(bf16[8,128,128]{2,1,0:T(8,128)(2,1)S(1)} %slice.15.refs_0_) | copy-start | bytes 786436
  100.7 25.1 %collective-permute-start.8 = (bf16[8,128,128]{2,1,0:T(8,128)(2,1)S(1)}, bf16[8,128,128]{2,1,0:T(8,128)(2,1)S(1)}, u32[]{:S(2)}, u32[]{:S(2)}) collective-permute-start(bf16[8,128,128]{2,1,0:T(8,128)(2,1)S(1)} %slice.15.refs_0_), channel_id=1, source_target_pairs={{0,32},{8,40},{16,48},{24,56},{32,0},{40,8},{48,16},{56,24},{64,96... | collective-permute-start | bytes 786440 | tf_op jit(solution)/shard_map/ppermute | solution.py:444
  104.3 22.8 %collective-permute-start.7 = (bf16[8,128,128]{2,1,0:T(8,128)(2,1)S(1)}, bf16[8,128,128]{2,1,0:T(8,128)(2,1)S(1)}, u32[]{:S(2)}, u32[]{:S(2)}) collective-permute-start(bf16[8,128,128]{2,1,0:T(8,128)(2,1)S(1)} %slice.15.refs_0_), channel_id=1, source_target_pairs={{0,48},{8,56},{16,0},{24,8},{32,16},{40,24},{48,32},{56,40},{64,11... | collective-permute-start | bytes 786440 | tf_op jit(solution)/shard_map/ppermute | solution.py:444
  105.5 22.8 %collective-permute-start.6 = (bf16[8,128,128]{2,1,0:T(8,128)(2,1)S(1)}, bf16[8,128,128]{2,1,0:T(8,128)(2,1)S(1)}, u32[]{:S(2)}, u32[]{:S(2)}) collective-permute-start(bf16[8,128,128]{2,1,0:T(8,128)(2,1)S(1)} %slice.15.refs_0_), channel_id=1, source_target_pairs={{0,16},{8,24},{16,32},{24,40},{32,48},{40,56},{48,0},{56,8},{64,80... | collective-permute-start | bytes 786440 | tf_op jit(solution)/shard_map/ppermute | solution.py:444
  106.4 19.4 %copy-start.4 = (bf16[8,256,128]{2,1,0:T(8,128)(2,1)}, bf16[8,256,128]{2,1,0:T(8,128)(2,1)S(1)}, u32[]{:S(2)}) copy-start(bf16[8,256,128]{2,1,0:T(8,128)(2,1)S(1)} %slice.16.refs_3_.refs_1_) | copy-start | bytes 1572868
  106.4 23.5 %copy-start.13 = (f32[384]{0:T(512)S(1)}, f32[384]{0:T(512)}, u32[]{:S(2)}) copy-start(f32[384]{0:T(512)} %param.26) | copy-start | bytes 4612
  106.4 21.9 %collective-permute-start.10 = (bf16[8,256,128]{2,1,0:T(8,128)(2,1)S(1)}, bf16[8,256,128]{2,1,0:T(8,128)(2,1)S(1)}, u32[]{:S(2)}, u32[]{:S(2)}) collective-permute-start(bf16[8,256,128]{2,1,0:T(8,128)(2,1)S(1)} %slice.16.refs_3_.refs_1_), channel_id=1, source_target_pairs={{0,8},{8,0},{16,24},{24,16},{32,40},{40,32},{48,56},{56,48},{64,72... | collective-permute-start | bytes 1572872 | tf_op jit(solution)/shard_map/ppermute | solution.py:444
  106.5 23.3 %collective-permute-start.9 = (bf16[8,256,128]{2,1,0:T(8,128)(2,1)S(1)}, bf16[8,256,128]{2,1,0:T(8,128)(2,1)}, u32[]{:S(2)}, u32[]{:S(2)}) collective-permute-start(bf16[8,256,128]{2,1,0:T(8,128)(2,1)S(1)} %slice.16.refs_3_.refs_1_), channel_id=1, source_target_pairs={{0,64},{8,72},{16,80},{24,88},{32,96},{40,104},{48,112},{56,120},{... | collective-permute-start | bytes 1572872 | tf_op jit(solution)/shard_map/ppermute | solution.py:444
  129.8 17.1 %collective-permute-start.13 = (bf16[8,256,128]{2,1,0:T(8,128)(2,1)}, bf16[8,256,128]{2,1,0:T(8,128)(2,1)S(1)}, u32[]{:S(2)}, u32[]{:S(2)}) collective-permute-start(bf16[8,256,128]{2,1,0:T(8,128)(2,1)} %collective-permute-done.9.refs_5_.refs_3_), channel_id=1, source_target_pairs={{0,8},{8,0},{16,24},{24,16},{32,40},{40,32},{48,56},{56,48},{64,72... | collective-permute-start | bytes 1572872 | tf_op jit(solution)/shard_map/ppermute | solution.py:444
  130.6 11.3 %copy-start.21 = (bf16[144,1024]{1,0:T(8,128)(2,1)S(1)}, bf16[144,1024]{1,0:T(8,128)(2,1)}, u32[]{:S(2)}) copy-start(bf16[144,1024]{1,0:T(8,128)(2,1)} %get-tuple-element.60) | copy-start | bytes 884740
  130.6 14.0 %copy-start.20 = (bf16[144,1024]{1,0:T(8,128)(2,1)S(1)}, bf16[144,1024]{1,0:T(8,128)(2,1)}, u32[]{:S(2)}) copy-start(bf16[144,1024]{1,0:T(8,128)(2,1)} %get-tuple-element.61) | copy-start | bytes 884740
  130.6 14.0 %copy-start.19 = (bf16[144,1024]{1,0:T(8,128)(2,1)S(1)}, bf16[144,1024]{1,0:T(8,128)(2,1)}, u32[]{:S(2)}) copy-start(bf16[144,1024]{1,0:T(8,128)(2,1)} %get-tuple-element.81) | copy-start | bytes 884740
  135.9 25.1 %all-to-all-start.4 = ((bf16[16,192,128]{2,1,0:T(8,128)(2,1)}), bf16[16,192,128]{2,1,0:T(8,128)(2,1)S(1)}, u32[]{:S(2)}, u32[]{:S(2)}) async-start(bf16[16,192,128]{2,1,0:T(8,128)(2,1)} %project.1), calls=%async_computation.4 | async-start | bytes 1572864 | tf_op jit(solution)/shard_map/all_to_all | solution.py:560
  141.8 19.2 %collective-permute-start.11 = (bf16[144,1024]{1,0:T(8,128)(2,1)S(1)}, bf16[144,1024]{1,0:T(8,128)(2,1)S(1)}, u32[]{:S(2)}, u32[]{:S(2)}) collective-permute-start(bf16[144,1024]{1,0:T(8,128)(2,1)S(1)} %copy-done.21), channel_id=1, source_target_pairs={{0,48},{8,56},{16,0},{24,8},{32,16},{40,24},{48,32},{56,40},{64,11... | collective-permute-start | bytes 884744 | tf_op jit(solution)/shard_map/ppermute | solution.py:444
  144.6 16.5 %collective-permute-start.12 = (bf16[144,1024]{1,0:T(8,128)(2,1)S(1)}, bf16[144,1024]{1,0:T(8,128)(2,1)S(1)}, u32[]{:S(2)}, u32[]{:S(2)}) collective-permute-start(bf16[144,1024]{1,0:T(8,128)(2,1)S(1)} %copy-done.20), channel_id=1, source_target_pairs={{0,16},{8,24},{16,32},{24,40},{32,48},{40,56},{48,0},{56,8},{64,80... | collective-permute-start | bytes 884744 | tf_op jit(solution)/shard_map/ppermute | solution.py:444
  144.6 26.7 %collective-permute-start.17 = (bf16[144,1024]{1,0:T(8,128)(2,1)S(1)}, bf16[144,1024]{1,0:T(8,128)(2,1)S(1)}, u32[]{:S(2)}, u32[]{:S(2)}) collective-permute-start(bf16[144,1024]{1,0:T(8,128)(2,1)S(1)} %copy-done.19), channel_id=1, source_target_pairs={{0,32},{8,40},{16,48},{24,56},{32,0},{40,8},{48,16},{56,24},{64,96... | collective-permute-start | bytes 884744 | tf_op jit(solution)/shard_map/ppermute | solution.py:444
  161.1 18.4 %collective-permute-start.14 = (bf16[144,1024]{1,0:T(8,128)(2,1)}, bf16[144,1024]{1,0:T(8,128)(2,1)S(1)}, u32[]{:S(2)}, u32[]{:S(2)}) collective-permute-start(bf16[144,1024]{1,0:T(8,128)(2,1)} %get-tuple-element.72), channel_id=1, source_target_pairs={{0,48},{8,56},{16,0},{24,8},{32,16},{40,24},{48,32},{56,40},{64,11... | collective-permute-start | bytes 884744 | tf_op jit(solution)/shard_map/ppermute | solution.py:444
  162.3 17.1 %collective-permute-start.15 = (bf16[144,1024]{1,0:T(8,128)(2,1)}, bf16[144,1024]{1,0:T(8,128)(2,1)S(1)}, u32[]{:S(2)}, u32[]{:S(2)}) collective-permute-start(bf16[144,1024]{1,0:T(8,128)(2,1)} %get-tuple-element.73), channel_id=1, source_target_pairs={{0,16},{8,24},{16,32},{24,40},{32,48},{40,56},{48,0},{56,8},{64,80... | collective-permute-start | bytes 884744 | tf_op jit(solution)/shard_map/ppermute | solution.py:444
  163.2 16.6 %collective-permute-start.16 = (bf16[144,1024]{1,0:T(8,128)(2,1)}, bf16[144,1024]{1,0:T(8,128)(2,1)S(1)}, u32[]{:S(2)}, u32[]{:S(2)}) collective-permute-start(bf16[144,1024]{1,0:T(8,128)(2,1)} %get-tuple-element.74), channel_id=1, source_target_pairs={{0,32},{8,40},{16,48},{24,56},{32,0},{40,8},{48,16},{56,24},{64,96... | collective-permute-start | bytes 884744 | tf_op jit(solution)/shard_map/ppermute | solution.py:444
  (16 other events, 53.5 us)
